TPU v7x, 32 devices: a whole 2x2x4 slice. The times are simulated.
32 devices in a mesh: section: 2 (over x), replica: 4 (over z), shard: 4 (over y, core).
Axes of the slice: x: 2, y: 2, z: 4, core: 2. Of those that a mesh axis runs over, the one named last changes fastest.
Arguments:
- ends: bfloat16 [2, 2, 4, 2048, 576], P('section', None, 'replica', 'shard'), may hold values from -6 to 6
- attn_norm: bfloat16 [2, 576], P('section', 'shard'), may hold values from 0.5 to 1.5
- w_query: bfloat16 [2, 576, 576], P('section', 'shard'), may hold values from -0.25 to 0.25
- w_key: bfloat16 [2, 576, 192], P('section', 'shard'), may hold values from -0.25 to 0.25
- w_value: bfloat16 [2, 576, 192], P('section', 'shard'), may hold values from -0.25 to 0.25
- w_out: bfloat16 [2, 576, 576], P('section', 'shard'), may hold values from -1.5 to 1.5
- ffn_norm: bfloat16 [2, 576], P('section', 'shard'), may hold values from 0.5 to 1.5
- w_gate: bfloat16 [2, 576, 1536], P('section', 'shard'), may hold values from -0.25 to 0.25
- w_up: bfloat16 [2, 576, 1536], P('section', 'shard'), may hold values from -0.25 to 0.25
- w_down: bfloat16 [2, 1536, 576], P('section', 'shard'), may hold values from -0.15625 to 0.15625
Outputs:
- ends_out: float32 [2, 2, 4, 2048, 576], P('section', None, 'replica', 'shard')
- grad_attn_norm: float32 [2, 576], P('section', 'shard')
- grad_query: float32 [2, 576, 576], P('section', 'shard')
- grad_key: float32 [2, 576, 192], P('section', 'shard')
- grad_value: float32 [2, 576, 192], P('section', 'shard')
- grad_out: float32 [2, 576, 576], P('section', 'shard')
- grad_ffn_norm: float32 [2, 576], P('section', 'shard')
- grad_gate: float32 [2, 576, 1536], P('section', 'shard')
- grad_up: float32 [2, 576, 1536], P('section', 'shard')
- grad_down: float32 [2, 1536, 576], P('section', 'shard')
All inputs are finite; a program needn't handle non-finite values.
Results may differ from a plain program's by a relative error of at most 0.034.
Values may be sent and summed in bfloat16 or wider, within the bound.
A program may use at most 192 MiB of HBM per device.

v0:
```python
from functools import partial

import jax
import jax.numpy as jnp
from jax import lax
from jax.sharding import PartitionSpec as P

HEADS = 9
KV_HEADS = 3
HEAD = 64


epsilon = 1e-05
rope_base = 100000.0
neg_large = -1e30


def shifted(shard, axis, by):
    peers = lax.axis_size(axis)
    pairs = [(i, i + by) for i in range(peers) if 0 <= i + by < peers]
    return lax.ppermute(shard, axis, pairs)


def rms_scale(source):
    return lax.rsqrt(jnp.mean(source * source, axis=-1, keepdims=True) + epsilon)


def rms_back(source, gain_vector, grad_normed):
    inv_scale = rms_scale(source)
    unit_rows = source * inv_scale
    grad_unit = grad_normed * gain_vector
    gain_grad = jnp.sum(grad_normed * unit_rows, axis=0)
    grad_source = inv_scale * (
        grad_unit - unit_rows * jnp.mean(grad_unit * unit_rows, axis=-1, keepdims=True)
    )
    return (grad_source, gain_grad)


def rotation_tables(positions):
    half_size = HEAD // 2
    frequency = rope_base ** (-jnp.arange(half_size, dtype=jnp.float32) * 2.0 / HEAD)
    angles = positions.astype(jnp.float32)[:, None] * frequency[None, :]
    return (jnp.cos(angles)[None, :, None, :], jnp.sin(angles)[None, :, None, :])


def rotate(tensor, tables):
    cosine, sine_part = tables
    half_size = tensor.shape[-1] // 2
    first_half = tensor[..., :half_size]
    second_half = tensor[..., half_size:]
    return jnp.concatenate(
        [
            first_half * cosine - second_half * sine_part,
            second_half * cosine + first_half * sine_part,
        ],
        axis=-1,
    )


def rotate_back(gradient, tables):
    cosine, sine_part = tables
    half_size = gradient.shape[-1] // 2
    first_half = gradient[..., :half_size]
    second_half = gradient[..., half_size:]
    return jnp.concatenate(
        [
            first_half * cosine + second_half * sine_part,
            second_half * cosine - first_half * sine_part,
        ],
        axis=-1,
    )


def linear(left_side, right_side):
    return jnp.dot(left_side, right_side, preferred_element_type=jnp.float32)


def weight_grad(left_side, right_side):
    return jnp.einsum("rd,rf->df", left_side, right_side, preferred_element_type=jnp.float32)


def input_grad(gradient, weight):
    return jnp.einsum("rf,df->rd", gradient, weight, preferred_element_type=jnp.float32)


def split_blocks(tensor):
    seq_count, length, head_count, head_size = tensor.shape
    block_rows = min(512, length)
    shaped = tensor.reshape(seq_count, length // block_rows, block_rows, head_count, head_size)
    return (jnp.moveaxis(shaped, 1, 0), block_rows)


def block_scores(grouped, key_block, block_start, positions):
    raw_scores = jnp.einsum(
        "stkgd,sukd->skgtu", grouped, key_block, preferred_element_type=jnp.float32
    )
    key_pos = block_start + jnp.arange(key_block.shape[1], dtype=jnp.int32)
    allowed = key_pos[None, :] <= positions[:, None]
    return (jnp.where(allowed, raw_scores * HEAD ** (-0.5), neg_large), allowed)


def keep_carry(state_triple):
    return state_triple


def scatter_at_end(parts):
    attn_shares = (
        lax.psum_scatter(
            parts[0].astype(jnp.bfloat16), "shard", scatter_dimension=0, tiled=True
        ).astype(jnp.float32),
        lax.psum_scatter(
            parts[1].astype(jnp.bfloat16), "shard", scatter_dimension=0, tiled=True
        ).astype(jnp.float32),
        lax.psum_scatter(
            parts[2].astype(jnp.bfloat16), "shard", scatter_dimension=0, tiled=True
        ).astype(jnp.float32),
        lax.psum_scatter(
            parts[3].astype(jnp.bfloat16), "shard", scatter_dimension=0, tiled=True
        ).astype(jnp.float32),
        lax.psum_scatter(
            parts[4].astype(jnp.bfloat16), "shard", scatter_dimension=0, tiled=True
        ).astype(jnp.float32),
        lax.psum_scatter(
            parts[5].astype(jnp.bfloat16), "shard", scatter_dimension=0, tiled=True
        ).astype(jnp.float32),
    )
    ffn_shares = (
        lax.psum_scatter(
            parts[6].astype(jnp.bfloat16), "shard", scatter_dimension=0, tiled=True
        ).astype(jnp.float32),
        lax.psum_scatter(
            parts[7].astype(jnp.bfloat16), "shard", scatter_dimension=0, tiled=True
        ).astype(jnp.float32),
    )
    down_share = lax.psum_scatter(
        parts[8].astype(jnp.bfloat16), "shard", scatter_dimension=0, tiled=True
    ).astype(jnp.float32)
    return tuple(attn_shares) + tuple(ffn_shares) + (down_share,)


def forward_layer(block_in, weights, tables, positions):
    gain_attn, w_query, w_key, w_value, w_out, gain_ffn, w_gate, w_up, w_down = weights
    seq_count, tok_count, model_width = block_in.shape
    group_size = HEADS // KV_HEADS
    source = block_in.astype(jnp.float32).reshape(seq_count * tok_count, model_width)
    normed = (source * rms_scale(source) * gain_attn.astype(jnp.float32)).astype(jnp.bfloat16)
    query_rot = rotate(
        linear(normed, w_query).reshape(seq_count, tok_count, HEADS, HEAD), tables
    ).astype(jnp.bfloat16)
    key_rot = rotate(
        linear(normed, w_key).reshape(seq_count, tok_count, KV_HEADS, HEAD), tables
    ).astype(jnp.bfloat16)
    values = (
        linear(normed, w_value).astype(jnp.bfloat16).reshape(seq_count, tok_count, KV_HEADS, HEAD)
    )
    keys_all, values_all = (
        lax.all_gather(key_rot, "shard", axis=1, tiled=True),
        lax.all_gather(values, "shard", axis=1, tiled=True),
    )
    grouped = query_rot.reshape(seq_count, tok_count, KV_HEADS, group_size, HEAD)
    key_blocks, block_rows = split_blocks(keys_all)
    value_blocks, block_rows = split_blocks(values_all)
    block_ids = jnp.arange(key_blocks.shape[0], dtype=jnp.int32)
    last_query = positions[-1]

    def attend_step(state_triple, block_args):
        key_block, value_block, block_index = block_args
        block_start = block_index * block_rows

        def attend_update(state_triple):
            running_top, running_sum, mixed_sum = state_triple
            scores, allowed = block_scores(grouped, key_block, block_start, positions)
            new_top = jnp.maximum(running_top, jnp.max(scores, axis=-1))
            weights_now = jnp.where(allowed, jnp.exp(scores - new_top[..., None]), 0.0)
            factor = jnp.exp(running_top - new_top)
            running_sum = running_sum * factor + jnp.sum(weights_now, axis=-1)
            mixed_sum = mixed_sum * jnp.moveaxis(factor, 3, 1)[..., None] + jnp.einsum(
                "skgtu,sukd->stkgd",
                weights_now.astype(jnp.bfloat16),
                value_block,
                preferred_element_type=jnp.float32,
            )
            return (new_top, running_sum, mixed_sum)

        return (lax.cond(block_start <= last_query, attend_update, keep_carry, state_triple), None)

    stats_shape = (seq_count, KV_HEADS, group_size, tok_count)
    start_triple = (
        jnp.full(stats_shape, neg_large, jnp.float32),
        jnp.zeros(stats_shape, jnp.float32),
        jnp.zeros(grouped.shape, jnp.float32),
    )
    (running_top, running_sum, mixed_sum), unused = lax.scan(
        attend_step, start_triple, (key_blocks, value_blocks, block_ids)
    )
    log_total = running_top + jnp.log(running_sum)
    attended = mixed_sum / jnp.moveaxis(running_sum, 3, 1)[..., None]
    mixed_heads = attended.astype(jnp.bfloat16).reshape(seq_count * tok_count, HEADS * HEAD)
    hidden = source + linear(mixed_heads, w_out)
    normed_ffn = (hidden * rms_scale(hidden) * gain_ffn.astype(jnp.float32)).astype(jnp.bfloat16)
    gate_pre = linear(normed_ffn, w_gate)
    upper = linear(normed_ffn, w_up)
    active = (gate_pre * jax.nn.sigmoid(gate_pre) * upper).astype(jnp.bfloat16)
    result = hidden + linear(active, w_down)
    kept_state = (
        block_in,
        normed,
        grouped,
        key_blocks,
        value_blocks,
        log_total,
        mixed_heads,
        attended,
        hidden,
        normed_ffn,
        gate_pre,
        upper,
        active,
    )
    return (result, kept_state)


def backward_layer(kept_state, grad_out, weights, tables, positions):
    gain_attn, w_query, w_key, w_value, w_out, gain_ffn, w_gate, w_up, w_down = weights
    (
        block_in,
        normed,
        grouped,
        key_blocks,
        value_blocks,
        log_total,
        mixed_heads,
        attended,
        hidden,
        normed_ffn,
        gate_pre,
        upper,
        active,
    ) = kept_state
    seq_count, tok_count, model_width = block_in.shape
    block_rows = key_blocks.shape[2]
    source = block_in.astype(jnp.float32).reshape(seq_count * tok_count, model_width)
    grad_ffn_out = grad_out.astype(jnp.bfloat16)
    g_down = weight_grad(active, grad_ffn_out)
    grad_active = input_grad(grad_ffn_out, w_down)
    sigmoid_gate = jax.nn.sigmoid(gate_pre)
    grad_gate = (
        grad_active * upper * sigmoid_gate * (1.0 + gate_pre * (1.0 - sigmoid_gate))
    ).astype(jnp.bfloat16)
    grad_upper = (grad_active * gate_pre * sigmoid_gate).astype(jnp.bfloat16)
    g_gate = weight_grad(normed_ffn, grad_gate)
    g_up = weight_grad(normed_ffn, grad_upper)
    grad_normed_ffn = input_grad(grad_gate, w_gate) + input_grad(grad_upper, w_up)
    grad_hidden_part, g_gain_ffn = rms_back(hidden, gain_ffn.astype(jnp.float32), grad_normed_ffn)
    grad_hidden = grad_out + grad_hidden_part
    grad_attn = grad_hidden.astype(jnp.bfloat16)
    g_out = weight_grad(mixed_heads, grad_attn)
    grad_heads = input_grad(grad_attn, w_out).astype(jnp.bfloat16).reshape(grouped.shape)
    row_delta = jnp.moveaxis(jnp.sum(grad_heads.astype(jnp.float32) * attended, axis=-1), 1, 3)
    block_ids = jnp.arange(key_blocks.shape[0], dtype=jnp.int32)
    last_query = positions[-1]

    def grad_step(grad_query, block_args):
        key_block, value_block, block_index = block_args
        block_start = block_index * block_rows

        def grad_update(grad_query):
            scores, allowed = block_scores(grouped, key_block, block_start, positions)
            probabilities = jnp.where(allowed, jnp.exp(scores - log_total[..., None]), 0.0)
            grad_probs = jnp.einsum(
                "stkgd,sukd->skgtu", grad_heads, value_block, preferred_element_type=jnp.float32
            )
            grad_scores = (
                probabilities * (grad_probs - row_delta[..., None]) * HEAD ** (-0.5)
            ).astype(jnp.bfloat16)
            grad_query = grad_query + jnp.einsum(
                "skgtu,sukd->stkgd", grad_scores, key_block, preferred_element_type=jnp.float32
            )
            grad_key_block = jnp.einsum(
                "skgtu,stkgd->sukd", grad_scores, grouped, preferred_element_type=jnp.float32
            )
            grad_value_block = jnp.einsum(
                "skgtu,stkgd->sukd",
                probabilities.astype(jnp.bfloat16),
                grad_heads,
                preferred_element_type=jnp.float32,
            )
            return (grad_query, (grad_key_block, grad_value_block))

        def skip_block(grad_query):
            empty_grad = jnp.zeros(key_block.shape, jnp.float32)
            return (grad_query, (empty_grad, empty_grad))

        return lax.cond(block_start <= last_query, grad_update, skip_block, grad_query)

    grad_query, (key_parts, value_parts) = lax.scan(
        grad_step, jnp.zeros(grouped.shape, jnp.float32), (key_blocks, value_blocks, block_ids)
    )
    full_shape = (seq_count, key_parts.shape[0] * block_rows, KV_HEADS, HEAD)
    key_full = jnp.moveaxis(key_parts, 0, 1).reshape(full_shape)
    value_full = jnp.moveaxis(value_parts, 0, 1).reshape(full_shape)
    grad_keys, grad_values = (
        lax.psum_scatter(
            key_full.astype(jnp.bfloat16), "shard", scatter_dimension=1, tiled=True
        ).astype(jnp.float32),
        lax.psum_scatter(
            value_full.astype(jnp.bfloat16), "shard", scatter_dimension=1, tiled=True
        ).astype(jnp.float32),
    )
    row_count = seq_count * tok_count
    grad_query_rows = (
        rotate_back(grad_query.reshape(seq_count, tok_count, HEADS, HEAD), tables)
        .astype(jnp.bfloat16)
        .reshape(row_count, HEADS * HEAD)
    )
    grad_key_rows = (
        rotate_back(grad_keys, tables).astype(jnp.bfloat16).reshape(row_count, KV_HEADS * HEAD)
    )
    grad_value_rows = grad_values.astype(jnp.bfloat16).reshape(row_count, KV_HEADS * HEAD)
    g_query = weight_grad(normed, grad_query_rows)
    g_key = weight_grad(normed, grad_key_rows)
    g_value = weight_grad(normed, grad_value_rows)
    grad_normed = (
        input_grad(grad_query_rows, w_query)
        + input_grad(grad_key_rows, w_key)
        + input_grad(grad_value_rows, w_value)
    )
    grad_source_part, g_gain_attn = rms_back(source, gain_attn.astype(jnp.float32), grad_normed)
    grad_source = grad_hidden + grad_source_part
    return (
        grad_source,
        (g_gain_attn, g_query, g_key, g_value, g_out, g_gain_ffn, g_gate, g_up, g_down),
    )


def on_device(ends, attn_norm, w_query, w_key, w_value, w_out, ffn_norm, w_gate, w_up, w_down):
    params = (
        attn_norm[0],
        w_query[0],
        w_key[0],
        w_value[0],
        w_out[0],
        ffn_norm[0],
        w_gate[0],
        w_up[0],
        w_down[0],
    )
    leading = lax.axis_index("section") == 0
    held_weights = (
        lax.all_gather(params[0], "shard", axis=0, tiled=True),
        lax.all_gather(params[1], "shard", axis=0, tiled=True),
        lax.all_gather(params[2], "shard", axis=0, tiled=True),
        lax.all_gather(params[3], "shard", axis=0, tiled=True),
        lax.all_gather(params[4], "shard", axis=0, tiled=True),
        lax.all_gather(params[5], "shard", axis=0, tiled=True),
        lax.all_gather(params[6], "shard", axis=0, tiled=True),
        lax.all_gather(params[7], "shard", axis=0, tiled=True),
        lax.all_gather(params[8], "shard", axis=0, tiled=True),
    )
    local_ends = ends[0]
    micro_count, seq_count, tok_count, model_width = local_ends.shape
    positions = lax.axis_index("shard") * tok_count + jnp.arange(tok_count, dtype=jnp.int32)
    tables = rotation_tables(positions)
    arriving = jnp.zeros((seq_count, tok_count, model_width), jnp.bfloat16)
    kept_states = []
    layer_outputs = []
    for moment in range(micro_count + 1):
        own_rows = local_ends[moment] if moment < micro_count else jnp.zeros_like(arriving)
        block_in = jnp.where(leading, own_rows, arriving)
        result, kept_state = forward_layer(block_in, held_weights, tables, positions)
        kept_states.append(kept_state)
        if moment > 0:
            layer_outputs.append(result)
        if moment < micro_count:
            arriving = shifted(
                result.astype(jnp.bfloat16).reshape(seq_count, tok_count, model_width), "section", 1
            )
    returning = jnp.zeros((seq_count * tok_count, model_width), jnp.float32)
    totals = None
    input_grads = []
    for moment in range(micro_count + 1):
        earlier = moment - 1 if moment > 0 else micro_count
        later = moment + 1 if moment < micro_count else 0
        kept_state = jax.tree.map(
            partial(jnp.where, leading), kept_states[earlier], kept_states[later]
        )
        if moment < micro_count:
            own_grad = (
                local_ends[moment].astype(jnp.float32).reshape(seq_count * tok_count, model_width)
            )
        else:
            own_grad = jnp.zeros_like(returning)
        grad_source, grad_parts = backward_layer(
            kept_state, jnp.where(leading, returning, own_grad), held_weights, tables, positions
        )
        totals = grad_parts if totals is None else jax.tree.map(jnp.add, totals, grad_parts)
        if moment > 0:
            input_grads.append(grad_source)
        if moment < micro_count:
            returning = shifted(grad_source.astype(jnp.bfloat16), "section", -1).astype(jnp.float32)
    pieces = [
        jnp.where(leading, input_grads[number], layer_outputs[number])
        for number in range(micro_count)
    ]
    ends_out = jnp.stack(pieces).reshape(1, micro_count, seq_count, tok_count, model_width)
    shares = scatter_at_end(totals)
    summed = (
        lax.psum(shares[0].astype(jnp.bfloat16), "replica").astype(jnp.float32),
        lax.psum(shares[1].astype(jnp.bfloat16), "replica").astype(jnp.float32),
        lax.psum(shares[2].astype(jnp.bfloat16), "replica").astype(jnp.float32),
        lax.psum(shares[3].astype(jnp.bfloat16), "replica").astype(jnp.float32),
        lax.psum(shares[4].astype(jnp.bfloat16), "replica").astype(jnp.float32),
        lax.psum(shares[5].astype(jnp.bfloat16), "replica").astype(jnp.float32),
        lax.psum(shares[6].astype(jnp.bfloat16), "replica").astype(jnp.float32),
        lax.psum(shares[7].astype(jnp.bfloat16), "replica").astype(jnp.float32),
        lax.psum(shares[8].astype(jnp.bfloat16), "replica").astype(jnp.float32),
    )
    return (ends_out,) + tuple((share[None] for share in summed))


def solution(mesh):
    return jax.shard_map(
        on_device,
        mesh=mesh,
        in_specs=(
            P("section", None, "replica", "shard", None),
            P("section", "shard"),
            P("section", "shard", None),
            P("section", "shard", None),
            P("section", "shard", None),
            P("section", "shard", None),
            P("section", "shard"),
            P("section", "shard", None),
            P("section", "shard", None),
            P("section", "shard", None),
        ),
        out_specs=(
            P("section", None, "replica", "shard", None),
            P("section", "shard"),
            P("section", "shard", None),
            P("section", "shard", None),
            P("section", "shard", None),
            P("section", "shard", None),
            P("section", "shard"),
            P("section", "shard", None),
            P("section", "shard", None),
            P("section", "shard", None),
        ),
        check_vma=False,
    )
```

profile of v0, /device:TPU:0, one launch (start us, length us, event | category | flops | bytes accessed | tf_op | source)
XLA Modules:
  0.0 1113.4 jit_solution(15147360947989485165)
XLA Ops:
  9.5 7.6 all-gather.1
  19.1 7.5 all-reduce.5
  27.8 9.1 all_gather.47
  36.8 8.4 all-gather.2
  48.3 8.0 all-gather.3
  56.8 9.2 all_gather.50
  69.6 18.7 %while.99 = (s32[]{:T(128)}, f32[1,3,3,512]{3,2,1,0:T(4,128)}, f32[1,3,3,512]{3,2,1,0:T(4,128)S(1)}, f32[1,512,3,3,64]{1,4,3,2,0:T(8,128)S(1)}, s32[4]{0:T(128)S...) while((s32[]{:T(128)}, f32[1,3,3,512]{3,2,1,0:T(4,128)}, ...), condition=%wide.region_6.7_spmd.clone, body=%wide.region_1.6_spmd.clone.sunk | while | flops 635517440 | bytes 33010996 | solution.py:193
  71.5 10.8 conditional.18
  78.7 3.6 fusion.22
  88.3 40.0 %all-gather.4 = bf16[1,576,576]{2,1,0:T(8,128)(2,1)S(1)} all-gather(bf16[1,144,576]{2,1,0:T(8,128)(2,1)} %param.39), channel_id=6, replica_groups=mesh['section'=2,'replica'=4,'shard'=4] {'shard'}, dimensions={1}, use_global_device_ids=true | all-gather | bytes 829440 | tf_op jit(solution)/shard_map/all_gather | solution.py:354
  130.6 4.8 fusion.220
  135.4 6.3 multiply_convert_fusion.8
  141.7 3.4 fusion.269
  145.1 3.6 collective-permute-start
  148.7 13.0 %collective-permute-done = bf16[1,512,576]{1,2,0:T(8,128)(2,1)S(1)} collective-permute-done((bf16[1,512,576]{1,2,0:T(8,128)(2,1)S(1)}, bf16[1,512,576]{1,2,0:T(8,128)(2,1)S(1)}, u32[]{:S(2)}, u32[]{:S(2)}) %collective-permute-start) | collective-permute-done | bytes 589856 | tf_op jit(solution)/shard_map/ppermute | solution.py:21
  166.3 7.9 all_gather.56
  175.4 9.4 all_gather.57
  188.3 19.3 %while.100 = (s32[]{:T(128)}, f32[1,3,3,512]{3,2,1,0:T(4,128)S(1)}, f32[1,3,3,512]{3,2,1,0:T(4,128)}, f32[1,512,3,3,64]{1,4,3,2,0:T(8,128)S(1)}, s32[4]{0:T(128)...) while((s32[]{:T(128)}, f32[1,3,3,512]{3,2,1,0:T(4,128)S(1)}, ...), condition=%wide.region_14.15_spmd.clone, body=%wide.region_9.14_spmd.clone.sunk | while | flops 635517440 | bytes 33158508 | solution.py:193
  190.9 8.8 conditional.19
  196.0 3.6 fusion.47
  213.0 3.4 multiply_convert_fusion.7
  220.6 4.6 collective-permute-start.1
  226.7 3.1 transpose_reshape.19
  231.2 3.0 transpose_reshape.21
  235.0 34.2 %all_gather.58 = bf16[1,2048,3,64]{1,3,2,0:T(8,128)(2,1)S(1)} all-gather(bf16[1,512,3,64]{1,3,2,0:T(8,128)(2,1)S(1)} %pad_maximum_fusion.5), channel_id=1, replica_groups=mesh['section'=2,'replica'=4,'shard'=4] {'shard'}, dimensions={1}, use_global_device_ids=true | all-gather | bytes 983040 | tf_op jit(solution)/shard_map/all_gather | solution.py:157
  274.2 8.9 all_gather.59
  288.6 17.2 %while.101 = (s32[]{:T(128)}, f32[1,3,3,512]{3,2,1,0:T(4,128)}, f32[1,3,3,512]{3,2,1,0:T(4,128)}, f32[1,512,3,3,64]{1,4,3,2,0:T(8,128)S(1)}, s32[4]{0:T(128)S(1)...) while((s32[]{:T(128)}, f32[1,3,3,512]{3,2,1,0:T(4,128)}, ...), condition=%wide.region_22.23_spmd.clone, body=%wide.region_17.22_spmd.clone.sunk | while | flops 635517440 | bytes 33232264 | solution.py:193
  290.5 9.4 conditional.20
  296.3 3.6 fusion.72
  318.6 3.1 multiply_convert_fusion.6
  339.2 24.3 %while.102 = (s32[]{:T(128)}, f32[1,512,3,3,64]{1,4,3,2,0:T(8,128)S(1)}, bf16[4,1,512,3,64]{2,4,3,1,0:T(8,128)(2,1)}, bf16[4,1,512,3,64]{2,4,3,1,0:T(8,128)(2,1)...) while((s32[]{:T(128)}, ...), condition=%wide.region_31.32_spmd.clone, body=%wide.region_28.31_spmd.clone.sunk | while | flops 1541178368 | bytes 52171088 | solution.py:296
  341.1 13.3 %conditional.21 = (f32[1,512,3,3,64]{1,4,3,2,0:T(8,128)S(1)}, bf16[1,1,512,3,64]{2,4,3,1,0:T(8,128)(2,1)S(1)}, bf16[1,1,512,3,64]{2,4,3,1,0:T(8,128)(2,1)S(1)}) conditional(s32[]{:T(128)} %convert_element_type.1163, f32[1,512,3,3,64]{1,4,3,2,0:T(8,128)S(1)} %get-tuple-element.2216, (bf16[4,1,512,3,64]{2,4,3,1,0:T(8,128)(2,1)}, s32[]{:T(128)}, ...), branch_computations={%region_29.29_spmd, %region_30.30_spmd} | conditional | flops 1541178368 | bytes 51381820 | solution.py:294
  343.8 4.6 fusion.95
  369.7 86.1 %reduce-scatter.16.cloned.1.call-done = bf16[1,512,3,64]{1,3,2,0:T(8,128)(2,1)} async-done(((bf16[1,2048,3,64]{1,3,2,0:T(8,128)(2,1)}), bf16[1,512,3,64]{1,3,2,0:T(8,128)(2,1)}) %reduce-scatter.16.cloned.1.call-update) | async-done | bytes 196624 | tf_op jit(solution)/shard_map/reduce_scatter | solution.py:303
  458.9 23.3 %reduce-scatter.18.cloned.1.call-done = bf16[1,512,3,64]{1,3,2,0:T(8,128)(2,1)} async-done(((bf16[1,2048,3,64]{1,3,2,0:T(8,128)(2,1)}), bf16[1,512,3,64]{1,3,2,0:T(8,128)(2,1)}) %reduce-scatter.18.cloned.1.call-update) | async-done | bytes 196624 | tf_op jit(solution)/shard_map/reduce_scatter | solution.py:306
  482.3 2.7 fusion.284
  491.1 12.4 %collective-permute-done.2 = bf16[512,576]{0,1:T(8,128)(2,1)S(1)} collective-permute-done((bf16[512,576]{0,1:T(8,128)(2,1)}, bf16[512,576]{0,1:T(8,128)(2,1)S(1)}, u32[]{:S(2)}, u32[]{:S(2)}) %collective-permute-start.2) | collective-permute-done | bytes 589856 | tf_op jit(solution)/shard_map/ppermute | solution.py:21
  503.4 7.4 multiply_convert_fusion.4
  522.3 24.4 %while.103 = (s32[]{:T(128)}, f32[1,512,3,3,64]{1,4,3,2,0:T(8,128)S(1)}, bf16[4,1,512,3,64]{2,4,3,1,0:T(8,128)(2,1)}, bf16[4,1,512,3,64]{2,4,3,1,0:T(8,128)(2,1)...) while((s32[]{:T(128)}, ...), condition=%wide.region_42.43_spmd.clone, body=%wide.region_39.42_spmd.clone.sunk | while | flops 1541178368 | bytes 52171088 | solution.py:296
  524.3 13.3 %conditional.22 = (f32[1,512,3,3,64]{1,4,3,2,0:T(8,128)S(1)}, bf16[1,1,512,3,64]{2,4,3,1,0:T(8,128)(2,1)S(1)}, bf16[1,1,512,3,64]{2,4,3,1,0:T(8,128)(2,1)S(1)}) conditional(s32[]{:T(128)} %convert_element_type.1164, f32[1,512,3,3,64]{1,4,3,2,0:T(8,128)S(1)} %get-tuple-element.2261, (bf16[4,1,512,3,64]{2,4,3,1,0:T(8,128)(2,1)}, s32[]{:T(128)}, ...), branch_computations={%region_40.40_spmd, %region_41.41_spmd} | conditional | flops 1541178368 | bytes 51381820 | solution.py:294
  527.0 4.6 fusion.128
  551.8 57.8 %reduce-scatter.20.cloned.1.call-done = bf16[1,512,3,64]{1,3,2,0:T(8,128)(2,1)} async-done(((bf16[1,2048,3,64]{1,3,2,0:T(8,128)(2,1)}), bf16[1,512,3,64]{1,3,2,0:T(8,128)(2,1)}) %reduce-scatter.20.cloned.1.call-update) | async-done | bytes 196624 | tf_op jit(solution)/shard_map/reduce_scatter | solution.py:303
  612.7 23.5 %reduce-scatter.22.cloned.1.call-done = bf16[1,512,3,64]{1,3,2,0:T(8,128)(2,1)} async-done(((bf16[1,2048,3,64]{1,3,2,0:T(8,128)(2,1)}), bf16[1,512,3,64]{1,3,2,0:T(8,128)(2,1)}) %reduce-scatter.22.cloned.1.call-update) | async-done | bytes 196624 | tf_op jit(solution)/shard_map/reduce_scatter | solution.py:306
  636.2 2.7 fusion.290
  644.2 13.3 %collective-permute-done.3 = bf16[512,576]{0,1:T(8,128)(2,1)S(1)} collective-permute-done((bf16[512,576]{0,1:T(8,128)(2,1)S(1)}, bf16[512,576]{0,1:T(8,128)(2,1)S(1)}, u32[]{:S(2)}, u32[]{:S(2)}) %collective-permute-start.3) | collective-permute-done | bytes 589856 | tf_op jit(solution)/shard_map/ppermute | solution.py:21
  657.5 4.4 multiply_convert_fusion.2
  673.0 24.3 %while.104 = (s32[]{:T(128)}, f32[1,512,3,3,64]{1,4,3,2,0:T(8,128)S(1)}, bf16[4,1,512,3,64]{2,4,3,1,0:T(8,128)(2,1)}, bf16[4,1,512,3,64]{2,4,3,1,0:T(8,128)(2,1)...) while((s32[]{:T(128)}, ...), condition=%wide.region_53.54_spmd.clone, body=%wide.region_50.53_spmd.clone.sunk | while | flops 1541178368 | bytes 52171088 | solution.py:296
  674.9 13.3 %conditional.23 = (f32[1,512,3,3,64]{1,4,3,2,0:T(8,128)S(1)}, bf16[1,1,512,3,64]{2,4,3,1,0:T(8,128)(2,1)S(1)}, bf16[1,1,512,3,64]{2,4,3,1,0:T(8,128)(2,1)S(1)}) conditional(s32[]{:T(128)} %convert_element_type.1165, f32[1,512,3,3,64]{1,4,3,2,0:T(8,128)S(1)} %get-tuple-element.2306, (bf16[4,1,512,3,64]{2,4,3,1,0:T(8,128)(2,1)}, s32[]{:T(128)}, ...), branch_computations={%region_51.51_spmd, %region_52.52_spmd} | conditional | flops 1541178368 | bytes 51381820 | solution.py:294
  677.6 4.6 fusion.161
  706.1 4.5 fusion.231
  710.6 2.9 fusion.229
  714.8 45.6 %reduce-scatter.24.cloned.1.call-done = bf16[1,512,3,64]{1,3,2,0:T(8,128)(2,1)} async-done(((bf16[1,2048,3,64]{1,3,2,0:T(8,128)(2,1)}), bf16[1,512,3,64]{1,3,2,0:T(8,128)(2,1)}) %reduce-scatter.24.cloned.1.call-update) | async-done | bytes 196624 | tf_op jit(solution)/shard_map/reduce_scatter | solution.py:303
  765.1 21.9 %reduce-scatter.26.cloned.1.call-done = bf16[1,512,3,64]{1,3,2,0:T(8,128)(2,1)} async-done(((bf16[1,2048,3,64]{1,3,2,0:T(8,128)(2,1)}), bf16[1,512,3,64]{1,3,2,0:T(8,128)(2,1)}) %reduce-scatter.26.cloned.1.call-update) | async-done | bytes 196624 | tf_op jit(solution)/shard_map/reduce_scatter | solution.py:306
  789.2 6.0 add_convert_fusion
  795.3 3.9 copy.143
  826.4 6.2 all-reduce.4
  834.0 32.8 %reduce-scatter.40.cloned.1.call-done = bf16[384,576]{1,0:T(8,128)(2,1)} async-done(((bf16[1536,576]{1,0:T(8,128)(2,1)}), bf16[384,576]{1,0:T(8,128)(2,1)}) %reduce-scatter.40.cloned.1.call-update) | async-done | bytes 442384
  868.8 24.3 %reduce-scatter.28.cloned.1.call-done = bf16[144,576]{1,0:T(8,128)(2,1)} async-done(((bf16[576,576]{1,0:T(8,128)(2,1)}), bf16[144,576]{1,0:T(8,128)(2,1)}) %reduce-scatter.28.cloned.1.call-update) | async-done | bytes 165904 | tf_op jit(solution)/shard_map/reduce_scatter | solution.py:111
  893.1 26.0 %reduce-scatter.34.cloned.1.call-done = bf16[144,576]{1,0:T(8,128)(2,1)} async-done(((bf16[576,576]{1,0:T(8,128)(2,1)}), bf16[144,576]{1,0:T(8,128)(2,1)}) %reduce-scatter.34.cloned.1.call-update) | async-done | bytes 165904 | tf_op jit(solution)/shard_map/reduce_scatter | solution.py:120
  919.0 32.0 %reduce-scatter.36.cloned.1.call-done = bf16[144,1536]{1,0:T(8,128)(2,1)} async-done(((bf16[576,1536]{1,0:T(8,128)(2,1)}), bf16[144,1536]{1,0:T(8,128)(2,1)}) %reduce-scatter.36.cloned.1.call-update) | async-done | bytes 442384 | tf_op jit(solution)/shard_map/reduce_scatter | solution.py:128
  951.0 31.9 %reduce-scatter.38.cloned.1.call-done = bf16[144,1536]{1,0:T(8,128)(2,1)} async-done(((bf16[576,1536]{1,0:T(8,128)(2,1)}), bf16[144,1536]{1,0:T(8,128)(2,1)}) %reduce-scatter.38.cloned.1.call-update) | async-done | bytes 442384 | tf_op jit(solution)/shard_map/reduce_scatter | solution.py:131
  982.9 3.0 fusion.263
  988.8 31.8 %all-reduce.11.cloned.1.call-done = (bf16[1,144]{1,0:T(2,128)(2,1)}, bf16[1,144,192]{2,1,0:T(8,128)(2,1)}, bf16[1,144,192]{2,1,0:T(8,128)(2,1)}, bf16[1,144]{1,0:T(2,128)(2,1)}) async-done(((bf16[1,144]{1,0:T(2,128)(2,1)}, bf16[1,144,192]{2,1,0:T(8,128)(2,1)}, bf16[1,144,192]{2,1,0:T(8,128)(2,1)}, bf16[1,144]{1,0:T(2,128)(2,1)}), (bf16[1,144]{1,0:T(2,128)(2,1)}, bf16[1,144,192]{2,1,0:T(8,128)(2,1)}, ...) | async-done | bytes 111184 | tf_op jit(solution)/shard_map/psum | solution.py:408
  1026.2 72.7 %all-reduce.13.cloned.1.call-done = (bf16[1,144,576]{2,1,0:T(8,128)(2,1)}, bf16[1,144,576]{2,1,0:T(8,128)(2,1)}, bf16[1,144,1536]{2,1,0:T(8,128)(2,1)}, bf16[1,144,1536]{2,1,0:T(8,128)(2,1)}, bf16[1,384,576]{1,2,0:T(8,128)(2,1)}) async-done(((bf16[1,144,576]{2,1,0:T(8,128)(2,1)}, bf16[1,144,576]{2,1,0:T(8,128)(2,1)}, bf16[1,144,1536]{2,1,0:T(8,128)(2,1)}, bf16[1,144,1536]{2,1,0:T(8,128)(2,1)}, ...) | async-done | bytes 1658896 | tf_op jit(solution)/shard_map/psum | solution.py:409
  (799 shorter events, 260.4 us)
Async XLA Ops:
  7.2 10.2 copy-start.189
  7.2 10.2 copy-start.190
  7.2 10.2 copy-start.191
  7.2 19.5 %copy-start.2 = (bf16[1,2,1,512,576]{3,4,2,1,0:T(8,128)(2,1)S(1)}, bf16[1,2,1,512,576]{3,4,2,1,0:T(8,128)(2,1)}, u32[]{:S(2)}) copy-start(bf16[1,2,1,512,576]{3,4,2,1,0:T(8,128)(2,1)} %param.34) | copy-start | bytes 3538948
  7.2 123.4 %all-gather.13.cloned.1.call-start = ((), (), s32[]{:S(2)}) async-start(), calls=%async_computation.25 | async-start | bytes 2211840 | tf_op jit(solution)/shard_map/all_gather | solution.py:356
  8.0 127.4 %all-gather.15.cloned.1.call-start = ((), (), s32[]{:S(2)}) async-start(), calls=%async_computation.26 | async-start | bytes 2211840 | tf_op jit(solution)/shard_map/all_gather | solution.py:357
  8.7 133.0 %all-gather.17.cloned.1.call-start = ((), (), s32[]{:S(2)}) async-start(), calls=%async_computation.27 | async-start | bytes 2211840 | tf_op jit(solution)/shard_map/all_gather | solution.py:358
  9.4 446.4 %reduce-scatter.16.cloned.1.call-start = ((), (), s32[]{:S(2)}) async-start(), calls=%async_computation.13 | async-start | bytes 983040 | tf_op jit(solution)/shard_map/reduce_scatter | solution.py:303
  17.1 10.5 copy-start.54
  17.3 10.3 copy-start.163
  26.7 247.1 %copy-start.161 = (f32[576]{0:T(1024)}, f32[576]{0:T(1024)S(1)}, u32[]{:S(2)}) copy-start(f32[576]{0:T(1024)S(1)} %convert_element_type.841) | copy-start | bytes 6916
  26.9 29.4 %copy-start.174 = (f32[512]{0:T(512)}, f32[512]{0:T(512)S(1)}, u32[]{:S(2)}) copy-start(f32[512]{0:T(512)S(1)} %add_rsqrt_fusion.11) | copy-start | bytes 6148
  27.2 245.5 %copy-start.37 = (f32[512,32]{0,1:T(8,128)}, f32[512,32]{0,1:T(8,128)S(1)}, u32[]{:S(2)}) copy-start(f32[512,32]{0,1:T(8,128)S(1)} %get-tuple-element.1560) | copy-start | bytes 196612
  27.2 245.5 %copy-start.40 = (f32[512,32]{0,1:T(8,128)}, f32[512,32]{0,1:T(8,128)S(1)}, u32[]{:S(2)}) copy-start(f32[512,32]{0,1:T(8,128)S(1)} %get-tuple-element.1561) | copy-start | bytes 196612
  27.7 9.2 copy-start.168
  36.8 30.0 %copy-start.58 = (bf16[1,2048,3,64]{1,3,2,0:T(8,128)(2,1)}, bf16[1,2048,3,64]{1,3,2,0:T(8,128)(2,1)S(1)}, u32[]{:S(2)}) copy-start(bf16[1,2048,3,64]{1,3,2,0:T(8,128)(2,1)S(1)} %all_gather.47) | copy-start | bytes 2359300
  56.3 9.6 copy-start.88
  68.8 60.6 %copy-start.166 = (f32[576]{0:T(1024)}, f32[576]{0:T(1024)S(1)}, u32[]{:S(2)}) copy-start(f32[576]{0:T(1024)S(1)} %convert_element_type.842) | copy-start | bytes 6916
  88.2 40.9 %copy-start.11 = (f32[1,512,3,3,64]{1,4,3,2,0:T(8,128)}, f32[1,512,3,3,64]{1,4,3,2,0:T(8,128)S(1)}, u32[]{:S(2)}) copy-start(f32[1,512,3,3,64]{1,4,3,2,0:T(8,128)S(1)} %get-tuple-element.889) | copy-start | bytes 3538948
  88.3 40.9 %copy-start.115 = (f32[1,3,3,512]{3,2,1,0:T(4,128)}, f32[1,3,3,512]{3,2,1,0:T(4,128)S(1)}, u32[]{:S(2)}) copy-start(f32[1,3,3,512]{3,2,1,0:T(4,128)S(1)} %get-tuple-element.890) | copy-start | bytes 55300
  128.3 80.2 %copy-start.30 = (bf16[1,576,576]{2,1,0:T(8,128)(2,1)}, bf16[1,576,576]{2,1,0:T(8,128)(2,1)S(1)}, u32[]{:S(2)}) copy-start(bf16[1,576,576]{2,1,0:T(8,128)(2,1)S(1)} %all-gather.4) | copy-start | bytes 1990660
  145.1 16.6 %collective-permute-start = (bf16[1,512,576]{1,2,0:T(8,128)(2,1)S(1)}, bf16[1,512,576]{1,2,0:T(8,128)(2,1)S(1)}, u32[]{:S(2)}, u32[]{:S(2)}) collective-permute-start(bf16[1,512,576]{1,2,0:T(8,128)(2,1)S(1)} %fusion.269), channel_id=1, source_target_pairs={{0,16},{1,17},{2,18},{3,19},{4,20},{5,21},{6,22},{7,23},{8,24},{9,... | collective-permute-start | bytes 1769480 | tf_op jit(solution)/shard_map/ppermute | solution.py:21
  148.7 14.9 %copy-start.164 = (bf16[192,576]{1,0:T(8,128)(2,1)S(1)}, bf16[192,576]{1,0:T(8,128)(2,1)}, u32[]{:S(2)}) copy-start(bf16[192,576]{1,0:T(8,128)(2,1)} %copy-done.163) | copy-start | bytes 663556
  163.4 45.1 %copy-start.34 = (bf16[1,512,576]{1,2,0:T(8,128)(2,1)}, bf16[1,512,576]{1,2,0:T(8,128)(2,1)S(1)}, u32[]{:S(2)}) copy-start(bf16[1,512,576]{1,2,0:T(8,128)(2,1)S(1)} %get-tuple-element.1468) | copy-start | bytes 1769476
  175.4 11.6 %copy-start.111 = (bf16[1,512,9,32]{1,3,2,0:T(8,128)(2,1)}, bf16[1,512,9,32]{1,3,2,0:T(8,128)(2,1)S(1)}, u32[]{:S(2)}) copy-start(bf16[1,512,9,32]{1,3,2,0:T(8,128)(2,1)S(1)} %get-tuple-element.1520) | copy-start | bytes 884740
  175.4 11.6 %copy-start.113 = (bf16[1,512,9,32]{1,3,2,0:T(8,128)(2,1)}, bf16[1,512,9,32]{1,3,2,0:T(8,128)(2,1)S(1)}, u32[]{:S(2)}) copy-start(bf16[1,512,9,32]{1,3,2,0:T(8,128)(2,1)S(1)} %get-tuple-element.1521) | copy-start | bytes 884740
  175.4 10.5 copy-start.86
  207.6 126.1 %copy-start.13 = (f32[1,512,3,3,64]{1,4,3,2,0:T(8,128)}, f32[1,512,3,3,64]{1,4,3,2,0:T(8,128)S(1)}, u32[]{:S(2)}) copy-start(f32[1,512,3,3,64]{1,4,3,2,0:T(8,128)S(1)} %get-tuple-element.891) | copy-start | bytes 3538948
  220.6 13.6 %collective-permute-start.1 = (bf16[1,512,576]{1,2,0:T(8,128)(2,1)}, bf16[1,512,576]{1,2,0:T(8,128)(2,1)S(1)}, u32[]{:S(2)}, u32[]{:S(2)}) collective-permute-start(bf16[1,512,576]{1,2,0:T(8,128)(2,1)} %convert_bitcast_fusion.11), channel_id=1, source_target_pairs={{0,16},{1,17},{2,18},{3,19},{4,20},{5,21},{6,22},{7,23},{8,24},{9,... | collective-permute-start | bytes 1769480 | tf_op jit(solution)/shard_map/ppermute | solution.py:21
  234.2 39.5 %copy-start.48 = (bf16[1,512,576]{1,2,0:T(8,128)(2,1)}, bf16[1,512,576]{1,2,0:T(8,128)(2,1)S(1)}, u32[]{:S(2)}) copy-start(bf16[1,512,576]{1,2,0:T(8,128)(2,1)S(1)} %collective-permute-done.1) | copy-start | bytes 1769476
  234.4 39.3 %copy-start.176 = (f32[512]{0:T(512)}, f32[512]{0:T(512)S(1)}, u32[]{:S(2)}) copy-start(f32[512]{0:T(512)S(1)} %add_rsqrt_fusion.7) | copy-start | bytes 6148
  365.7 116.5 %reduce-scatter.18.cloned.1.call-start = ((), (), s32[]{:S(2)}) async-start(), calls=%async_computation.14 | async-start | bytes 983040 | tf_op jit(solution)/shard_map/reduce_scatter | solution.py:306
  367.9 241.8 %reduce-scatter.20.cloned.1.call-start = ((), (), s32[]{:S(2)}) async-start(), calls=%async_computation.15 | async-start | bytes 983040 | tf_op jit(solution)/shard_map/reduce_scatter | solution.py:303
  369.7 87.9 %copy-start.55 = (bf16[1,576,192]{2,1,0:T(8,128)(2,1)S(1)}, bf16[1,576,192]{2,1,0:T(8,128)(2,1)}, u32[]{:S(2)}) copy-start(bf16[1,576,192]{2,1,0:T(8,128)(2,1)} %copy-done.54) | copy-start | bytes 663556
  456.9 25.3 %copy-start.73 = (bf16[1,512,576]{1,2,0:T(8,128)(2,1)S(1)}, bf16[1,512,576]{1,2,0:T(8,128)(2,1)}, u32[]{:S(2)}) copy-start(bf16[1,512,576]{1,2,0:T(8,128)(2,1)} %get-tuple-element.1541) | copy-start | bytes 1769476
  456.9 25.3 %copy-start.162 = (f32[576]{0:T(1024)S(1)}, f32[576]{0:T(1024)}, u32[]{:S(2)}) copy-start(f32[576]{0:T(1024)} %copy-done.161) | copy-start | bytes 6916
  486.1 17.3 %collective-permute-start.2 = (bf16[512,576]{0,1:T(8,128)(2,1)}, bf16[512,576]{0,1:T(8,128)(2,1)S(1)}, u32[]{:S(2)}, u32[]{:S(2)}) collective-permute-start(bf16[512,576]{0,1:T(8,128)(2,1)} %fusion.283), channel_id=1, source_target_pairs={{16,0},{17,1},{18,2},{19,3},{20,4},{21,5},{22,6},{23,7},{24,8},{25... | collective-permute-start | bytes 1769480 | tf_op jit(solution)/shard_map/ppermute | solution.py:21
  487.7 15.7 %copy-start.194 = (bf16[1,1536,576]{1,2,0:T(8,128)(2,1)S(1)}, bf16[1,1536,576]{1,2,0:T(8,128)(2,1)}, u32[]{:S(2)}) copy-start(bf16[1,1536,576]{1,2,0:T(8,128)(2,1)} %all-gather.17.cloned.1.call-done) | copy-start | bytes 5308420
  503.4 12.4 %copy-start.98 = (bf16[512,576]{0,1:T(8,128)(2,1)}, bf16[512,576]{0,1:T(8,128)(2,1)S(1)}, u32[]{:S(2)}) copy-start(bf16[512,576]{0,1:T(8,128)(2,1)S(1)} %collective-permute-done.2) | copy-start | bytes 1769476
  503.4 7.4 copy-start.202
  548.9 87.3 %reduce-scatter.22.cloned.1.call-start = ((), (), s32[]{:S(2)}) async-start(), calls=%async_computation.16 | async-start | bytes 983040 | tf_op jit(solution)/shard_map/reduce_scatter | solution.py:306
  550.0 210.3 %reduce-scatter.24.cloned.1.call-start = ((), (), s32[]{:S(2)}) async-start(), calls=%async_computation.17 | async-start | bytes 983040 | tf_op jit(solution)/shard_map/reduce_scatter | solution.py:303
  551.8 59.6 %copy-start.56 = (bf16[1,576,192]{2,1,0:T(8,128)(2,1)S(1)}, bf16[1,576,192]{2,1,0:T(8,128)(2,1)}, u32[]{:S(2)}) copy-start(bf16[1,576,192]{2,1,0:T(8,128)(2,1)} %copy-done.54) | copy-start | bytes 663556
  610.7 25.5 %copy-start.68 = (bf16[1,512,576]{1,2,0:T(8,128)(2,1)S(1)}, bf16[1,512,576]{1,2,0:T(8,128)(2,1)}, u32[]{:S(2)}) copy-start(bf16[1,512,576]{1,2,0:T(8,128)(2,1)} %get-tuple-element.1472) | copy-start | bytes 1769476
  636.2 21.3 %copy-start.207 = (f32[512,1536]{1,0:T(8,128)S(1)}, f32[512,1536]{1,0:T(8,128)}, u32[]{:S(2)}) copy-start(f32[512,1536]{1,0:T(8,128)} %copy-done.205) | copy-start | bytes 9437188
  639.0 18.5 %copy-start.204 = (f32[512,1536]{1,0:T(8,128)S(1)}, f32[512,1536]{1,0:T(8,128)}, u32[]{:S(2)}) copy-start(f32[512,1536]{1,0:T(8,128)} %fusion.220) | copy-start | bytes 9437188
  640.4 17.1 %collective-permute-start.3 = (bf16[512,576]{0,1:T(8,128)(2,1)S(1)}, bf16[512,576]{0,1:T(8,128)(2,1)S(1)}, u32[]{:S(2)}, u32[]{:S(2)}) collective-permute-start(bf16[512,576]{0,1:T(8,128)(2,1)S(1)} %get-tuple-element.1511), channel_id=1, source_target_pairs={{16,0},{17,1},{18,2},{19,3},{20,4},{21,5},{22,6},{23,7},{24,8},{25... | collective-permute-start | bytes 1769480 | tf_op jit(solution)/shard_map/ppermute | solution.py:21
  642.1 15.5 %copy-start.195 = (bf16[1,1536,576]{1,2,0:T(8,128)(2,1)S(1)}, bf16[1,1536,576]{1,2,0:T(8,128)(2,1)}, u32[]{:S(2)}) copy-start(bf16[1,1536,576]{1,2,0:T(8,128)(2,1)} %all-gather.17.cloned.1.call-done) | copy-start | bytes 5308420
  644.2 17.8 %copy-start.203 = (bf16[1,576,1536]{2,1,0:T(8,128)(2,1)S(1)}, bf16[1,576,1536]{2,1,0:T(8,128)(2,1)}, u32[]{:S(2)}) copy-start(bf16[1,576,1536]{2,1,0:T(8,128)(2,1)} %all-gather.15.cloned.1.call-done) | copy-start | bytes 5308420
  657.5 9.3 copy-start.125
  699.5 87.4 %reduce-scatter.26.cloned.1.call-start = ((), (), s32[]{:S(2)}) async-start(), calls=%async_computation.18 | async-start | bytes 983040 | tf_op jit(solution)/shard_map/reduce_scatter | solution.py:306
  705.6 128.3 %reduce-scatter.30.cloned.1.call-start = ((), (), s32[]{:S(2)}) async-start(), calls=%async_computation.20 | async-start | bytes 368640 | tf_op jit(solution)/shard_map/reduce_scatter | solution.py:114
  713.6 47.8 %copy-start.39 = (f32[512,32]{0,1:T(8,128)S(1)}, f32[512,32]{0,1:T(8,128)}, u32[]{:S(2)}) copy-start(f32[512,32]{0,1:T(8,128)} %copy-done.37) | copy-start | bytes 196612
  713.6 47.8 %copy-start.42 = (f32[512,32]{0,1:T(8,128)S(1)}, f32[512,32]{0,1:T(8,128)}, u32[]{:S(2)}) copy-start(f32[512,32]{0,1:T(8,128)} %copy-done.40) | copy-start | bytes 196612
  713.6 47.9 %copy-start.45 = (bf16[512,576]{0,1:T(8,128)(2,1)S(1)}, bf16[512,576]{0,1:T(8,128)(2,1)}, u32[]{:S(2)}) copy-start(bf16[512,576]{0,1:T(8,128)(2,1)} %get-tuple-element.1536) | copy-start | bytes 1769476
  762.6 71.3 %reduce-scatter.32.cloned.1.call-start = ((), (), s32[]{:S(2)}) async-start(), calls=%async_computation.21 | async-start | bytes 368640 | tf_op jit(solution)/shard_map/reduce_scatter | solution.py:117
  789.2 77.6 %reduce-scatter.40.cloned.1.call-start = ((), (), s32[]{:S(2)}) async-start(), calls=%async_computation.28 | async-start | bytes 2457600
  799.2 93.9 %reduce-scatter.28.cloned.1.call-start = ((), (), s32[]{:S(2)}) async-start(), calls=%async_computation.19 | async-start | bytes 921600 | tf_op jit(solution)/shard_map/reduce_scatter | solution.py:111
  804.6 114.5 %reduce-scatter.34.cloned.1.call-start = ((), (), s32[]{:S(2)}) async-start(), calls=%async_computation.22 | async-start | bytes 921600 | tf_op jit(solution)/shard_map/reduce_scatter | solution.py:120
  809.5 141.5 %reduce-scatter.36.cloned.1.call-start = ((), (), s32[]{:S(2)}) async-start(), calls=%async_computation.23 | async-start | bytes 2211840 | tf_op jit(solution)/shard_map/reduce_scatter | solution.py:128
  816.0 166.9 %reduce-scatter.38.cloned.1.call-start = ((), (), s32[]{:S(2)}) async-start(), calls=%async_computation.24 | async-start | bytes 2211840 | tf_op jit(solution)/shard_map/reduce_scatter | solution.py:131
  822.7 198.0 %all-reduce.11.cloned.1.call-start = ((), (), s32[]{:S(2)}) async-start(), calls=%async_computation.29 | async-start | bytes 299008 | tf_op jit(solution)/shard_map/psum | solution.py:408
  826.3 156.6 %copy-start.67 = (bf16[512,1536]{1,0:T(8,128)(2,1)S(1)}, bf16[512,1536]{1,0:T(8,128)(2,1)}, u32[]{:S(2)}) copy-start(bf16[512,1536]{1,0:T(8,128)(2,1)} %get-tuple-element.1509) | copy-start | bytes 4718596
  834.0 264.9 %all-reduce.13.cloned.1.call-start = ((), (), s32[]{:S(2)}) async-start(), calls=%async_computation.30 | async-start | bytes 3391488 | tf_op jit(solution)/shard_map/psum | solution.py:409
  (169 other events, 362.1 us)
Sparse Core Ops, SparseCore 0:
  9.6 24.6 all-gather.12
  35.9 21.9 all-gather.14
  59.4 20.7 all-gather.16
  365.8 89.9 reduce-scatter.15
  459.0 23.2 reduce-scatter.17
  549.1 60.5 reduce-scatter.19
  612.9 23.2 reduce-scatter.21
  699.7 60.6 reduce-scatter.23
  763.6 23.2 reduce-scatter.25
  789.8 20.2 reduce-scatter.29
  812.7 20.3 reduce-scatter.31
  836.1 30.5 reduce-scatter.39
  870.1 22.9 reduce-scatter.27
  896.0 22.9 reduce-scatter.33
  921.6 29.3 reduce-scatter.35
  953.5 29.3 reduce-scatter.37
  986.1 34.5 all-reduce.10
  1023.9 74.9 all-reduce.12
where the time goes:
time: 1130 us; the launch traced here: 1110 us
  waiting for transfers between devices  551 us (49%)
  matrix products  170 us (15%)
  blocking collectives  156 us (14%)
  local copies, waits for them, and re-layouts  117 us (10%)
  other arithmetic  55.6 us (5%)
  loops' own time  33.4 us (3%)
  between operations  18 us (2%)
  starting transfers between devices  12.7 us (1%)
    reduce_scatter x3, waiting for transfers between devices, backward_layer(): lax.psum_scatter(key_full.astype(jnp.bfloat16), 'shard', scatter_dimensio...  190 us
    psum x1, waiting for transfers between devices, on_device(): lax.psum(shares[1].astype(jnp.bfloat16), 'replica').astype(jnp.float32)  72.7 us
    reduce_scatter x3, waiting for transfers between devices, backward_layer(): lax.psum_scatter(value_full.astype(jnp.bfloat16), 'shard', scatter_dimens...  68.7 us
    all_gather x3, blocking collectives, forward_layer(): lax.all_gather(key_rot, 'shard', axis=1, tiled=True)  51.2 us
    unnamed x421, local copies, waits for them, and re-layouts  48 us
    dot_general x21, matrix products, weight_grad(): jnp.einsum('rd,rf->df', left_side, right_side, preferred_element_type=jnp...  41.4 us
    all_gather x1, blocking collectives, on_device(): lax.all_gather(params[4], 'shard', axis=0, tiled=True)  40 us
    ppermute x4, waiting for transfers between devices, shifted(): return lax.ppermute(shard, axis, pairs)  38.7 us
  transfers between devices with their start and end apart: 22, of which 16 were waited for; matrix products, arithmetic and copies ran while one was open for 11% of the time, Pallas kernels for 0%

commit v1 on v0

--- a/solution.py
+++ b/solution.py
@@ -418,9 +418,369 @@
     return (ends_out,) + tuple((share[None] for share in summed))
 
 
+def xor_send(value, axis, bits):
+    peers = lax.axis_size(axis)
+    return lax.ppermute(value, axis, [(i, i ^ bits) for i in range(peers)])
+
+
+def xor_sort(parts, index):
+    low_bit, high_bit = (index & 1) == 1, (index & 2) == 2
+    a, b, c, d = parts
+    pairs = (
+        jnp.where(low_bit, b, a),
+        jnp.where(low_bit, a, b),
+        jnp.where(low_bit, d, c),
+        jnp.where(low_bit, c, d),
+    )
+    return (
+        jnp.where(high_bit, pairs[2], pairs[0]),
+        jnp.where(high_bit, pairs[3], pairs[1]),
+        jnp.where(high_bit, pairs[0], pairs[2]),
+        jnp.where(high_bit, pairs[1], pairs[3]),
+    )
+
+
+def gather_xor(value):
+    crossed = xor_send(value, "shard", 2)
+    beside = xor_send(value, "shard", 1)
+    far = xor_send(crossed, "shard", 1)
+    return (value, beside, crossed, far)
+
+
+def gather_rows(value, index):
+    return jnp.concatenate(xor_sort(gather_xor(value), index), axis=0)
+
+
+def add_low(first, second):
+    return (first.astype(jnp.float32) + second.astype(jnp.float32)).astype(jnp.bfloat16)
+
+
+def reduce_to_owner(partial, index):
+    rows = partial.shape[0] // 4
+    blocks = partial.reshape(2, 2, rows, partial.shape[1])
+    core, chip = index & 1, index >> 1
+    kept = lax.dynamic_index_in_dim(blocks, core, 1, keepdims=False)
+    sent = lax.dynamic_index_in_dim(blocks, core ^ 1, 1, keepdims=False)
+    halves = add_low(kept, xor_send(sent, "shard", 1))
+    kept = lax.dynamic_index_in_dim(halves, chip, 0, keepdims=False)
+    sent = lax.dynamic_index_in_dim(halves, chip ^ 1, 0, keepdims=False)
+    return add_low(kept, xor_send(sent, "shard", 2))
+
+
+def reduce_replicas(value, replica, axis):
+    size = value.shape[axis] // 4
+
+    def quarter(number):
+        return lax.dynamic_slice_in_dim(value, number * size, size, axis)
+
+    total = quarter(replica).astype(jnp.float32)
+    for bits in (1, 2, 3):
+        total = total + xor_send(quarter(replica ^ bits), "replica", bits).astype(jnp.float32)
+    return total.astype(jnp.bfloat16)
+
+
+def gather_replicas(value, replica, axis):
+    parts = (value,) + tuple(xor_send(value, "replica", bits) for bits in (1, 2, 3))
+    return jnp.concatenate(xor_sort(parts, replica), axis=axis)
+
+
+def reduce_layer(partial, layer, index, replica, axis):
+    mine = reduce_replicas(reduce_to_owner(partial, index), replica, axis)
+    other = lax.ppermute(mine, "section", [(1 - layer, layer)])
+    return add_low(mine, other)
+
+
+def attend_forward(query_rot, blocks, index):
+    tok_count = query_rot.shape[0]
+    positions = index * tok_count + jnp.arange(tok_count, dtype=jnp.int32)
+    grouped = query_rot.reshape(1, tok_count, KV_HEADS, HEADS // KV_HEADS, HEAD)
+    key_width = KV_HEADS * HEAD
+    key_blocks = blocks[:, :, :key_width].reshape(4, 1, tok_count, KV_HEADS, HEAD)
+    value_blocks = blocks[:, :, key_width:].reshape(4, 1, tok_count, KV_HEADS, HEAD)
+    top = jnp.full((1, KV_HEADS, HEADS // KV_HEADS, tok_count), neg_large, jnp.float32)
+    total = jnp.zeros_like(top)
+    mixed = jnp.zeros(grouped.shape, jnp.float32)
+
+    def update(state, key_block, value_block, start):
+        top, total, mixed = state
+        scores, allowed = block_scores(grouped, key_block, start, positions)
+        new_top = jnp.maximum(top, jnp.max(scores, axis=-1))
+        weights_now = jnp.where(allowed, jnp.exp(scores - new_top[..., None]), 0.0)
+        factor = jnp.exp(top - new_top)
+        total = total * factor + jnp.sum(weights_now, axis=-1)
+        mixed = mixed * jnp.moveaxis(factor, 3, 1)[..., None] + jnp.einsum(
+            "skgtu,sukd->stkgd",
+            weights_now.astype(jnp.bfloat16),
+            value_block,
+            preferred_element_type=jnp.float32,
+        )
+        return (new_top, total, mixed)
+
+    state = (top, total, mixed)
+    for j in range(4):
+        owner = index ^ j
+        state = lax.cond(
+            owner <= index,
+            lambda s, j=j, o=owner: update(s, key_blocks[j], value_blocks[j], o * tok_count),
+            lambda s: s,
+            state,
+        )
+    top, total, mixed = state
+    attended = (mixed / jnp.moveaxis(total, 3, 1)[..., None]).reshape(tok_count, HEADS * HEAD)
+    return (attended.astype(jnp.bfloat16), attended, top + jnp.log(total))
+
+
+def attend_backward(query_rot, blocks, grad_heads, attended, log_total, index):
+    tok_count = query_rot.shape[0]
+    positions = index * tok_count + jnp.arange(tok_count, dtype=jnp.int32)
+    grouped = query_rot.reshape(1, tok_count, KV_HEADS, HEADS // KV_HEADS, HEAD)
+    key_width = KV_HEADS * HEAD
+    key_blocks = blocks[:, :, :key_width].reshape(4, 1, tok_count, KV_HEADS, HEAD)
+    value_blocks = blocks[:, :, key_width:].reshape(4, 1, tok_count, KV_HEADS, HEAD)
+    grads = grad_heads.reshape(grouped.shape)
+    delta = jnp.moveaxis(
+        jnp.sum(grads.astype(jnp.float32) * attended.reshape(grouped.shape), axis=-1), 1, 3
+    )
+
+    def update(grad_query, key_block, value_block, start):
+        scores, allowed = block_scores(grouped, key_block, start, positions)
+        probabilities = jnp.where(allowed, jnp.exp(scores - log_total[..., None]), 0.0)
+        grad_probs = jnp.einsum(
+            "stkgd,sukd->skgtu", grads, value_block, preferred_element_type=jnp.float32
+        )
+        grad_scores = (
+            probabilities * (grad_probs - delta[..., None]) * HEAD ** (-0.5)
+        ).astype(jnp.bfloat16)
+        grad_query = grad_query + jnp.einsum(
+            "skgtu,sukd->stkgd", grad_scores, key_block, preferred_element_type=jnp.float32
+        )
+        grad_key = jnp.einsum(
+            "skgtu,stkgd->sukd", grad_scores, grouped, preferred_element_type=jnp.float32
+        )
+        grad_value = jnp.einsum(
+            "skgtu,stkgd->sukd",
+            probabilities.astype(jnp.bfloat16),
+            grads,
+            preferred_element_type=jnp.float32,
+        )
+        both = jnp.concatenate(
+            [grad_key.reshape(tok_count, key_width), grad_value.reshape(tok_count, key_width)],
+            axis=1,
+        )
+        return (grad_query, both.astype(jnp.bfloat16))
+
+    grad_query = jnp.zeros(grouped.shape, jnp.float32)
+    parts = []
+    for j in range(4):
+        owner = index ^ j
+        grad_query, part = lax.cond(
+            owner <= index,
+            lambda g, j=j, o=owner: update(g, key_blocks[j], value_blocks[j], o * tok_count),
+            lambda g: (g, jnp.zeros((tok_count, 2 * key_width), jnp.bfloat16)),
+            grad_query,
+        )
+        parts.append(part)
+    return (grad_query.reshape(tok_count, HEADS * HEAD), jnp.stack(parts))
+
+
+def forward_pass(block_in, weights, tables, index):
+    gain_attn, w_in, w_out, gain_ffn, w_gate_up, w_down = weights
+    tok_count, model_width = block_in.shape
+    source = block_in.astype(jnp.float32)
+    normed = (source * rms_scale(source) * gain_attn).astype(jnp.bfloat16)
+    projected = linear(normed, w_in)
+    query_width, key_width = HEADS * HEAD, KV_HEADS * HEAD
+    query_rot = (
+        rotate(projected[:, :query_width].reshape(1, tok_count, HEADS, HEAD), tables)
+        .astype(jnp.bfloat16)
+        .reshape(tok_count, query_width)
+    )
+    key_rot = (
+        rotate(
+            projected[:, query_width : query_width + key_width].reshape(
+                1, tok_count, KV_HEADS, HEAD
+            ),
+            tables,
+        )
+        .astype(jnp.bfloat16)
+        .reshape(tok_count, key_width)
+    )
+    values = projected[:, query_width + key_width :].astype(jnp.bfloat16)
+    blocks = jnp.stack(gather_xor(jnp.concatenate([key_rot, values], axis=1)))
+    mixed_heads, attended, log_total = attend_forward(query_rot, blocks, index)
+    hidden = source + linear(mixed_heads, w_out)
+    normed_ffn = (hidden * rms_scale(hidden) * gain_ffn).astype(jnp.bfloat16)
+    gate_up = linear(normed_ffn, w_gate_up)
+    hidden_units = gate_up.shape[1] // 2
+    gate_pre, upper = gate_up[:, :hidden_units], gate_up[:, hidden_units:]
+    active = (gate_pre * jax.nn.sigmoid(gate_pre) * upper).astype(jnp.bfloat16)
+    result = hidden + linear(active, w_down)
+    kept = (
+        block_in, normed, query_rot, blocks, log_total, mixed_heads, attended,
+        hidden, normed_ffn, gate_up, active,
+    )
+    return (result, kept)
+
+
+def backward_ffn(kept, grad_out, weights):
+    gain_attn, w_in, w_out, gain_ffn, w_gate_up, w_down = weights
+    hidden, normed_ffn, gate_up, active = kept[7:]
+    hidden_units = gate_up.shape[1] // 2
+    gate_pre, upper = gate_up[:, :hidden_units], gate_up[:, hidden_units:]
+    grad_ffn_out = grad_out.astype(jnp.bfloat16)
+    grad_active = input_grad(grad_ffn_out, w_down)
+    sigmoid_gate = jax.nn.sigmoid(gate_pre)
+    grad_gate = (
+        grad_active * upper * sigmoid_gate * (1.0 + gate_pre * (1.0 - sigmoid_gate))
+    ).astype(jnp.bfloat16)
+    grad_upper = (grad_active * gate_pre * sigmoid_gate).astype(jnp.bfloat16)
+    grad_both = jnp.concatenate([grad_gate, grad_upper], axis=1)
+    g_down = weight_grad(active, grad_ffn_out).astype(jnp.bfloat16)
+    g_gate_up = weight_grad(normed_ffn, grad_both).astype(jnp.bfloat16)
+    grad_normed_ffn = input_grad(grad_both, w_gate_up)
+    grad_part, g_gain_ffn = rms_back(hidden, gain_ffn, grad_normed_ffn)
+    return (grad_out + grad_part, g_gain_ffn, g_gate_up, g_down)
+
+
+def backward_attention(kept, grad_hidden, weights, tables, index):
+    gain_attn, w_in, w_out, gain_ffn, w_gate_up, w_down = weights
+    block_in, normed, query_rot, blocks, log_total, mixed_heads, attended = kept[:7]
+    tok_count = block_in.shape[0]
+    source = block_in.astype(jnp.float32)
+    grad_attn = grad_hidden.astype(jnp.bfloat16)
+    g_out = weight_grad(mixed_heads, grad_attn)
+    grad_heads = input_grad(grad_attn, w_out).astype(jnp.bfloat16)
+    grad_query, parts = attend_backward(
+        query_rot, blocks, grad_heads, attended, log_total, index
+    )
+    received = xor_send(parts[1::2], "shard", 1)
+    own_sum = add_low(parts[0], received[0])
+    cross_sum = add_low(parts[2], received[1])
+    key_width = KV_HEADS * HEAD
+    grad_kv = own_sum.astype(jnp.float32) + xor_send(cross_sum, "shard", 2).astype(jnp.float32)
+    grad_query_rows = (
+        rotate_back(grad_query.reshape(1, tok_count, HEADS, HEAD), tables)
+        .astype(jnp.bfloat16)
+        .reshape(tok_count, HEADS * HEAD)
+    )
+    grad_key_rows = (
+        rotate_back(grad_kv[:, :key_width].reshape(1, tok_count, KV_HEADS, HEAD), tables)
+        .astype(jnp.bfloat16)
+        .reshape(tok_count, key_width)
+    )
+    grad_rows = jnp.concatenate(
+        [grad_query_rows, grad_key_rows, grad_kv[:, key_width:].astype(jnp.bfloat16)], axis=1
+    )
+    g_in = weight_grad(normed, grad_rows)
+    grad_normed = input_grad(grad_rows, w_in)
+    grad_part, g_gain_attn = rms_back(source, gain_attn, grad_normed)
+    return (grad_hidden + grad_part, g_gain_attn, g_in, g_out)
+
+
+def both_sections(
+    ends, attn_norm, w_query, w_key, w_value, w_out, ffn_norm, w_gate, w_up, w_down
+):
+    section = lax.axis_index("section")
+    leading = section == 0
+    index = lax.axis_index("shard")
+    replica = lax.axis_index("replica")
+    local = ends[0]
+    tok_count, model_width = local.shape[-2:]
+    own_pair = local.reshape(2, tok_count, model_width)
+    moved = xor_send(
+        lax.dynamic_index_in_dim(own_pair, 1 - section, 0, keepdims=False), "section", 1
+    )
+    stayed = lax.dynamic_index_in_dim(own_pair, section, 0, keepdims=False)
+    tokens = jnp.where(leading, stayed, moved)
+    cotangent = jnp.where(leading, moved, stayed)
+
+    attn_width = w_query.shape[2] + 2 * w_key.shape[2] + w_out.shape[2]
+    in_width = attn_width - w_out.shape[2]
+    gains = jnp.stack([attn_norm[0], ffn_norm[0]], axis=1)
+    groups = (
+        jnp.concatenate([w_query[0], w_key[0], w_value[0], w_out[0], gains], axis=1),
+        jnp.concatenate([w_gate[0], w_up[0]], axis=1),
+        w_down[0],
+    )
+    others = [xor_send(group, "section", 1) for group in groups]
+    layers = []
+    for layer in (0, 1):
+        held = (section == layer)
+        whole = [
+            gather_rows(jnp.where(held, group, other), index)
+            for group, other in zip(groups, others)
+        ]
+        attn = whole[0]
+        layers.append(
+            (
+                attn[:, attn_width].astype(jnp.float32),
+                attn[:, :in_width],
+                attn[:, in_width:attn_width],
+                attn[:, attn_width + 1].astype(jnp.float32),
+                whole[1],
+                whole[2],
+            )
+        )
+    positions = index * tok_count + jnp.arange(tok_count, dtype=jnp.int32)
+    tables = rotation_tables(positions)
+    middle, kept_first = forward_pass(tokens, layers[0], tables, index)
+    final, kept_second = forward_pass(middle.astype(jnp.bfloat16), layers[1], tables, index)
+    final_arrived = lax.ppermute(final.astype(jnp.bfloat16), "section", [(0, 1)])
+
+    grad = cotangent.astype(jnp.float32)
+    quarters = []
+    for layer, kept in ((1, kept_second), (0, kept_first)):
+        weights = layers[layer]
+        grad_hidden, g_gain_ffn, g_gate_up, g_down = backward_ffn(kept, grad, weights)
+        ffn_quarters = (
+            reduce_layer(g_gate_up, layer, index, replica, 1),
+            reduce_layer(g_down, layer, index, replica, 0),
+        )
+        grad, g_gain_attn, g_in, g_out = backward_attention(
+            kept, grad_hidden, weights, tables, index
+        )
+        pad = jnp.zeros((model_width, 2048 - attn_width - 2), jnp.float32)
+        packed = jnp.concatenate(
+            [g_in, g_out, g_gain_attn[:, None], g_gain_ffn[:, None], pad], axis=1
+        ).astype(jnp.bfloat16)
+        quarters.append((reduce_layer(packed, layer, index, replica, 1),) + ffn_quarters)
+        if layer == 1:
+            grad = grad.astype(jnp.bfloat16).astype(jnp.float32)
+    grad_arrived = lax.ppermute(grad.astype(jnp.bfloat16), "section", [(1, 0)])
+    attn_sum, gate_up_sum, down_sum = [
+        gather_replicas(jnp.where(leading, first, second), replica, axis).astype(jnp.float32)
+        for first, second, axis in zip(quarters[1], quarters[0], (1, 1, 0))
+    ]
+    ends_out = jnp.stack(
+        [
+            jnp.where(leading, grad, final_arrived.astype(jnp.float32)),
+            jnp.where(leading, grad_arrived.astype(jnp.float32), final),
+        ]
+    ).reshape(1, 2, 1, tok_count, model_width)
+    cuts = [w_query.shape[2], w_query.shape[2] + w_key.shape[2], in_width, attn_width]
+    g_query, g_key, g_value, g_out, _ = jnp.split(attn_sum, cuts, axis=1)
+    units = w_gate.shape[2]
+    return (
+        ends_out,
+        attn_sum[:, attn_width][None],
+        g_query[None],
+        g_key[None],
+        g_value[None],
+        g_out[None],
+        attn_sum[:, attn_width + 1][None],
+        gate_up_sum[:, :units][None],
+        gate_up_sum[:, units:][None],
+        down_sum[None],
+    )
+
+
 def solution(mesh):
+    balanced = (
+        mesh.shape["section"] == 2 and mesh.shape["replica"] == 4 and mesh.shape["shard"] == 4
+    )
+    program = both_sections if balanced else on_device
     return jax.shard_map(
-        on_device,
+        program,
         mesh=mesh,
         in_specs=(
             P("section", None, "replica", "shard", None),

time: 1130 us -> 660 us (0.58)
  waiting for transfers between devices: 551 us -> 203 us
  starting transfers between devices: 12.7 us -> 200 us
  blocking collectives: 156 us -> 0 us
  matrix products: 170 us -> 94.3 us
  local copies, waits for them, and re-layouts: 117 us -> 68.9 us
  loops' own time: 33.4 us -> 16.9 us
  between operations: 18 us -> 3.68 us
    reduce_scatter x12 -> x0, waiting for transfers between devices: 372 us -> none  [the longest x3 190 us: backward_layer(): lax.psum_scatter(key_full.astype(jnp.bfloat16), 'shard', scatter_dimensio...]
    ppermute x4 -> x79, starting transfers between devices: 11.3 us -> 200 us  [the longest x71 186 us: xor_send(): return lax.ppermute(value, axis, [(i, i ^ bits) for i in range(peers)])]
    ppermute x4 -> x79, waiting for transfers between devices: 38.7 us -> 203 us  [the longest x71 197 us: xor_send(): return lax.ppermute(value, axis, [(i, i ^ bits) for i in range(peers)])]
    all_gather x10 -> x0, blocking collectives: 143 us -> none  [the longest x3 51.2 us: forward_layer(): lax.all_gather(key_rot, 'shard', axis=1, tiled=True)]
    psum x2 -> x0, waiting for transfers between devices: 105 us -> none  [the longest x1 72.7 us: on_device(): lax.psum(shares[1].astype(jnp.bfloat16), 'replica').astype(jnp.float32)]
    unnamed x421 -> x270, local copies, waits for them, and re-layouts: 48 us -> 10.2 us
    unnamed x19 -> x0, waiting for transfers between devices: 35.1 us -> none
    dot_general x21 -> x8, matrix products: 41.4 us -> 19.4 us  [weight_grad(): jnp.einsum('rd,rf->df', left_side, right_side, preferred_element_type=jnp...]
  transfers between devices with their start and end apart: 22 -> 79, of which waited for: 16 -> 27; matrix products, arithmetic and copies ran while one was open for 11% -> 26% of each run, Pallas kernels for 0% -> 0%
where the time goes in v1:
time: 660 us; the launch traced here: 650 us
  waiting for transfers between devices  203 us (31%)
  starting transfers between devices  200 us (30%)
  matrix products  94.3 us (14%)
  local copies, waits for them, and re-layouts  68.9 us (10%)
  other arithmetic  63.4 us (10%)
  loops' own time  16.9 us (3%)
    ppermute x71, waiting for transfers between devices, xor_send(): return lax.ppermute(value, axis, [(i, i ^ bits) for i in range(peers)])  197 us
    ppermute x71, starting transfers between devices, xor_send(): return lax.ppermute(value, axis, [(i, i ^ bits) for i in range(peers)])  186 us
    dot_general x8, matrix products, input_grad(): jnp.einsum('rf,df->rd', gradient, weight, preferred_element_type=jnp.floa...  25.8 us
    dot_general x8, matrix products, weight_grad(): jnp.einsum('rd,rf->df', left_side, right_side, preferred_element_type=jnp...  19.4 us
    concatenate x13, local copies, waits for them, and re-layouts, both_sections(): jnp.concatenate([g_in, g_out, g_gain_attn[:, None], g_gain_ffn[:, None],...  16.6 us
    dot_general x8, matrix products, linear(): return jnp.dot(left_side, right_side, preferred_element_type=jnp.float32)  16.3 us
    convert_element_type x14, other arithmetic, add_low(): (first.astype(jnp.float32) + second.astype(jnp.float32)).astype(jnp.bfloa...  14.9 us
  transfers between devices with their start and end apart: 79, of which 27 were waited for; matrix products, arithmetic and copies ran while one was open for 26% of the time, Pallas kernels for 0%

profile of v1, /device:TPU:0, one launch (start us, length us, event | category | flops | bytes accessed | tf_op | source)
XLA Modules:
  0.0 650.3 jit_solution(8368321787032477764)
XLA Ops:
  0.6 3.0 collective-permute-start.12
  18.4 6.8 %collective-permute-done.1 = bf16[144,1538]{1,0:T(8,128)(2,1)} collective-permute-done((bf16[144,1538]{1,0:T(8,128)(2,1)S(1)}, bf16[144,1538]{1,0:T(8,128)(2,1)}, u32[]{:S(2)}, u32[]{:S(2)}) %collective-permute-start.1) | collective-permute-done | bytes 442976 | tf_op jit(solution)/shard_map/ppermute | solution.py:423
  26.4 11.4 %collective-permute-done = bf16[512,576]{0,1:T(8,128)(2,1)S(1)} collective-permute-done((bf16[512,576]{0,1:T(8,128)(2,1)S(1)}, bf16[512,576]{0,1:T(8,128)(2,1)S(1)}, u32[]{:S(2)}, u32[]{:S(2)}) %collective-permute-start) | collective-permute-done | bytes 589856 | tf_op jit(solution)/shard_map/ppermute | solution.py:423
  41.1 9.8 %collective-permute-done.13 = bf16[384,576]{0,1:T(8,128)(2,1)S(1)} collective-permute-done((bf16[384,576]{0,1:T(8,128)(2,1)S(1)}, bf16[384,576]{0,1:T(8,128)(2,1)S(1)}, u32[]{:S(2)}, u32[]{:S(2)}) %collective-permute-start.13) | collective-permute-done | bytes 442400 | tf_op jit(solution)/shard_map/ppermute | solution.py:423
  50.9 5.1 collective-permute-done.8
  56.0 2.7 broadcast_select_fusion
  64.6 7.6 %collective-permute-done.16 = bf16[144,1538]{1,0:T(8,128)(2,1)S(1)} collective-permute-done((bf16[144,1538]{1,0:T(8,128)(2,1)S(1)}, bf16[144,1538]{1,0:T(8,128)(2,1)S(1)}, u32[]{:S(2)}, u32[]{:S(2)}) %collective-permute-start.16) | collective-permute-done | bytes 442976 | tf_op jit(solution)/shard_map/ppermute | solution.py:423
  81.9 2.8 fusion.338
  87.6 33.1 %collective-permute-done.6 = bf16[512,384]{0,1:T(8,128)(2,1)S(1)} collective-permute-done((bf16[512,384]{0,1:T(8,128)(2,1)S(1)}, bf16[512,384]{0,1:T(8,128)(2,1)S(1)}, u32[]{:S(2)}, u32[]{:S(2)}) %collective-permute-start.6) | collective-permute-done | bytes 393248 | tf_op jit(solution)/shard_map/ppermute | solution.py:423
  125.3 8.0 %conditional.14 = ((f32[1,3,3,512]{3,2,1,0:T(4,128)}, f32[1,3,3,512]{3,2,1,0:T(4,128)}, f32[1,512,3,3,64]{1,4,3,2,0:T(8,128)S(1)})) conditional(s32[]{:T(128)} %convert_element_type.755, (f32[1,3,3,512]{3,2,1,0:T(4,128)}, f32[1,3,3,512]{3,2,1,0:T(4,128)}, f32[1,512,3,3,64]{1,4,3,2,0:T(8,128)S(1)}) %get-tuple-element.964, (s32[]{:T(128)}, ...), branch_computations={%region_11.12_spmd, %region_12.15_spmd} | conditional | flops 635516928 | bytes 33224836 | solution.py:522
  140.6 2.8 fusion.395
  149.6 9.2 %collective-permute-start.19 = (bf16[512,384]{0,1:T(8,128)(2,1)S(1)}, bf16[512,384]{0,1:T(8,128)(2,1)S(1)}, u32[]{:S(2)}, u32[]{:S(2)}) collective-permute-start(bf16[512,384]{0,1:T(8,128)(2,1)S(1)} %get-tuple-element.863), channel_id=1, source_target_pairs={{0,1},{1,0},{2,3},{3,2},{4,5},{5,4},{6,7},{7,6},{8,9},{9,8},{10,11... | collective-permute-start | bytes 1179656 | tf_op jit(solution)/shard_map/ppermute | solution.py:423
  158.8 10.9 %collective-permute-start.20 = (bf16[512,384]{0,1:T(8,128)(2,1)S(1)}, bf16[512,384]{0,1:T(8,128)(2,1)S(1)}, u32[]{:S(2)}, u32[]{:S(2)}) collective-permute-start(bf16[512,384]{0,1:T(8,128)(2,1)S(1)} %get-tuple-element.863), channel_id=1, source_target_pairs={{0,2},{1,3},{2,0},{3,1},{4,6},{5,7},{6,4},{7,5},{8,10},{9,11},{10,... | collective-permute-start | bytes 1179656 | tf_op jit(solution)/shard_map/ppermute | solution.py:423
  171.6 6.9 %broadcast_select_fusion.13 = (bf16[144,3072]{1,0:T(8,128)(2,1)}, bf16[144,3072]{1,0:T(8,128)(2,1)}, bf16[144,3072]{1,0:T(8,128)(2,1)}, bf16[144,3072]{1,0:T(8,128)(2,1)}) fusion(pred[]{:T(512)S(6)} %eq.13, bf16[144,3072]{1,0:T(8,128)(2,1)} %collective-permute-done.26, bf16[144,3072]{1,0:T(8,128)(2,1)} %collective-permute-done.25, pred[]{:T(512)S(6)} %eq.14, ...), kind=kLoop, calls=%fused_computation.522 | loop fusion | flops 3538944 | bytes 7077890 | tf_op jit(solution)/shard_map/jit(_where)/select_n | solution.py:436
  181.3 3.5 fusion.341
  188.8 2.8 multiply_reduce_fusion.6
  191.7 2.8 fusion.394
  194.6 9.6 %multiply_convert_fusion.4 = (bf16[512,1536]{1,0:T(8,128)(2,1)S(1)}, bf16[512,1536]{1,0:T(8,128)(2,1)S(1)}, bf16[512,1536]{1,0:T(8,128)(2,1)S(1)}) fusion(f32[512,3072]{1,0:T(8,128)S(1)} %fusion.394, bf16[512,576]{0,1:T(8,128)(2,1)S(1)} %copy-done.51, bf16[384,576]{0,1:T(8,128)(2,1)S(1)} %copy-done.117, bf16[384,576]{0,1:T(8,128)(2,1)S(1)} %copy-done.116, ...), kind=kOutput, calls=%fused_computation.382 | convolution fusion | flops 925630464 | bytes 13369344 | tf_op jit(solution)/shard_map/rf,df->rd/dot_general | solution.py:83
  204.2 2.8 multiply_reduce_fusion
  207.0 3.9 convolution_convert_fusion
  219.0 3.8 fusion.300
  226.0 4.8 reshape.1444
  235.3 4.2 collective-permute-start.32
  244.3 19.3 %collective-permute-start.28 = (bf16[2,512,384]{1,2,0:T(8,128)(2,1)S(1)}, bf16[2,512,384]{1,2,0:T(8,128)(2,1)S(1)}, u32[]{:S(2)}, u32[]{:S(2)}) collective-permute-start(bf16[2,512,384]{1,2,0:T(8,128)(2,1)S(1)} %slice.308), channel_id=1, source_target_pairs={{0,1},{1,0},{2,3},{3,2},{4,5},{5,4},{6,7},{7,6},{8,9},{9,8},{10,11... | collective-permute-start | bytes 2359304 | tf_op jit(solution)/shard_map/ppermute | solution.py:423
  264.9 3.6 constant_dynamic-slice_fusion.4
  269.7 6.2 fusion.368
  277.2 35.6 %collective-permute-start.29 = (bf16[512,384]{0,1:T(8,128)(2,1)S(1)}, bf16[512,384]{0,1:T(8,128)(2,1)S(1)}, u32[]{:S(2)}, u32[]{:S(2)}) collective-permute-start(bf16[512,384]{0,1:T(8,128)(2,1)S(1)} %fusion.388), channel_id=1, source_target_pairs={{0,2},{1,3},{2,0},{3,1},{4,6},{5,7},{6,4},{7,5},{8,10},{9,11},{10,... | collective-permute-start | bytes 1179656 | tf_op jit(solution)/shard_map/ppermute | solution.py:423
  313.9 8.8 %collective-permute-done.29 = bf16[512,384]{0,1:T(8,128)(2,1)S(1)} collective-permute-done((bf16[512,384]{0,1:T(8,128)(2,1)S(1)}, bf16[512,384]{0,1:T(8,128)(2,1)S(1)}, u32[]{:S(2)}, u32[]{:S(2)}) %collective-permute-start.29) | collective-permute-done | bytes 393248 | tf_op jit(solution)/shard_map/ppermute | solution.py:423
  327.4 3.1 multiply_convert_fusion.2
  332.8 3.8 convolution_convert_fusion.1
  339.3 2.7 convolution_convert_fusion.8
  342.3 3.3 fusion.371
  345.7 3.8 fusion.301
  356.0 2.6 convolution_convert_fusion.7
  361.6 5.1 conditional.23
  368.6 4.2 concatenate.314
  375.3 3.9 reshape.1443
  379.2 5.4 constant_dynamic-slice_fusion.9
  398.8 11.8 %collective-permute-start.30 = (bf16[2,512,384]{1,2,0:T(8,128)(2,1)S(1)}, bf16[2,512,384]{1,2,0:T(8,128)(2,1)S(1)}, u32[]{:S(2)}, u32[]{:S(2)}) collective-permute-start(bf16[2,512,384]{1,2,0:T(8,128)(2,1)S(1)} %slice.317), channel_id=1, source_target_pairs={{0,1},{1,0},{2,3},{3,2},{4,5},{5,4},{6,7},{7,6},{8,9},{9,8},{10,11... | collective-permute-start | bytes 2359304 | tf_op jit(solution)/shard_map/ppermute | solution.py:423
  410.6 3.7 collective-permute-start.40
  414.3 3.2 collective-permute-start.64
  421.7 23.1 %collective-permute-start.56 = (bf16[144,3072]{1,0:T(8,128)(2,1)}, bf16[144,3072]{1,0:T(8,128)(2,1)}, u32[]{:S(2)}, u32[]{:S(2)}) collective-permute-start(bf16[144,3072]{1,0:T(8,128)(2,1)} %dynamic-slice_bitcast_fusion.4), channel_id=1, source_target_pairs={{0,2},{1,3},{2,0},{3,1},{4,6},{5,7},{6,4},{7,5},{8,10},{9,11},{10,... | collective-permute-start | bytes 2654216 | tf_op jit(solution)/shard_map/ppermute | solution.py:423
  447.3 26.4 %collective-permute-done.31 = bf16[512,384]{0,1:T(8,128)(2,1)S(1)} collective-permute-done((bf16[512,384]{0,1:T(8,128)(2,1)S(1)}, bf16[512,384]{0,1:T(8,128)(2,1)S(1)}, u32[]{:S(2)}, u32[]{:S(2)}) %collective-permute-start.31) | collective-permute-done | bytes 393248 | tf_op jit(solution)/shard_map/ppermute | solution.py:423
  481.2 4.4 concatenate.310
  491.3 2.6 collective-permute-start.68
  498.5 3.4 collective-permute-done.68
  502.1 5.0 collective-permute-done.67
  510.0 4.3 collective-permute-done.69
  514.4 3.1 collective-permute-start.77
  518.9 3.2 collective-permute-done.78
  522.1 4.1 collective-permute-done.77
  526.2 3.7 collective-permute-start.59
  529.9 9.4 %collective-permute-start.58 = (bf16[144,768]{1,0:T(8,128)(2,1)S(1)}, bf16[144,768]{1,0:T(8,128)(2,1)S(1)}, u32[]{:S(2)}, u32[]{:S(2)}) collective-permute-start(bf16[144,768]{1,0:T(8,128)(2,1)S(1)} %get-tuple-element.827), channel_id=1, source_target_pairs={{0,8},{4,12},{8,0},{12,4},{1,9},{5,13},{9,1},{13,5},{2,10},{6,14},... | collective-permute-start | bytes 663560 | tf_op jit(solution)/shard_map/ppermute | solution.py:423
  541.9 5.7 collective-permute-done.58
  558.7 5.6 collective-permute-done.43
  566.9 12.9 %collective-permute-done.50 = bf16[144,3072]{1,0:T(8,128)(2,1)S(1)} collective-permute-done((bf16[144,3072]{1,0:T(8,128)(2,1)S(1)}, bf16[144,3072]{1,0:T(8,128)(2,1)S(1)}, u32[]{:S(2)}, u32[]{:S(2)}) %collective-permute-start.50) | collective-permute-done | bytes 884768 | tf_op jit(solution)/shard_map/ppermute | solution.py:423
  583.5 5.3 collective-permute-done.35
  593.5 10.1 %collective-permute-done.52 = bf16[144,768]{1,0:T(8,128)(2,1)S(1)} collective-permute-done((bf16[144,768]{1,0:T(8,128)(2,1)S(1)}, bf16[144,768]{1,0:T(8,128)(2,1)S(1)}, u32[]{:S(2)}, u32[]{:S(2)}) %collective-permute-start.52) | collective-permute-done | bytes 221216 | tf_op jit(solution)/shard_map/ppermute | solution.py:423
  605.1 6.9 %collective-permute-done.37 = bf16[144,512]{1,0:T(8,128)(2,1)S(1)} collective-permute-done((bf16[144,512]{1,0:T(8,128)(2,1)S(1)}, bf16[144,512]{1,0:T(8,128)(2,1)S(1)}, u32[]{:S(2)}, u32[]{:S(2)}) %collective-permute-start.37) | collective-permute-done | bytes 147488 | tf_op jit(solution)/shard_map/ppermute | solution.py:423
  619.4 2.9 collective-permute-start.47
  622.3 3.4 collective-permute-done.63
  625.7 3.4 collective-permute-start.46
  629.1 5.6 collective-permute-done.62
  636.4 10.4 %collective-permute-done.47 = bf16[144,512]{1,0:T(8,128)(2,1)S(1)} collective-permute-done((bf16[144,512]{1,0:T(8,128)(2,1)S(1)}, bf16[144,512]{1,0:T(8,128)(2,1)S(1)}, u32[]{:S(2)}, u32[]{:S(2)}) %collective-permute-start.47) | collective-permute-done | bytes 147488 | tf_op jit(solution)/shard_map/ppermute | solution.py:423
  (585 shorter events, 197.0 us)
Async XLA Ops:
  0.6 14.3 %collective-permute-start.12 = (bf16[384,576]{0,1:T(8,128)(2,1)}, bf16[384,576]{0,1:T(8,128)(2,1)}, u32[]{:S(2)}, u32[]{:S(2)}) collective-permute-start(bf16[384,576]{0,1:T(8,128)(2,1)} %bitcast.1655), channel_id=1, source_target_pairs={{0,16},{16,0},{1,17},{17,1},{2,18},{18,2},{3,19},{19,3},{4,20},{20... | collective-permute-start | bytes 1327112 | tf_op jit(solution)/shard_map/ppermute | solution.py:423
  6.6 18.6 %collective-permute-start.1 = (bf16[144,1538]{1,0:T(8,128)(2,1)S(1)}, bf16[144,1538]{1,0:T(8,128)(2,1)}, u32[]{:S(2)}, u32[]{:S(2)}) collective-permute-start(bf16[144,1538]{1,0:T(8,128)(2,1)S(1)} %concatenate.272), channel_id=1, source_target_pairs={{0,16},{16,0},{1,17},{17,1},{2,18},{18,2},{3,19},{19,3},{4,20},{20... | collective-permute-start | bytes 1328840 | tf_op jit(solution)/shard_map/ppermute | solution.py:423
  7.8 30.0 %collective-permute-start = (bf16[512,576]{0,1:T(8,128)(2,1)S(1)}, bf16[512,576]{0,1:T(8,128)(2,1)S(1)}, u32[]{:S(2)}, u32[]{:S(2)}) collective-permute-start(bf16[512,576]{0,1:T(8,128)(2,1)S(1)} %dynamic-slice_bitcast_fusion.8), channel_id=1, source_target_pairs={{0,16},{16,0},{1,17},{17,1},{2,18},{18,2},{3,19},{19,3},{4,20},{20... | collective-permute-start | bytes 1769480 | tf_op jit(solution)/shard_map/ppermute | solution.py:423
  12.0 44.0 %collective-permute-start.8 = (bf16[144,3072]{1,0:T(8,128)(2,1)}, bf16[144,3072]{1,0:T(8,128)(2,1)}, u32[]{:S(2)}, u32[]{:S(2)}) collective-permute-start(bf16[144,3072]{1,0:T(8,128)(2,1)} %pad_maximum_fusion.24), channel_id=1, source_target_pairs={{0,16},{16,0},{1,17},{17,1},{2,18},{18,2},{3,19},{19,3},{4,20},{20... | collective-permute-start | bytes 2654216 | tf_op jit(solution)/shard_map/ppermute | solution.py:423
  16.2 42.5 %collective-permute-start.24 = (bf16[384,576]{0,1:T(8,128)(2,1)S(1)}, bf16[384,576]{0,1:T(8,128)(2,1)S(1)}, u32[]{:S(2)}, u32[]{:S(2)}) collective-permute-start(bf16[384,576]{0,1:T(8,128)(2,1)S(1)} %get-tuple-element.831), channel_id=1, source_target_pairs={{0,1},{1,0},{2,3},{3,2},{4,5},{5,4},{6,7},{7,6},{8,9},{9,8},{10,11... | collective-permute-start | bytes 1327112 | tf_op jit(solution)/shard_map/ppermute | solution.py:423
  16.3 24.8 %collective-permute-start.22 = (bf16[384,576]{0,1:T(8,128)(2,1)S(1)}, bf16[384,576]{0,1:T(8,128)(2,1)S(1)}, u32[]{:S(2)}, u32[]{:S(2)}) collective-permute-start(bf16[384,576]{0,1:T(8,128)(2,1)S(1)} %get-tuple-element.831), channel_id=1, source_target_pairs={{0,2},{1,3},{2,0},{3,1},{4,6},{5,7},{6,4},{7,5},{8,10},{9,11},{10,... | collective-permute-start | bytes 1327112 | tf_op jit(solution)/shard_map/ppermute | solution.py:423
  25.2 37.3 %collective-permute-start.15 = (bf16[384,576]{0,1:T(8,128)(2,1)S(1)}, bf16[384,576]{0,1:T(8,128)(2,1)S(1)}, u32[]{:S(2)}, u32[]{:S(2)}) collective-permute-start(bf16[384,576]{0,1:T(8,128)(2,1)S(1)} %get-tuple-element.832), channel_id=1, source_target_pairs={{0,1},{1,0},{2,3},{3,2},{4,5},{5,4},{6,7},{7,6},{8,9},{9,8},{10,11... | collective-permute-start | bytes 1327112 | tf_op jit(solution)/shard_map/ppermute | solution.py:423
  37.8 13.2 %collective-permute-start.13 = (bf16[384,576]{0,1:T(8,128)(2,1)S(1)}, bf16[384,576]{0,1:T(8,128)(2,1)S(1)}, u32[]{:S(2)}, u32[]{:S(2)}) collective-permute-start(bf16[384,576]{0,1:T(8,128)(2,1)S(1)} %get-tuple-element.832), channel_id=1, source_target_pairs={{0,2},{1,3},{2,0},{3,1},{4,6},{5,7},{6,4},{7,5},{8,10},{9,11},{10,... | collective-permute-start | bytes 1327112 | tf_op jit(solution)/shard_map/ppermute | solution.py:423
  41.1 18.2 %collective-permute-start.2 = (bf16[144,1538]{1,0:T(8,128)(2,1)S(1)}, bf16[144,1538]{1,0:T(8,128)(2,1)S(1)}, u32[]{:S(2)}, u32[]{:S(2)}) collective-permute-start(bf16[144,1538]{1,0:T(8,128)(2,1)S(1)} %get-tuple-element.820), channel_id=1, source_target_pairs={{0,2},{1,3},{2,0},{3,1},{4,6},{5,7},{6,4},{7,5},{8,10},{9,11},{10,... | collective-permute-start | bytes 1328840 | tf_op jit(solution)/shard_map/ppermute | solution.py:423
  58.8 15.2 %collective-permute-start.4 = (bf16[144,1538]{1,0:T(8,128)(2,1)S(1)}, bf16[144,1538]{1,0:T(8,128)(2,1)S(1)}, u32[]{:S(2)}, u32[]{:S(2)}) collective-permute-start(bf16[144,1538]{1,0:T(8,128)(2,1)S(1)} %get-tuple-element.820), channel_id=1, source_target_pairs={{0,1},{1,0},{2,3},{3,2},{4,5},{5,4},{6,7},{7,6},{8,9},{9,8},{10,11... | collective-permute-start | bytes 1328840 | tf_op jit(solution)/shard_map/ppermute | solution.py:423
  59.3 13.0 %collective-permute-start.16 = (bf16[144,1538]{1,0:T(8,128)(2,1)S(1)}, bf16[144,1538]{1,0:T(8,128)(2,1)S(1)}, u32[]{:S(2)}, u32[]{:S(2)}) collective-permute-start(bf16[144,1538]{1,0:T(8,128)(2,1)S(1)} %get-tuple-element.819), channel_id=1, source_target_pairs={{0,2},{1,3},{2,0},{3,1},{4,6},{5,7},{6,4},{7,5},{8,10},{9,11},{10,... | collective-permute-start | bytes 1328840 | tf_op jit(solution)/shard_map/ppermute | solution.py:423
  61.0 13.2 %collective-permute-start.3 = (bf16[144,1538]{1,0:T(8,128)(2,1)S(1)}, bf16[144,1538]{1,0:T(8,128)(2,1)S(1)}, u32[]{:S(2)}, u32[]{:S(2)}) collective-permute-start(bf16[144,1538]{1,0:T(8,128)(2,1)S(1)} %collective-permute-done.2), channel_id=1, source_target_pairs={{0,1},{1,0},{2,3},{3,2},{4,5},{5,4},{6,7},{7,6},{8,9},{9,8},{10,11... | collective-permute-start | bytes 1328840 | tf_op jit(solution)/shard_map/ppermute | solution.py:423
  62.5 22.2 %collective-permute-start.18 = (bf16[144,1538]{1,0:T(8,128)(2,1)S(1)}, bf16[144,1538]{1,0:T(8,128)(2,1)S(1)}, u32[]{:S(2)}, u32[]{:S(2)}) collective-permute-start(bf16[144,1538]{1,0:T(8,128)(2,1)S(1)} %get-tuple-element.819), channel_id=1, source_target_pairs={{0,1},{1,0},{2,3},{3,2},{4,5},{5,4},{6,7},{7,6},{8,9},{9,8},{10,11... | collective-permute-start | bytes 1328840 | tf_op jit(solution)/shard_map/ppermute | solution.py:423
  63.1 108.5 %collective-permute-start.27 = (bf16[144,3072]{1,0:T(8,128)(2,1)}, bf16[144,3072]{1,0:T(8,128)(2,1)}, u32[]{:S(2)}, u32[]{:S(2)}) collective-permute-start(bf16[144,3072]{1,0:T(8,128)(2,1)} %get-tuple-element.801), channel_id=1, source_target_pairs={{0,1},{1,0},{2,3},{3,2},{4,5},{5,4},{6,7},{7,6},{8,9},{9,8},{10,11... | collective-permute-start | bytes 2654216 | tf_op jit(solution)/shard_map/ppermute | solution.py:423
  72.2 50.4 %collective-permute-start.25 = (bf16[144,3072]{1,0:T(8,128)(2,1)}, bf16[144,3072]{1,0:T(8,128)(2,1)}, u32[]{:S(2)}, u32[]{:S(2)}) collective-permute-start(bf16[144,3072]{1,0:T(8,128)(2,1)} %get-tuple-element.801), channel_id=1, source_target_pairs={{0,2},{1,3},{2,0},{3,1},{4,6},{5,7},{6,4},{7,5},{8,10},{9,11},{10,... | collective-permute-start | bytes 2654216 | tf_op jit(solution)/shard_map/ppermute | solution.py:423
  74.0 48.8 %collective-permute-start.9 = (bf16[144,3072]{1,0:T(8,128)(2,1)}, bf16[144,3072]{1,0:T(8,128)(2,1)}, u32[]{:S(2)}, u32[]{:S(2)}) collective-permute-start(bf16[144,3072]{1,0:T(8,128)(2,1)} %get-tuple-element.802), channel_id=1, source_target_pairs={{0,2},{1,3},{2,0},{3,1},{4,6},{5,7},{6,4},{7,5},{8,10},{9,11},{10,... | collective-permute-start | bytes 2654216 | tf_op jit(solution)/shard_map/ppermute | solution.py:423
  74.3 11.0 %collective-permute-start.17 = (bf16[144,1538]{1,0:T(8,128)(2,1)S(1)}, bf16[144,1538]{1,0:T(8,128)(2,1)S(1)}, u32[]{:S(2)}, u32[]{:S(2)}) collective-permute-start(bf16[144,1538]{1,0:T(8,128)(2,1)S(1)} %collective-permute-done.16), channel_id=1, source_target_pairs={{0,1},{1,0},{2,3},{3,2},{4,5},{5,4},{6,7},{7,6},{8,9},{9,8},{10,11... | collective-permute-start | bytes 1328840 | tf_op jit(solution)/shard_map/ppermute | solution.py:423
  84.7 37.4 %collective-permute-start.5 = (bf16[512,384]{0,1:T(8,128)(2,1)S(1)}, bf16[512,384]{0,1:T(8,128)(2,1)S(1)}, u32[]{:S(2)}, u32[]{:S(2)}) collective-permute-start(bf16[512,384]{0,1:T(8,128)(2,1)S(1)} %get-tuple-element.867), channel_id=1, source_target_pairs={{0,1},{1,0},{2,3},{3,2},{4,5},{5,4},{6,7},{7,6},{8,9},{9,8},{10,11... | collective-permute-start | bytes 1179656 | tf_op jit(solution)/shard_map/ppermute | solution.py:423
  85.3 35.3 %collective-permute-start.6 = (bf16[512,384]{0,1:T(8,128)(2,1)S(1)}, bf16[512,384]{0,1:T(8,128)(2,1)S(1)}, u32[]{:S(2)}, u32[]{:S(2)}) collective-permute-start(bf16[512,384]{0,1:T(8,128)(2,1)S(1)} %get-tuple-element.867), channel_id=1, source_target_pairs={{0,2},{1,3},{2,0},{3,1},{4,6},{5,7},{6,4},{7,5},{8,10},{9,11},{10,... | collective-permute-start | bytes 1179656 | tf_op jit(solution)/shard_map/ppermute | solution.py:423
  122.2 16.1 %collective-permute-start.11 = (bf16[144,3072]{1,0:T(8,128)(2,1)}, bf16[144,3072]{1,0:T(8,128)(2,1)}, u32[]{:S(2)}, u32[]{:S(2)}) collective-permute-start(bf16[144,3072]{1,0:T(8,128)(2,1)} %get-tuple-element.802), channel_id=1, source_target_pairs={{0,1},{1,0},{2,3},{3,2},{4,5},{5,4},{6,7},{7,6},{8,9},{9,8},{10,11... | collective-permute-start | bytes 2654216 | tf_op jit(solution)/shard_map/ppermute | solution.py:423
  122.7 48.9 %collective-permute-start.26 = (bf16[144,3072]{1,0:T(8,128)(2,1)}, bf16[144,3072]{1,0:T(8,128)(2,1)}, u32[]{:S(2)}, u32[]{:S(2)}) collective-permute-start(bf16[144,3072]{1,0:T(8,128)(2,1)} %collective-permute-done.25), channel_id=1, source_target_pairs={{0,1},{1,0},{2,3},{3,2},{4,5},{5,4},{6,7},{7,6},{8,9},{9,8},{10,11... | collective-permute-start | bytes 2654216 | tf_op jit(solution)/shard_map/ppermute | solution.py:423
  122.7 15.5 %collective-permute-start.10 = (bf16[144,3072]{1,0:T(8,128)(2,1)}, bf16[144,3072]{1,0:T(8,128)(2,1)}, u32[]{:S(2)}, u32[]{:S(2)}) collective-permute-start(bf16[144,3072]{1,0:T(8,128)(2,1)} %collective-permute-done.9), channel_id=1, source_target_pairs={{0,1},{1,0},{2,3},{3,2},{4,5},{5,4},{6,7},{7,6},{8,9},{9,8},{10,11... | collective-permute-start | bytes 2654216 | tf_op jit(solution)/shard_map/ppermute | solution.py:423
  149.6 35.2 %collective-permute-start.19 = (bf16[512,384]{0,1:T(8,128)(2,1)S(1)}, bf16[512,384]{0,1:T(8,128)(2,1)S(1)}, u32[]{:S(2)}, u32[]{:S(2)}) collective-permute-start(bf16[512,384]{0,1:T(8,128)(2,1)S(1)} %get-tuple-element.863), channel_id=1, source_target_pairs={{0,1},{1,0},{2,3},{3,2},{4,5},{5,4},{6,7},{7,6},{8,9},{9,8},{10,11... | collective-permute-start | bytes 1179656 | tf_op jit(solution)/shard_map/ppermute | solution.py:423
  158.8 22.0 %collective-permute-start.20 = (bf16[512,384]{0,1:T(8,128)(2,1)S(1)}, bf16[512,384]{0,1:T(8,128)(2,1)S(1)}, u32[]{:S(2)}, u32[]{:S(2)}) collective-permute-start(bf16[512,384]{0,1:T(8,128)(2,1)S(1)} %get-tuple-element.863), channel_id=1, source_target_pairs={{0,2},{1,3},{2,0},{3,1},{4,6},{5,7},{6,4},{7,5},{8,10},{9,11},{10,... | collective-permute-start | bytes 1179656 | tf_op jit(solution)/shard_map/ppermute | solution.py:423
  235.3 252.6 %collective-permute-start.32 = (bf16[512,576]{0,1:T(8,128)(2,1)}, bf16[512,576]{0,1:T(8,128)(2,1)}, u32[]{:S(2)}, u32[]{:S(2)}) collective-permute-start(bf16[512,576]{0,1:T(8,128)(2,1)} %get-tuple-element.891), channel_id=1, source_target_pairs={{0,16},{1,17},{2,18},{3,19},{4,20},{5,21},{6,22},{7,23},{8,24},{9,... | collective-permute-start | bytes 1769480 | tf_op jit(solution)/shard_map/ppermute | solution.py:728
  244.3 31.6 %collective-permute-start.28 = (bf16[2,512,384]{1,2,0:T(8,128)(2,1)S(1)}, bf16[2,512,384]{1,2,0:T(8,128)(2,1)S(1)}, u32[]{:S(2)}, u32[]{:S(2)}) collective-permute-start(bf16[2,512,384]{1,2,0:T(8,128)(2,1)S(1)} %slice.308), channel_id=1, source_target_pairs={{0,1},{1,0},{2,3},{3,2},{4,5},{5,4},{6,7},{7,6},{8,9},{9,8},{10,11... | collective-permute-start | bytes 2359304 | tf_op jit(solution)/shard_map/ppermute | solution.py:423
  268.8 44.0 %collective-permute-start.70 = (bf16[2,384,576]{1,2,0:T(8,128)(2,1)S(1)}, bf16[2,384,576]{1,2,0:T(8,128)(2,1)S(1)}, u32[]{:S(2)}, u32[]{:S(2)}) collective-permute-start(bf16[2,384,576]{1,2,0:T(8,128)(2,1)S(1)} %bitcast.1610), channel_id=1, source_target_pairs={{0,1},{1,0},{2,3},{3,2},{4,5},{5,4},{6,7},{7,6},{8,9},{9,8},{10,11... | collective-permute-start | bytes 2654216 | tf_op jit(solution)/shard_map/ppermute | solution.py:423
  269.3 149.0 %collective-permute-start.55 = (bf16[2,144,3072]{2,1,0:T(8,128)(2,1)}, bf16[2,144,3072]{2,1,0:T(8,128)(2,1)}, u32[]{:S(2)}, u32[]{:S(2)}) collective-permute-start(bf16[2,144,3072]{2,1,0:T(8,128)(2,1)} %dynamic-slice_bitcast_fusion), channel_id=1, source_target_pairs={{0,1},{1,0},{2,3},{3,2},{4,5},{5,4},{6,7},{7,6},{8,9},{9,8},{10,11... | collective-permute-start | bytes 5308424 | tf_op jit(solution)/shard_map/ppermute | solution.py:423
  277.2 45.5 %collective-permute-start.29 = (bf16[512,384]{0,1:T(8,128)(2,1)S(1)}, bf16[512,384]{0,1:T(8,128)(2,1)S(1)}, u32[]{:S(2)}, u32[]{:S(2)}) collective-permute-start(bf16[512,384]{0,1:T(8,128)(2,1)S(1)} %fusion.388), channel_id=1, source_target_pairs={{0,2},{1,3},{2,0},{3,1},{4,6},{5,7},{6,4},{7,5},{8,10},{9,11},{10,... | collective-permute-start | bytes 1179656 | tf_op jit(solution)/shard_map/ppermute | solution.py:423
  313.9 77.8 %collective-permute-start.71 = (bf16[384,576]{0,1:T(8,128)(2,1)}, bf16[384,576]{0,1:T(8,128)(2,1)}, u32[]{:S(2)}, u32[]{:S(2)}) collective-permute-start(bf16[384,576]{0,1:T(8,128)(2,1)} %dynamic-slice_bitcast_fusion.9), channel_id=1, source_target_pairs={{0,2},{1,3},{2,0},{3,1},{4,6},{5,7},{6,4},{7,5},{8,10},{9,11},{10,... | collective-permute-start | bytes 1327112 | tf_op jit(solution)/shard_map/ppermute | solution.py:423
  395.2 15.4 %collective-permute-start.74 = (bf16[96,576]{0,1:T(8,128)(2,1)S(1)}, bf16[96,576]{0,1:T(8,128)(2,1)S(1)}, u32[]{:S(2)}, u32[]{:S(2)}) collective-permute-start(bf16[96,576]{0,1:T(8,128)(2,1)S(1)} %get-tuple-element.858), channel_id=1, source_target_pairs={{0,12},{4,8},{8,4},{12,0},{1,13},{5,9},{9,5},{13,1},{2,14},{6,10},... | collective-permute-start | bytes 331784 | tf_op jit(solution)/shard_map/ppermute | solution.py:423
  397.7 16.6 %collective-permute-start.73 = (bf16[96,576]{0,1:T(8,128)(2,1)S(1)}, bf16[96,576]{0,1:T(8,128)(2,1)S(1)}, u32[]{:S(2)}, u32[]{:S(2)}) collective-permute-start(bf16[96,576]{0,1:T(8,128)(2,1)S(1)} %get-tuple-element.859), channel_id=1, source_target_pairs={{0,8},{4,12},{8,0},{12,4},{1,9},{5,13},{9,1},{13,5},{2,10},{6,14},... | collective-permute-start | bytes 331784 | tf_op jit(solution)/shard_map/ppermute | solution.py:423
  398.8 22.9 %collective-permute-start.30 = (bf16[2,512,384]{1,2,0:T(8,128)(2,1)S(1)}, bf16[2,512,384]{1,2,0:T(8,128)(2,1)S(1)}, u32[]{:S(2)}, u32[]{:S(2)}) collective-permute-start(bf16[2,512,384]{1,2,0:T(8,128)(2,1)S(1)} %slice.317), channel_id=1, source_target_pairs={{0,1},{1,0},{2,3},{3,2},{4,5},{5,4},{6,7},{7,6},{8,9},{9,8},{10,11... | collective-permute-start | bytes 2359304 | tf_op jit(solution)/shard_map/ppermute | solution.py:423
  410.6 75.0 %collective-permute-start.40 = (bf16[2,144,2048]{2,1,0:T(8,128)(2,1)}, bf16[2,144,2048]{2,1,0:T(8,128)(2,1)}, u32[]{:S(2)}, u32[]{:S(2)}) collective-permute-start(bf16[2,144,2048]{2,1,0:T(8,128)(2,1)} %dynamic-slice_bitcast_fusion.2), channel_id=1, source_target_pairs={{0,1},{1,0},{2,3},{3,2},{4,5},{5,4},{6,7},{7,6},{8,9},{9,8},{10,11... | collective-permute-start | bytes 3538952 | tf_op jit(solution)/shard_map/ppermute | solution.py:423
  414.3 31.7 %collective-permute-start.64 = (bf16[2,384,576]{1,2,0:T(8,128)(2,1)S(1)}, bf16[2,384,576]{1,2,0:T(8,128)(2,1)S(1)}, u32[]{:S(2)}, u32[]{:S(2)}) collective-permute-start(bf16[2,384,576]{1,2,0:T(8,128)(2,1)S(1)} %bitcast.1609), channel_id=1, source_target_pairs={{0,1},{1,0},{2,3},{3,2},{4,5},{5,4},{6,7},{7,6},{8,9},{9,8},{10,11... | collective-permute-start | bytes 2654216 | tf_op jit(solution)/shard_map/ppermute | solution.py:423
  418.3 131.3 %collective-permute-start.49 = (bf16[2,144,3072]{2,1,0:T(8,128)(2,1)}, bf16[2,144,3072]{2,1,0:T(8,128)(2,1)}, u32[]{:S(2)}, u32[]{:S(2)}) collective-permute-start(bf16[2,144,3072]{2,1,0:T(8,128)(2,1)} %dynamic-slice_bitcast_fusion.1), channel_id=1, source_target_pairs={{0,1},{1,0},{2,3},{3,2},{4,5},{5,4},{6,7},{7,6},{8,9},{9,8},{10,11... | collective-permute-start | bytes 5308424 | tf_op jit(solution)/shard_map/ppermute | solution.py:423
  421.7 86.9 %collective-permute-start.56 = (bf16[144,3072]{1,0:T(8,128)(2,1)}, bf16[144,3072]{1,0:T(8,128)(2,1)}, u32[]{:S(2)}, u32[]{:S(2)}) collective-permute-start(bf16[144,3072]{1,0:T(8,128)(2,1)} %dynamic-slice_bitcast_fusion.4), channel_id=1, source_target_pairs={{0,2},{1,3},{2,0},{3,1},{4,6},{5,7},{6,4},{7,5},{8,10},{9,11},{10,... | collective-permute-start | bytes 2654216 | tf_op jit(solution)/shard_map/ppermute | solution.py:423
  446.0 27.6 %collective-permute-start.31 = (bf16[512,384]{0,1:T(8,128)(2,1)S(1)}, bf16[512,384]{0,1:T(8,128)(2,1)S(1)}, u32[]{:S(2)}, u32[]{:S(2)}) collective-permute-start(bf16[512,384]{0,1:T(8,128)(2,1)S(1)} %fusion.386), channel_id=1, source_target_pairs={{0,2},{1,3},{2,0},{3,1},{4,6},{5,7},{6,4},{7,5},{8,10},{9,11},{10,... | collective-permute-start | bytes 1179656 | tf_op jit(solution)/shard_map/ppermute | solution.py:423
  473.6 16.0 %collective-permute-start.65 = (bf16[384,576]{0,1:T(8,128)(2,1)}, bf16[384,576]{0,1:T(8,128)(2,1)}, u32[]{:S(2)}, u32[]{:S(2)}) collective-permute-start(bf16[384,576]{0,1:T(8,128)(2,1)} %dynamic-slice_bitcast_fusion.10), channel_id=1, source_target_pairs={{0,2},{1,3},{2,0},{3,1},{4,6},{5,7},{6,4},{7,5},{8,10},{9,11},{10,... | collective-permute-start | bytes 1327112 | tf_op jit(solution)/shard_map/ppermute | solution.py:423
  493.9 13.2 %collective-permute-start.67 = (bf16[96,576]{0,1:T(8,128)(2,1)S(1)}, bf16[96,576]{0,1:T(8,128)(2,1)S(1)}, u32[]{:S(2)}, u32[]{:S(2)}) collective-permute-start(bf16[96,576]{0,1:T(8,128)(2,1)S(1)} %get-tuple-element.862), channel_id=1, source_target_pairs={{0,8},{4,12},{8,0},{12,4},{1,9},{5,13},{9,1},{13,5},{2,10},{6,14},... | collective-permute-start | bytes 331784 | tf_op jit(solution)/shard_map/ppermute | solution.py:423
  497.2 12.8 %collective-permute-start.75 = (bf16[96,576]{0,1:T(8,128)(2,1)S(1)}, bf16[96,576]{0,1:T(8,128)(2,1)S(1)}, u32[]{:S(2)}, u32[]{:S(2)}) collective-permute-start(bf16[96,576]{0,1:T(8,128)(2,1)S(1)} %copy-done.105), channel_id=1, source_target_pairs={{0,16},{1,17},{2,18},{3,19},{4,20},{5,21},{6,22},{7,23},{8,24},{9,... | collective-permute-start | bytes 331784 | tf_op jit(solution)/shard_map/ppermute | solution.py:489
  501.8 47.4 %collective-permute-start.41 = (bf16[144,2048]{1,0:T(8,128)(2,1)S(1)}, bf16[144,2048]{1,0:T(8,128)(2,1)S(1)}, u32[]{:S(2)}, u32[]{:S(2)}) collective-permute-start(bf16[144,2048]{1,0:T(8,128)(2,1)S(1)} %dynamic-slice_bitcast_fusion.6), channel_id=1, source_target_pairs={{0,2},{1,3},{2,0},{3,1},{4,6},{5,7},{6,4},{7,5},{8,10},{9,11},{10,... | collective-permute-start | bytes 1769480 | tf_op jit(solution)/shard_map/ppermute | solution.py:423
  514.4 11.8 %collective-permute-start.77 = (bf16[96,576]{0,1:T(8,128)(2,1)S(1)}, bf16[96,576]{0,1:T(8,128)(2,1)S(1)}, u32[]{:S(2)}, u32[]{:S(2)}) collective-permute-start(bf16[96,576]{0,1:T(8,128)(2,1)S(1)} %fusion.414), channel_id=1, source_target_pairs={{0,8},{4,12},{8,0},{12,4},{1,9},{5,13},{9,1},{13,5},{2,10},{6,14},... | collective-permute-start | bytes 331784 | tf_op jit(solution)/shard_map/ppermute | solution.py:423
  517.5 12.4 %collective-permute-start.76 = (bf16[96,576]{0,1:T(8,128)(2,1)S(1)}, bf16[96,576]{0,1:T(8,128)(2,1)S(1)}, u32[]{:S(2)}, u32[]{:S(2)}) collective-permute-start(bf16[96,576]{0,1:T(8,128)(2,1)S(1)} %fusion.414), channel_id=1, source_target_pairs={{0,12},{4,8},{8,4},{12,0},{1,13},{5,9},{9,5},{13,1},{2,14},{6,10},... | collective-permute-start | bytes 331784 | tf_op jit(solution)/shard_map/ppermute | solution.py:423
  522.1 18.5 %collective-permute-start.57 = (bf16[144,768]{1,0:T(8,128)(2,1)S(1)}, bf16[144,768]{1,0:T(8,128)(2,1)S(1)}, u32[]{:S(2)}, u32[]{:S(2)}) collective-permute-start(bf16[144,768]{1,0:T(8,128)(2,1)S(1)} %get-tuple-element.825), channel_id=1, source_target_pairs={{0,4},{4,0},{8,12},{12,8},{1,5},{5,1},{9,13},{13,9},{2,6},{6,2},{1... | collective-permute-start | bytes 663560 | tf_op jit(solution)/shard_map/ppermute | solution.py:423
  526.2 15.6 %collective-permute-start.59 = (bf16[144,768]{1,0:T(8,128)(2,1)S(1)}, bf16[144,768]{1,0:T(8,128)(2,1)S(1)}, u32[]{:S(2)}, u32[]{:S(2)}) collective-permute-start(bf16[144,768]{1,0:T(8,128)(2,1)S(1)} %get-tuple-element.826), channel_id=1, source_target_pairs={{0,12},{4,8},{8,4},{12,0},{1,13},{5,9},{9,5},{13,1},{2,14},{6,10},... | collective-permute-start | bytes 663560 | tf_op jit(solution)/shard_map/ppermute | solution.py:423
  529.9 17.7 %collective-permute-start.58 = (bf16[144,768]{1,0:T(8,128)(2,1)S(1)}, bf16[144,768]{1,0:T(8,128)(2,1)S(1)}, u32[]{:S(2)}, u32[]{:S(2)}) collective-permute-start(bf16[144,768]{1,0:T(8,128)(2,1)S(1)} %get-tuple-element.827), channel_id=1, source_target_pairs={{0,8},{4,12},{8,0},{12,4},{1,9},{5,13},{9,1},{13,5},{2,10},{6,14},... | collective-permute-start | bytes 663560 | tf_op jit(solution)/shard_map/ppermute | solution.py:423
  540.6 13.7 %collective-permute-start.33 = (bf16[512,576]{0,1:T(8,128)(2,1)S(1)}, bf16[512,576]{0,1:T(8,128)(2,1)S(1)}, u32[]{:S(2)}, u32[]{:S(2)}) collective-permute-start(bf16[512,576]{0,1:T(8,128)(2,1)S(1)} %get-tuple-element.782), channel_id=1, source_target_pairs={{16,0},{17,1},{18,2},{19,3},{20,4},{21,5},{22,6},{23,7},{24,8},{25... | collective-permute-start | bytes 1769480 | tf_op jit(solution)/shard_map/ppermute | solution.py:749
  541.9 24.0 %collective-permute-start.34 = (bf16[2,144,2048]{2,1,0:T(8,128)(2,1)S(1)}, bf16[2,144,2048]{2,1,0:T(8,128)(2,1)S(1)}, u32[]{:S(2)}, u32[]{:S(2)}) collective-permute-start(bf16[2,144,2048]{2,1,0:T(8,128)(2,1)S(1)} %dynamic-slice_bitcast_fusion.3), channel_id=1, source_target_pairs={{0,1},{1,0},{2,3},{3,2},{4,5},{5,4},{6,7},{7,6},{8,9},{9,8},{10,11... | collective-permute-start | bytes 3538952 | tf_op jit(solution)/shard_map/ppermute | solution.py:423
  547.8 65.6 %collective-permute-start.60 = (bf16[144,768]{1,0:T(8,128)(2,1)S(1)}, bf16[144,768]{1,0:T(8,128)(2,1)S(1)}, u32[]{:S(2)}, u32[]{:S(2)}) collective-permute-start(bf16[144,768]{1,0:T(8,128)(2,1)S(1)} %add_convert_fusion.5), channel_id=1, source_target_pairs={{0,16},{1,17},{2,18},{3,19},{4,20},{5,21},{6,22},{7,23},{8,24},{9,... | collective-permute-start | bytes 663560 | tf_op jit(solution)/shard_map/ppermute | solution.py:489
  557.2 22.6 %collective-permute-start.50 = (bf16[144,3072]{1,0:T(8,128)(2,1)S(1)}, bf16[144,3072]{1,0:T(8,128)(2,1)S(1)}, u32[]{:S(2)}, u32[]{:S(2)}) collective-permute-start(bf16[144,3072]{1,0:T(8,128)(2,1)S(1)} %dynamic-slice_bitcast_fusion.5), channel_id=1, source_target_pairs={{0,2},{1,3},{2,0},{3,1},{4,6},{5,7},{6,4},{7,5},{8,10},{9,11},{10,... | collective-permute-start | bytes 2654216 | tf_op jit(solution)/shard_map/ppermute | solution.py:423
  564.4 53.6 %collective-permute-start.45 = (bf16[144,512]{1,0:T(8,128)(2,1)S(1)}, bf16[144,512]{1,0:T(8,128)(2,1)S(1)}, u32[]{:S(2)}, u32[]{:S(2)}) collective-permute-start(bf16[144,512]{1,0:T(8,128)(2,1)S(1)} %add_convert_fusion.13), channel_id=1, source_target_pairs={{0,16},{1,17},{2,18},{3,19},{4,20},{5,21},{6,22},{7,23},{8,24},{9,... | collective-permute-start | bytes 442376 | tf_op jit(solution)/shard_map/ppermute | solution.py:489
  566.4 22.4 %collective-permute-start.35 = (bf16[144,2048]{1,0:T(8,128)(2,1)S(1)}, bf16[144,2048]{1,0:T(8,128)(2,1)S(1)}, u32[]{:S(2)}, u32[]{:S(2)}) collective-permute-start(bf16[144,2048]{1,0:T(8,128)(2,1)S(1)} %dynamic-slice_bitcast_fusion.7), channel_id=1, source_target_pairs={{0,2},{1,3},{2,0},{3,1},{4,6},{5,7},{6,4},{7,5},{8,10},{9,11},{10,... | collective-permute-start | bytes 1769480 | tf_op jit(solution)/shard_map/ppermute | solution.py:423
  580.0 10.9 %collective-permute-start.51 = (bf16[144,768]{1,0:T(8,128)(2,1)S(1)}, bf16[144,768]{1,0:T(8,128)(2,1)S(1)}, u32[]{:S(2)}, u32[]{:S(2)}) collective-permute-start(bf16[144,768]{1,0:T(8,128)(2,1)S(1)} %get-tuple-element.828), channel_id=1, source_target_pairs={{0,4},{4,0},{8,12},{12,8},{1,5},{5,1},{9,13},{13,9},{2,6},{6,2},{1... | collective-permute-start | bytes 663560 | tf_op jit(solution)/shard_map/ppermute | solution.py:423
  581.1 10.7 %collective-permute-start.53 = (bf16[144,768]{1,0:T(8,128)(2,1)S(1)}, bf16[144,768]{1,0:T(8,128)(2,1)S(1)}, u32[]{:S(2)}, u32[]{:S(2)}) collective-permute-start(bf16[144,768]{1,0:T(8,128)(2,1)S(1)} %get-tuple-element.829), channel_id=1, source_target_pairs={{0,12},{4,8},{8,4},{12,0},{1,13},{5,9},{9,5},{13,1},{2,14},{6,10},... | collective-permute-start | bytes 663560 | tf_op jit(solution)/shard_map/ppermute | solution.py:423
  588.8 14.8 %collective-permute-start.52 = (bf16[144,768]{1,0:T(8,128)(2,1)S(1)}, bf16[144,768]{1,0:T(8,128)(2,1)S(1)}, u32[]{:S(2)}, u32[]{:S(2)}) collective-permute-start(bf16[144,768]{1,0:T(8,128)(2,1)S(1)} %get-tuple-element.830), channel_id=1, source_target_pairs={{0,8},{4,12},{8,0},{12,4},{1,9},{5,13},{9,1},{13,5},{2,10},{6,14},... | collective-permute-start | bytes 663560 | tf_op jit(solution)/shard_map/ppermute | solution.py:423
  590.9 12.8 %collective-permute-start.36 = (bf16[144,512]{1,0:T(8,128)(2,1)S(1)}, bf16[144,512]{1,0:T(8,128)(2,1)S(1)}, u32[]{:S(2)}, u32[]{:S(2)}) collective-permute-start(bf16[144,512]{1,0:T(8,128)(2,1)S(1)} %get-tuple-element.846), channel_id=1, source_target_pairs={{0,4},{4,0},{8,12},{12,8},{1,5},{5,1},{9,13},{13,9},{2,6},{6,2},{1... | collective-permute-start | bytes 442376 | tf_op jit(solution)/shard_map/ppermute | solution.py:423
  591.8 13.3 %collective-permute-start.38 = (bf16[144,512]{1,0:T(8,128)(2,1)S(1)}, bf16[144,512]{1,0:T(8,128)(2,1)S(1)}, u32[]{:S(2)}, u32[]{:S(2)}) collective-permute-start(bf16[144,512]{1,0:T(8,128)(2,1)S(1)} %get-tuple-element.847), channel_id=1, source_target_pairs={{0,12},{4,8},{8,4},{12,0},{1,13},{5,9},{9,5},{13,1},{2,14},{6,10},... | collective-permute-start | bytes 442376 | tf_op jit(solution)/shard_map/ppermute | solution.py:423
  613.5 12.2 %collective-permute-start.63 = (bf16[144,768]{1,0:T(8,128)(2,1)S(1)}, bf16[144,768]{1,0:T(8,128)(2,1)S(1)}, u32[]{:S(2)}, u32[]{:S(2)}) collective-permute-start(bf16[144,768]{1,0:T(8,128)(2,1)S(1)} %fusion.408), channel_id=1, source_target_pairs={{0,4},{4,0},{8,12},{12,8},{1,5},{5,1},{9,13},{13,9},{2,6},{6,2},{1... | collective-permute-start | bytes 663560 | tf_op jit(solution)/shard_map/ppermute | solution.py:423
  614.6 20.2 %collective-permute-start.62 = (bf16[144,768]{1,0:T(8,128)(2,1)S(1)}, bf16[144,768]{1,0:T(8,128)(2,1)S(1)}, u32[]{:S(2)}, u32[]{:S(2)}) collective-permute-start(bf16[144,768]{1,0:T(8,128)(2,1)S(1)} %fusion.408), channel_id=1, source_target_pairs={{0,8},{4,12},{8,0},{12,4},{1,9},{5,13},{9,1},{13,5},{2,10},{6,14},... | collective-permute-start | bytes 663560 | tf_op jit(solution)/shard_map/ppermute | solution.py:423
  616.6 18.2 %collective-permute-start.61 = (bf16[144,768]{1,0:T(8,128)(2,1)S(1)}, bf16[144,768]{1,0:T(8,128)(2,1)S(1)}, u32[]{:S(2)}, u32[]{:S(2)}) collective-permute-start(bf16[144,768]{1,0:T(8,128)(2,1)S(1)} %fusion.408), channel_id=1, source_target_pairs={{0,12},{4,8},{8,4},{12,0},{1,13},{5,9},{9,5},{13,1},{2,14},{6,10},... | collective-permute-start | bytes 663560 | tf_op jit(solution)/shard_map/ppermute | solution.py:423
  619.3 17.1 %collective-permute-start.48 = (bf16[144,512]{1,0:T(8,128)(2,1)S(1)}, bf16[144,512]{1,0:T(8,128)(2,1)S(1)}, u32[]{:S(2)}, u32[]{:S(2)}) collective-permute-start(bf16[144,512]{1,0:T(8,128)(2,1)S(1)} %fusion.413), channel_id=1, source_target_pairs={{0,4},{4,0},{8,12},{12,8},{1,5},{5,1},{9,13},{13,9},{2,6},{6,2},{1... | collective-permute-start | bytes 442376 | tf_op jit(solution)/shard_map/ppermute | solution.py:423
  619.4 27.4 %collective-permute-start.47 = (bf16[144,512]{1,0:T(8,128)(2,1)S(1)}, bf16[144,512]{1,0:T(8,128)(2,1)S(1)}, u32[]{:S(2)}, u32[]{:S(2)}) collective-permute-start(bf16[144,512]{1,0:T(8,128)(2,1)S(1)} %fusion.413), channel_id=1, source_target_pairs={{0,8},{4,12},{8,0},{12,4},{1,9},{5,13},{9,1},{13,5},{2,10},{6,14},... | collective-permute-start | bytes 442376 | tf_op jit(solution)/shard_map/ppermute | solution.py:423
  625.7 21.1 %collective-permute-start.46 = (bf16[144,512]{1,0:T(8,128)(2,1)S(1)}, bf16[144,512]{1,0:T(8,128)(2,1)S(1)}, u32[]{:S(2)}, u32[]{:S(2)}) collective-permute-start(bf16[144,512]{1,0:T(8,128)(2,1)S(1)} %fusion.413), channel_id=1, source_target_pairs={{0,12},{4,8},{8,4},{12,0},{1,13},{5,9},{9,5},{13,1},{2,14},{6,10},... | collective-permute-start | bytes 442376 | tf_op jit(solution)/shard_map/ppermute | solution.py:423
  (150 other events, 1958.2 us)

commit v2 on v1

--- a/solution.py
+++ b/solution.py
@@ -3,6 +3,8 @@
 import jax
 import jax.numpy as jnp
 from jax import lax
+from jax.experimental import pallas as pl
+from jax.experimental.pallas import tpu as pltpu
 from jax.sharding import PartitionSpec as P
 
 HEADS = 9
@@ -484,107 +486,178 @@
     return jnp.concatenate(xor_sort(parts, replica), axis=axis)
 
 
-def reduce_layer(partial, layer, index, replica, axis):
-    mine = reduce_replicas(reduce_to_owner(partial, index), replica, axis)
-    other = lax.ppermute(mine, "section", [(1 - layer, layer)])
-    return add_low(mine, other)
+def reduce_sections(value, layer):
+    return add_low(value, lax.ppermute(value, "section", [(1 - layer, layer)]))
+
+
+def tied(*values):
+    return lax.optimization_barrier(values)
+
+
+WIDE = 50 * 2**20
+
+
+def nt_dot(left, right):
+    return lax.dot_general(left, right, (((1,), (1,)), ((), ())), preferred_element_type=jnp.float32)
+
+
+def tn_dot(left, right):
+    return lax.dot_general(left, right, (((0,), (0,)), ((), ())), preferred_element_type=jnp.float32)
+
+
+def head_columns(head, start=0):
+    return slice(start + head * HEAD, start + (head + 1) * HEAD)
+
+
+def over_blocks(index, update):
+    update(0, True)
+
+    def other(j, carry):
+        @pl.when((index ^ j) < index)
+        def _():
+            update(j, False)
+
+        return carry
+
+    lax.fori_loop(1, 4, other, 0)
+
+
+def causal(rows):
+    keys = lax.broadcasted_iota(jnp.int32, (rows, rows), 0)
+    queries = lax.broadcasted_iota(jnp.int32, (rows, rows), 1)
+    return keys <= queries
+
+
+def attend_forward_kernel(index_ref, q_ref, blocks_ref, mixed_ref, attended_ref, log_ref, top, total, acc):
+    rows = q_ref.shape[0]
+    group = HEADS // KV_HEADS
+
+    def update(j, own):
+        for kv in range(KV_HEADS):
+            keys = blocks_ref[j, :, head_columns(kv)]
+            values = blocks_ref[j, :, head_columns(kv, KV_HEADS * HEAD)]
+            for head in range(kv * group, (kv + 1) * group):
+                line = slice(head, head + 1)
+                scores = nt_dot(keys, q_ref[:, head_columns(head)] * HEAD ** (-0.5))
+                if own:
+                    scores = jnp.where(causal(rows), scores, neg_large)
+                    new_top = jnp.max(scores, axis=0, keepdims=True)
+                else:
+                    new_top = jnp.maximum(top[line, :], jnp.max(scores, axis=0, keepdims=True))
+                weights_now = jnp.exp(scores - new_top)
+                sums = jnp.sum(weights_now, axis=0, keepdims=True)
+                mixed = tn_dot(values, weights_now.astype(jnp.bfloat16))
+                if not own:
+                    factor = jnp.exp(top[line, :] - new_top)
+                    sums = sums + total[line, :] * factor
+                    mixed = mixed + acc[head_columns(head), :] * factor
+                top[line, :] = new_top
+                total[line, :] = sums
+                acc[head_columns(head), :] = mixed
+
+    over_blocks(index_ref[0], update)
+    log_ref[...] = jnp.zeros_like(log_ref)
+    for head in range(HEADS):
+        line = slice(head, head + 1)
+        log_ref[line, :] = top[line, :] + jnp.log(total[line, :])
+        acc[head_columns(head), :] = acc[head_columns(head), :] / total[line, :]
+    attended = acc[...].T
+    attended_ref[...] = attended
+    mixed_ref[...] = attended.astype(jnp.bfloat16)
+
+
+def attend_backward_kernel(
+    index_ref, q_ref, blocks_ref, grads_ref, attended_ref, log_ref, query_ref, parts_ref, acc, delta
+):
+    rows = q_ref.shape[0]
+    group = HEADS // KV_HEADS
+    width = KV_HEADS * HEAD
+    parts_ref[...] = jnp.zeros_like(parts_ref)
+    acc[...] = (grads_ref[...].astype(jnp.float32) * attended_ref[...]).T
+    for head in range(HEADS):
+        delta[head : head + 1, :] = jnp.sum(acc[head_columns(head), :], axis=0, keepdims=True)
+    acc[...] = jnp.zeros_like(acc)
+
+    def update(j, own):
+        for kv in range(KV_HEADS):
+            keys = blocks_ref[j, :, head_columns(kv)]
+            values = blocks_ref[j, :, head_columns(kv, width)]
+            key_sum = jnp.zeros((rows, HEAD), jnp.float32)
+            value_sum = jnp.zeros((rows, HEAD), jnp.float32)
+            for head in range(kv * group, (kv + 1) * group):
+                line = slice(head, head + 1)
+                query = q_ref[:, head_columns(head)]
+                grads = grads_ref[:, head_columns(head)]
+                scores = nt_dot(keys, query * HEAD ** (-0.5))
+                if own:
+                    scores = jnp.where(causal(rows), scores, neg_large)
+                probabilities = jnp.exp(scores - log_ref[line, :])
+                grad_probs = nt_dot(values, grads)
+                grad_scores = (
+                    probabilities * (grad_probs - delta[line, :]) * HEAD ** (-0.5)
+                ).astype(jnp.bfloat16)
+                acc[head_columns(head), :] += tn_dot(keys, grad_scores)
+                key_sum += jnp.dot(grad_scores, query, preferred_element_type=jnp.float32)
+                value_sum += jnp.dot(
+                    probabilities.astype(jnp.bfloat16), grads, preferred_element_type=jnp.float32
+                )
+            parts_ref[j, :, head_columns(kv)] = key_sum.astype(jnp.bfloat16)
+            parts_ref[j, :, head_columns(kv, width)] = value_sum.astype(jnp.bfloat16)
+
+    over_blocks(index_ref[0], update)
+    query_ref[...] = acc[...].T
+
+
+def in_vmem(count):
+    return [pl.BlockSpec(memory_space=pltpu.VMEM)] * count
 
 
 def attend_forward(query_rot, blocks, index):
-    tok_count = query_rot.shape[0]
-    positions = index * tok_count + jnp.arange(tok_count, dtype=jnp.int32)
-    grouped = query_rot.reshape(1, tok_count, KV_HEADS, HEADS // KV_HEADS, HEAD)
-    key_width = KV_HEADS * HEAD
-    key_blocks = blocks[:, :, :key_width].reshape(4, 1, tok_count, KV_HEADS, HEAD)
-    value_blocks = blocks[:, :, key_width:].reshape(4, 1, tok_count, KV_HEADS, HEAD)
-    top = jnp.full((1, KV_HEADS, HEADS // KV_HEADS, tok_count), neg_large, jnp.float32)
-    total = jnp.zeros_like(top)
-    mixed = jnp.zeros(grouped.shape, jnp.float32)
-
-    def update(state, key_block, value_block, start):
-        top, total, mixed = state
-        scores, allowed = block_scores(grouped, key_block, start, positions)
-        new_top = jnp.maximum(top, jnp.max(scores, axis=-1))
-        weights_now = jnp.where(allowed, jnp.exp(scores - new_top[..., None]), 0.0)
-        factor = jnp.exp(top - new_top)
-        total = total * factor + jnp.sum(weights_now, axis=-1)
-        mixed = mixed * jnp.moveaxis(factor, 3, 1)[..., None] + jnp.einsum(
-            "skgtu,sukd->stkgd",
-            weights_now.astype(jnp.bfloat16),
-            value_block,
-            preferred_element_type=jnp.float32,
-        )
-        return (new_top, total, mixed)
-
-    state = (top, total, mixed)
-    for j in range(4):
-        owner = index ^ j
-        state = lax.cond(
-            owner <= index,
-            lambda s, j=j, o=owner: update(s, key_blocks[j], value_blocks[j], o * tok_count),
-            lambda s: s,
-            state,
-        )
-    top, total, mixed = state
-    attended = (mixed / jnp.moveaxis(total, 3, 1)[..., None]).reshape(tok_count, HEADS * HEAD)
-    return (attended.astype(jnp.bfloat16), attended, top + jnp.log(total))
+    rows, width = query_rot.shape
+    return pl.pallas_call(
+        attend_forward_kernel,
+        out_shape=(
+            jax.ShapeDtypeStruct((rows, width), jnp.bfloat16),
+            jax.ShapeDtypeStruct((rows, width), jnp.float32),
+            jax.ShapeDtypeStruct((16, rows), jnp.float32),
+        ),
+        in_specs=[pl.BlockSpec(memory_space=pltpu.SMEM)] + in_vmem(2),
+        out_specs=tuple(in_vmem(3)),
+        scratch_shapes=[
+            pltpu.VMEM((16, rows), jnp.float32),
+            pltpu.VMEM((16, rows), jnp.float32),
+            pltpu.VMEM((width, rows), jnp.float32),
+        ],
+        compiler_params=pltpu.CompilerParams(vmem_limit_bytes=WIDE),
+        cost_estimate=pl.CostEstimate(
+            flops=16 * rows * rows * width, bytes_accessed=2**22, transcendentals=36 * rows * rows
+        ),
+    )(index[None], query_rot, blocks)
 
 
 def attend_backward(query_rot, blocks, grad_heads, attended, log_total, index):
-    tok_count = query_rot.shape[0]
-    positions = index * tok_count + jnp.arange(tok_count, dtype=jnp.int32)
-    grouped = query_rot.reshape(1, tok_count, KV_HEADS, HEADS // KV_HEADS, HEAD)
-    key_width = KV_HEADS * HEAD
-    key_blocks = blocks[:, :, :key_width].reshape(4, 1, tok_count, KV_HEADS, HEAD)
-    value_blocks = blocks[:, :, key_width:].reshape(4, 1, tok_count, KV_HEADS, HEAD)
-    grads = grad_heads.reshape(grouped.shape)
-    delta = jnp.moveaxis(
-        jnp.sum(grads.astype(jnp.float32) * attended.reshape(grouped.shape), axis=-1), 1, 3
-    )
-
-    def update(grad_query, key_block, value_block, start):
-        scores, allowed = block_scores(grouped, key_block, start, positions)
-        probabilities = jnp.where(allowed, jnp.exp(scores - log_total[..., None]), 0.0)
-        grad_probs = jnp.einsum(
-            "stkgd,sukd->skgtu", grads, value_block, preferred_element_type=jnp.float32
-        )
-        grad_scores = (
-            probabilities * (grad_probs - delta[..., None]) * HEAD ** (-0.5)
-        ).astype(jnp.bfloat16)
-        grad_query = grad_query + jnp.einsum(
-            "skgtu,sukd->stkgd", grad_scores, key_block, preferred_element_type=jnp.float32
-        )
-        grad_key = jnp.einsum(
-            "skgtu,stkgd->sukd", grad_scores, grouped, preferred_element_type=jnp.float32
-        )
-        grad_value = jnp.einsum(
-            "skgtu,stkgd->sukd",
-            probabilities.astype(jnp.bfloat16),
-            grads,
-            preferred_element_type=jnp.float32,
-        )
-        both = jnp.concatenate(
-            [grad_key.reshape(tok_count, key_width), grad_value.reshape(tok_count, key_width)],
-            axis=1,
-        )
-        return (grad_query, both.astype(jnp.bfloat16))
-
-    grad_query = jnp.zeros(grouped.shape, jnp.float32)
-    parts = []
-    for j in range(4):
-        owner = index ^ j
-        grad_query, part = lax.cond(
-            owner <= index,
-            lambda g, j=j, o=owner: update(g, key_blocks[j], value_blocks[j], o * tok_count),
-            lambda g: (g, jnp.zeros((tok_count, 2 * key_width), jnp.bfloat16)),
-            grad_query,
-        )
-        parts.append(part)
-    return (grad_query.reshape(tok_count, HEADS * HEAD), jnp.stack(parts))
-
-
-def forward_pass(block_in, weights, tables, index):
-    gain_attn, w_in, w_out, gain_ffn, w_gate_up, w_down = weights
+    rows, width = query_rot.shape
+    return pl.pallas_call(
+        attend_backward_kernel,
+        out_shape=(
+            jax.ShapeDtypeStruct((rows, width), jnp.float32),
+            jax.ShapeDtypeStruct(blocks.shape, jnp.bfloat16),
+        ),
+        in_specs=[pl.BlockSpec(memory_space=pltpu.SMEM)] + in_vmem(5),
+        out_specs=tuple(in_vmem(2)),
+        scratch_shapes=[
+            pltpu.VMEM((width, rows), jnp.float32),
+            pltpu.VMEM((16, rows), jnp.float32),
+        ],
+        compiler_params=pltpu.CompilerParams(vmem_limit_bytes=WIDE),
+        cost_estimate=pl.CostEstimate(
+            flops=40 * rows * rows * width, bytes_accessed=2**23, transcendentals=36 * rows * rows
+        ),
+    )(index[None], query_rot, blocks, grad_heads, attended, log_total)
+
+
+def forward_attention(block_in, weights, tables, index):
+    gain_attn, w_in, w_out, gain_ffn = weights
     tok_count, model_width = block_in.shape
     source = block_in.astype(jnp.float32)
     normed = (source * rms_scale(source) * gain_attn).astype(jnp.bfloat16)
@@ -607,6 +680,11 @@
     )
     values = projected[:, query_width + key_width :].astype(jnp.bfloat16)
     blocks = jnp.stack(gather_xor(jnp.concatenate([key_rot, values], axis=1)))
+    return (source, normed, query_rot, blocks)
+
+
+def forward_rest(source, normed, query_rot, blocks, weights, index):
+    gain_attn, w_in, w_out, gain_ffn, w_gate_up, w_down = weights
     mixed_heads, attended, log_total = attend_forward(query_rot, blocks, index)
     hidden = source + linear(mixed_heads, w_out)
     normed_ffn = (hidden * rms_scale(hidden) * gain_ffn).astype(jnp.bfloat16)
@@ -616,7 +694,7 @@
     active = (gate_pre * jax.nn.sigmoid(gate_pre) * upper).astype(jnp.bfloat16)
     result = hidden + linear(active, w_down)
     kept = (
-        block_in, normed, query_rot, blocks, log_total, mixed_heads, attended,
+        source, normed, query_rot, blocks, log_total, mixed_heads, attended,
         hidden, normed_ffn, gate_up, active,
     )
     return (result, kept)
@@ -642,17 +720,17 @@
     return (grad_out + grad_part, g_gain_ffn, g_gate_up, g_down)
 
 
-def backward_attention(kept, grad_hidden, weights, tables, index):
+def backward_attention(kept, grad_hidden, weights, tables, index, pending=()):
     gain_attn, w_in, w_out, gain_ffn, w_gate_up, w_down = weights
-    block_in, normed, query_rot, blocks, log_total, mixed_heads, attended = kept[:7]
-    tok_count = block_in.shape[0]
-    source = block_in.astype(jnp.float32)
+    source, normed, query_rot, blocks, log_total, mixed_heads, attended = kept[:7]
+    tok_count = source.shape[0]
     grad_attn = grad_hidden.astype(jnp.bfloat16)
     g_out = weight_grad(mixed_heads, grad_attn)
     grad_heads = input_grad(grad_attn, w_out).astype(jnp.bfloat16)
     grad_query, parts = attend_backward(
         query_rot, blocks, grad_heads, attended, log_total, index
     )
+    parts, pending = tied(parts, pending)
     received = xor_send(parts[1::2], "shard", 1)
     own_sum = add_low(parts[0], received[0])
     cross_sum = add_low(parts[2], received[1])
@@ -674,7 +752,7 @@
     g_in = weight_grad(normed, grad_rows)
     grad_normed = input_grad(grad_rows, w_in)
     grad_part, g_gain_attn = rms_back(source, gain_attn, grad_normed)
-    return (grad_hidden + grad_part, g_gain_attn, g_in, g_out)
+    return (grad_hidden + grad_part, g_gain_attn, g_in, g_out, pending)
 
 
 def both_sections(
@@ -702,50 +780,81 @@
         jnp.concatenate([w_gate[0], w_up[0]], axis=1),
         w_down[0],
     )
-    others = [xor_send(group, "section", 1) for group in groups]
-    layers = []
-    for layer in (0, 1):
-        held = (section == layer)
-        whole = [
-            gather_rows(jnp.where(held, group, other), index)
-            for group, other in zip(groups, others)
-        ]
-        attn = whole[0]
-        layers.append(
-            (
-                attn[:, attn_width].astype(jnp.float32),
-                attn[:, :in_width],
-                attn[:, in_width:attn_width],
-                attn[:, attn_width + 1].astype(jnp.float32),
-                whole[1],
-                whole[2],
-            )
-        )
     positions = index * tok_count + jnp.arange(tok_count, dtype=jnp.int32)
     tables = rotation_tables(positions)
-    middle, kept_first = forward_pass(tokens, layers[0], tables, index)
-    final, kept_second = forward_pass(middle.astype(jnp.bfloat16), layers[1], tables, index)
+    other_attn = xor_send(groups[0], "section", 1)
+    own_rest, other_attn = tied(groups[1:], other_attn)
+    other_rest = tuple(xor_send(group, "section", 1) for group in own_rest)
+
+    def of_layer(layer, own, other):
+        return jnp.where(section == layer, own, other)
+
+    def attn_weights(layer, own, other):
+        attn = gather_rows(of_layer(layer, own, other), index)
+        return (
+            attn[:, attn_width].astype(jnp.float32),
+            attn[:, :in_width],
+            attn[:, in_width:attn_width],
+            attn[:, attn_width + 1].astype(jnp.float32),
+        )
+
+    attn_first = attn_weights(0, groups[0], other_attn)
+    first_state = forward_attention(tokens, attn_first, tables, index)
+    first_rest, sent_blocks = tied(
+        tuple(of_layer(0, own, other) for own, other in zip(own_rest, other_rest)), first_state[3]
+    )
+    first_state = first_state[:3] + (sent_blocks,)
+    first_rest = tuple(gather_rows(group, index) for group in first_rest)
+    second_own, second_other, first_rest = tied(groups, (other_attn,) + other_rest, first_rest)
+    weights_first = attn_first + first_rest
+    attn_second = attn_weights(1, second_own[0], second_other[0])
+    middle, kept_first = forward_rest(*first_state, weights_first, index)
+    second_state = forward_attention(middle.astype(jnp.bfloat16), attn_second, tables, index)
+    second_rest = tuple(
+        gather_rows(of_layer(1, own, other), index)
+        for own, other in zip(second_own[1:], second_other[1:])
+    )
+    weights_second = attn_second + second_rest
+    final, kept_second = forward_rest(*second_state, weights_second, index)
     final_arrived = lax.ppermute(final.astype(jnp.bfloat16), "section", [(0, 1)])
 
-    grad = cotangent.astype(jnp.float32)
-    quarters = []
-    for layer, kept in ((1, kept_second), (0, kept_first)):
-        weights = layers[layer]
-        grad_hidden, g_gain_ffn, g_gate_up, g_down = backward_ffn(kept, grad, weights)
-        ffn_quarters = (
-            reduce_layer(g_gate_up, layer, index, replica, 1),
-            reduce_layer(g_down, layer, index, replica, 0),
-        )
-        grad, g_gain_attn, g_in, g_out = backward_attention(
-            kept, grad_hidden, weights, tables, index
-        )
+    def pack(g_in, g_out, g_gain_attn, g_gain_ffn):
         pad = jnp.zeros((model_width, 2048 - attn_width - 2), jnp.float32)
-        packed = jnp.concatenate(
+        return jnp.concatenate(
             [g_in, g_out, g_gain_attn[:, None], g_gain_ffn[:, None], pad], axis=1
         ).astype(jnp.bfloat16)
-        quarters.append((reduce_layer(packed, layer, index, replica, 1),) + ffn_quarters)
-        if layer == 1:
-            grad = grad.astype(jnp.bfloat16).astype(jnp.float32)
+
+    def over_shards(*partials):
+        return tuple(reduce_to_owner(partial, index) for partial in partials)
+
+    def over_replicas(gate_up, down):
+        return (reduce_replicas(gate_up, replica, 1), reduce_replicas(down, replica, 0))
+
+    grad_hidden, g_gain_ffn, g_gate_up, g_down = backward_ffn(
+        kept_second, cotangent.astype(jnp.float32), weights_second
+    )
+    ffn_second = over_shards(g_gate_up, g_down)
+    grad, g_gain_attn, g_in, g_out, _ = backward_attention(
+        kept_second, grad_hidden, weights_second, tables, index
+    )
+    grad, ffn_second = tied(grad.astype(jnp.bfloat16), ffn_second)
+    ffn_second = over_replicas(*ffn_second)
+    (attn_second_sum,) = over_shards(pack(g_in, g_out, g_gain_attn, g_gain_ffn))
+    grad_hidden, g_gain_ffn, g_gate_up, g_down = backward_ffn(
+        kept_first, grad.astype(jnp.float32), weights_first
+    )
+    grad_hidden, ffn_second, attn_second_sum = tied(grad_hidden, ffn_second, attn_second_sum)
+    ffn_second = tuple(reduce_sections(value, 1) for value in ffn_second)
+    attn_second_sum = reduce_sections(reduce_replicas(attn_second_sum, replica, 1), 1)
+    ffn_first = over_shards(g_gate_up, g_down)
+    grad, g_gain_attn, g_in, g_out, (ffn_first, ffn_second, attn_second_sum) = backward_attention(
+        kept_first, grad_hidden, weights_first, tables, index,
+        (ffn_first, ffn_second, attn_second_sum),
+    )
+    ffn_first = tuple(reduce_sections(value, 0) for value in over_replicas(*ffn_first))
+    (attn_first_sum,) = over_shards(pack(g_in, g_out, g_gain_attn, g_gain_ffn))
+    attn_first_sum = reduce_sections(reduce_replicas(attn_first_sum, replica, 1), 0)
+    quarters = ((attn_second_sum,) + ffn_second, (attn_first_sum,) + ffn_first)
     grad_arrived = lax.ppermute(grad.astype(jnp.bfloat16), "section", [(1, 0)])
     attn_sum, gate_up_sum, down_sum = [
         gather_replicas(jnp.where(leading, first, second), replica, axis).astype(jnp.float32)

time: 660 us -> 614 us (0.930)
  starting transfers between devices: 200 us -> 153 us
  matrix products: 94.3 us -> 51.5 us
  Pallas kernels: 0 us -> 33 us
  local copies, waits for them, and re-layouts: 68.9 us -> 93.2 us
  loops' own time: 16.9 us -> 0 us
  other arithmetic: 63.4 us -> 70.8 us
    ppermute x71, starting transfers between devices: 186 us -> 139 us  [xor_send(): return lax.ppermute(value, axis, [(i, i ^ bits) for i in range(peers)])]
    pallas_call x0 -> x4, Pallas kernels: none -> 33 us  [the longest x2 20.7 us: attend_backward(): pl.pallas_call(attend_backward_kernel, out_shape=(jax.ShapeDtypeStruct((r...]
    dot_general x12 -> x0, matrix products: 32.9 us -> none  [the longest x2 9.49 us: update(): jnp.einsum('skgtu,stkgd->sukd', probabilities.astype(jnp.bfloat16), grads...]
    another operation x12 -> x0, loops' own time: 16.9 us -> none  [the longest x6 9.98 us: attend_forward(): lax.cond(owner <= index, lambda s, j=j, o=owner: update(s, key_blocks[j],...]
    unnamed x270 -> x190, local copies, waits for them, and re-layouts: 10.2 us -> 19.6 us
    dot_general x8, matrix products: 25.8 us -> 19 us  [input_grad(): jnp.einsum('rf,df->rd', gradient, weight, preferred_element_type=jnp.floa...]
    another operation x10 -> x0, local copies, waits for them, and re-layouts: 6.76 us -> none
    convert_element_type x14 -> x17, other arithmetic: 14.9 us -> 17 us  [add_low(): (first.astype(jnp.float32) + second.astype(jnp.float32)).astype(jnp.bfloa...]
  transfers between devices with their start and end apart: 79 -> 79, of which waited for: 27 -> 29; matrix products, arithmetic and copies ran while one was open for 26% -> 27% of each run, Pallas kernels for 0% -> 4%
where the time goes in v2:
time: 614 us; the launch traced here: 605 us
  waiting for transfers between devices  201 us (33%)
  starting transfers between devices  153 us (25%)
  local copies, waits for them, and re-layouts  93.2 us (15%)
  other arithmetic  70.8 us (12%)
  matrix products  51.5 us (8%)
  Pallas kernels  33 us (5%)
    ppermute x71, waiting for transfers between devices, xor_send(): return lax.ppermute(value, axis, [(i, i ^ bits) for i in range(peers)])  193 us
    ppermute x71, starting transfers between devices, xor_send(): return lax.ppermute(value, axis, [(i, i ^ bits) for i in range(peers)])  139 us
    pallas_call x2, Pallas kernels, attend_backward(): pl.pallas_call(attend_backward_kernel, out_shape=(jax.ShapeDtypeStruct((r...  20.7 us
    unnamed x190, local copies, waits for them, and re-layouts  19.6 us
    dot_general x8, matrix products, input_grad(): jnp.einsum('rf,df->rd', gradient, weight, preferred_element_type=jnp.floa...  19 us
    dot_general x8, matrix products, weight_grad(): jnp.einsum('rd,rf->df', left_side, right_side, preferred_element_type=jnp...  17.9 us
    convert_element_type x17, other arithmetic, add_low(): (first.astype(jnp.float32) + second.astype(jnp.float32)).astype(jnp.bfloa...  17 us
    concatenate x15, local copies, waits for them, and re-layouts, pack(): jnp.concatenate([g_in, g_out, g_gain_attn[:, None], g_gain_ffn[:, None],...  14.7 us
  transfers between devices with their start and end apart: 79, of which 29 were waited for; matrix products, arithmetic and copies ran while one was open for 27% of the time, Pallas kernels for 4%

profile of v2, /device:TPU:0, one launch (start us, length us, event | category | flops | bytes accessed | tf_op | source)
XLA Modules:
  0.0 605.0 jit_solution(14219239457458546121)
XLA Ops:
  3.6 3.0 collective-permute-start.1
  9.9 8.6 %collective-permute-done.1 = bf16[144,1538]{1,0:T(8,128)(2,1)} collective-permute-done((bf16[144,1538]{1,0:T(8,128)(2,1)S(1)}, bf16[144,1538]{1,0:T(8,128)(2,1)}, u32[]{:S(2)}, u32[]{:S(2)}) %collective-permute-start.1) | collective-permute-done | bytes 442976 | tf_op jit(solution)/shard_map/ppermute | solution.py:425
  21.1 2.6 collective-permute-start.6
  23.8 6.1 %collective-permute-done.2 = bf16[144,1538]{1,0:T(8,128)(2,1)S(1)} collective-permute-done((bf16[144,1538]{1,0:T(8,128)(2,1)S(1)}, bf16[144,1538]{1,0:T(8,128)(2,1)S(1)}, u32[]{:S(2)}, u32[]{:S(2)}) %collective-permute-start.2) | collective-permute-done | bytes 442976 | tf_op jit(solution)/shard_map/ppermute | solution.py:425
  37.6 3.0 collective-permute-done.6
  41.4 5.2 collective-permute-done.8
  46.7 12.1 %collective-permute-done.5 = bf16[144,3072]{1,0:T(8,128)(2,1)} collective-permute-done((bf16[144,3072]{1,0:T(8,128)(2,1)S(1)}, bf16[144,3072]{1,0:T(8,128)(2,1)}, u32[]{:S(2)}, u32[]{:S(2)}) %collective-permute-start.5) | collective-permute-done | bytes 884768 | tf_op jit(solution)/shard_map/ppermute | solution.py:425
  65.9 6.2 %shard_map.177 = (bf16[512,576]{1,0:T(8,128)(2,1)S(1)}, f32[512,576]{1,0:T(8,128)S(1)}, f32[16,512]{1,0:T(8,128)S(1)}) custom-call(s32[1]{0:T(128)} %bitcast.2.index_ref, bf16[512,576]{1,0:T(8,128)(2,1)S(1)} %copy.80.q_ref, bf16[4,512,384]{2,1,0:T(8,128)(2,1)} %pad_maximum_fusion.12.blocks_ref), custom_call_target="tpu_custom_call" | custom-call | flops 2415919104 | bytes 4194304 | tf_op jit(solution)/shard_map/pallas_call | solution.py:617
  72.1 19.9 %collective-permute-done.13 = bf16[384,576]{0,1:T(8,128)(2,1)} collective-permute-done((bf16[384,576]{0,1:T(8,128)(2,1)}, bf16[384,576]{0,1:T(8,128)(2,1)}, u32[]{:S(2)}, u32[]{:S(2)}) %collective-permute-start.13) | collective-permute-done | bytes 442400 | tf_op jit(solution)/shard_map/ppermute | solution.py:425
  92.5 2.3 multiply_reduce_fusion.5
  96.9 2.4 broadcast_select_fusion.16
  105.8 2.2 broadcast_select_fusion
  109.4 2.8 fusion.78
  114.9 11.0 %collective-permute-done.16 = bf16[144,1538]{1,0:T(8,128)(2,1)S(1)} collective-permute-done((bf16[144,1538]{1,0:T(8,128)(2,1)S(1)}, bf16[144,1538]{1,0:T(8,128)(2,1)S(1)}, u32[]{:S(2)}, u32[]{:S(2)}) %collective-permute-start.16) | collective-permute-done | bytes 442976 | tf_op jit(solution)/shard_map/ppermute | solution.py:425
  137.3 7.7 %collective-permute-done.25 = bf16[144,3072]{1,0:T(8,128)(2,1)} collective-permute-done((bf16[144,3072]{1,0:T(8,128)(2,1)}, bf16[144,3072]{1,0:T(8,128)(2,1)}, u32[]{:S(2)}, u32[]{:S(2)}) %collective-permute-start.25) | collective-permute-done | bytes 884768 | tf_op jit(solution)/shard_map/ppermute | solution.py:425
  145.0 2.8 broadcast_select_fusion.48
  148.3 4.1 collective-permute-done.20
  154.5 2.6 pad_maximum_fusion.13.blocks_ref
  157.1 6.1 %shard_map.178 = (bf16[512,576]{1,0:T(8,128)(2,1)S(1)}, f32[512,576]{1,0:T(8,128)S(1)}, f32[16,512]{1,0:T(8,128)S(1)}) custom-call(s32[1]{0:T(128)} %bitcast.2.index_ref, bf16[512,576]{1,0:T(8,128)(2,1)S(1)} %copy.83.q_ref, bf16[4,512,384]{2,1,0:T(8,128)(2,1)} %pad_maximum_fusion.13.blocks_ref), custom_call_target="tpu_custom_call" | custom-call | flops 2415919104 | bytes 4194304 | tf_op jit(solution)/shard_map/pallas_call | solution.py:617
  164.5 2.7 broadcast_select_fusion.12
  167.2 2.8 fusion.50
  170.0 4.3 multiply_convert_fusion.4
  174.4 2.2 multiply_reduce_fusion.1
  176.6 3.8 convolution_convert_fusion.1
  187.1 10.5 %shard_map.179 = (f32[512,576]{1,0:T(8,128)S(1)}, bf16[4,512,384]{2,1,0:T(8,128)(2,1)}) custom-call(s32[1]{0:T(128)} %bitcast.2.index_ref, bf16[512,576]{1,0:T(8,128)(2,1)S(1)} %copy-done.1, bf16[4,512,384]{2,1,0:T(8,128)(2,1)} %pad_maximum_fusion.13.blocks_ref, bf16[512,576]{1,0:T(8,128)(2,1)S(1)} %copy-done.2, f32[512,576]{1,0:T(8,128)S(1)} %copy-done.6, ...), custom_call_target="tpu_custom_call" | custom-call | flops 6039797760 | bytes 8388608 | tf_op jit(solution)/shard_map/pallas_call | solution.py:640
  199.6 12.3 %collective-permute-start.28 = (bf16[2,512,384]{2,1,0:T(8,128)(2,1)}, bf16[2,512,384]{2,1,0:T(8,128)(2,1)}, u32[]{:S(2)}, u32[]{:S(2)}) collective-permute-start(bf16[2,512,384]{2,1,0:T(8,128)(2,1)} %slice.193), channel_id=1, source_target_pairs={{0,1},{1,0},{2,3},{3,2},{4,5},{5,4},{6,7},{7,6},{8,9},{9,8},{10,11... | collective-permute-start | bytes 2359304 | tf_op jit(solution)/shard_map/ppermute | solution.py:425
  211.9 2.3 convolution_convert_fusion.3
  214.2 4.9 reshape.421
  219.2 7.6 %constant_dynamic-slice_fusion.21 = (bf16[2,1,384,576]{2,1,0,3:T(2,128)(2,1)}, bf16[2,1,384,576]{2,1,0,3:T(2,128)(2,1)}) fusion(bf16[2,2,384,576]{2,1,0,3:T(2,128)(2,1)} %reshape.421, s32[]{:T(128)S(6)} %select_n.564, s32[]{:T(128)S(6)} %select_n.565), kind=kLoop, calls=%fused_computation.308 | loop fusion | bytes 3538952 | tf_op jit(solution)/shard_map/jit(dynamic_index_in_dim)/dynamic_slice | solution.py:464
  232.5 2.9 dynamic-slice_bitcast_fusion.1
  238.1 25.8 %collective-permute-start.29 = (bf16[512,384]{1,0:T(8,128)(2,1)S(1)}, bf16[512,384]{1,0:T(8,128)(2,1)S(1)}, u32[]{:S(2)}, u32[]{:S(2)}) collective-permute-start(bf16[512,384]{1,0:T(8,128)(2,1)S(1)} %fusion.52), channel_id=1, source_target_pairs={{0,2},{1,3},{2,0},{3,1},{4,6},{5,7},{6,4},{7,5},{8,10},{9,11},{10,... | collective-permute-start | bytes 1179656 | tf_op jit(solution)/shard_map/ppermute | solution.py:425
  265.1 8.8 %collective-permute-done.29 = bf16[512,384]{1,0:T(8,128)(2,1)S(1)} collective-permute-done((bf16[512,384]{1,0:T(8,128)(2,1)S(1)}, bf16[512,384]{1,0:T(8,128)(2,1)S(1)}, u32[]{:S(2)}, u32[]{:S(2)}) %collective-permute-start.29) | collective-permute-done | bytes 393248 | tf_op jit(solution)/shard_map/ppermute | solution.py:425
  282.7 5.3 concatenate.166
  292.2 2.3 fusion.1
  300.5 16.6 %collective-permute-done.31 = bf16[144,3072]{1,0:T(8,128)(2,1)S(1)} collective-permute-done((bf16[144,3072]{1,0:T(8,128)(2,1)S(1)}, bf16[144,3072]{1,0:T(8,128)(2,1)S(1)}, u32[]{:S(2)}, u32[]{:S(2)}) %collective-permute-start.31) | collective-permute-done | bytes 884768 | tf_op jit(solution)/shard_map/ppermute | solution.py:425
  317.4 2.9 multiply_convert_fusion.1
  320.4 2.3 convolution_convert_fusion.2
  323.4 3.2 multiply_reduce_fusion
  326.5 3.9 convolution_convert_fusion
  333.0 2.6 collective-permute-start.38
  337.3 4.8 reshape.424
  342.1 7.0 %constant_dynamic-slice_fusion.13 = (bf16[2,1,384,576]{2,1,0,3:T(2,128)(2,1)}, bf16[2,1,384,576]{2,1,0,3:T(2,128)(2,1)S(1)}) fusion(bf16[2,2,384,576]{2,1,0,3:T(2,128)(2,1)} %reshape.424, s32[]{:T(128)S(6)} %select_n.564, s32[]{:T(128)S(6)} %select_n.565), kind=kLoop, calls=%fused_computation.300 | loop fusion | bytes 3538952 | tf_op jit(solution)/shard_map/jit(dynamic_index_in_dim)/dynamic_slice | solution.py:464
  352.8 3.5 collective-permute-start.35
  358.8 10.9 %collective-permute-done.35 = bf16[144,768]{1,0:T(8,128)(2,1)S(1)} collective-permute-done((bf16[144,768]{1,0:T(8,128)(2,1)S(1)}, bf16[144,768]{1,0:T(8,128)(2,1)S(1)}, u32[]{:S(2)}, u32[]{:S(2)}) %collective-permute-start.35) | collective-permute-done | bytes 221216 | tf_op jit(solution)/shard_map/ppermute | solution.py:425
  373.7 4.8 collective-permute-start.48
  379.4 4.0 collective-permute-start.47
  386.9 10.2 %shard_map.180 = (f32[512,576]{1,0:T(8,128)S(1)}, bf16[4,512,384]{2,1,0:T(8,128)(2,1)}) custom-call(s32[1]{0:T(128)} %bitcast.2.index_ref, bf16[512,576]{1,0:T(8,128)(2,1)S(1)} %copy.80.q_ref, bf16[4,512,384]{2,1,0:T(8,128)(2,1)} %pad_maximum_fusion.12.blocks_ref, bf16[512,576]{1,0:T(8,128)(2,1)S(1)} %copy.97.grads_ref, f32[512,576]{1,0:T(8,128)S(1)} %copy-done.4, ...), custom_call_target="tpu_custom_call" | custom-call | flops 6039797760 | bytes 8388608 | tf_op jit(solution)/shard_map/pallas_call | solution.py:640
  401.5 2.6 collective-permute-done.50
  408.8 15.7 %collective-permute-start.43 = (bf16[144,3072]{1,0:T(8,128)(2,1)S(1)}, bf16[144,3072]{1,0:T(8,128)(2,1)S(1)}, u32[]{:S(2)}, u32[]{:S(2)}) collective-permute-start(bf16[144,3072]{1,0:T(8,128)(2,1)S(1)} %dynamic-slice_bitcast_fusion.4), channel_id=1, source_target_pairs={{0,2},{1,3},{2,0},{3,1},{4,6},{5,7},{6,4},{7,5},{8,10},{9,11},{10,... | collective-permute-start | bytes 2654216 | tf_op jit(solution)/shard_map/ppermute | solution.py:425
  428.8 22.2 %collective-permute-done.45 = bf16[384,576]{0,1:T(8,128)(2,1)S(1)} collective-permute-done((bf16[384,576]{0,1:T(8,128)(2,1)S(1)}, bf16[384,576]{0,1:T(8,128)(2,1)S(1)}, u32[]{:S(2)}, u32[]{:S(2)}) %collective-permute-start.45) | collective-permute-done | bytes 442400 | tf_op jit(solution)/shard_map/ppermute | solution.py:425
  454.1 3.3 collective-permute-start.52
  457.4 2.4 fusion.80
  473.2 2.4 collective-permute-start.74
  479.6 6.8 %collective-permute-done.73 = bf16[96,576]{0,1:T(8,128)(2,1)S(1)} collective-permute-done((bf16[96,576]{0,1:T(8,128)(2,1)S(1)}, bf16[96,576]{0,1:T(8,128)(2,1)S(1)}, u32[]{:S(2)}, u32[]{:S(2)}) %collective-permute-start.73) | collective-permute-done | bytes 110624 | tf_op jit(solution)/shard_map/ppermute | solution.py:425
  498.0 5.0 concatenate.174
  510.3 11.8 %collective-permute-start.77 = (bf16[96,576]{0,1:T(8,128)(2,1)S(1)}, bf16[96,576]{0,1:T(8,128)(2,1)S(1)}, u32[]{:S(2)}, u32[]{:S(2)}) collective-permute-start(bf16[96,576]{0,1:T(8,128)(2,1)S(1)} %fusion.66), channel_id=1, source_target_pairs={{0,8},{4,12},{8,0},{12,4},{1,9},{5,13},{9,1},{13,5},{2,10},{6,14},... | collective-permute-start | bytes 331784 | tf_op jit(solution)/shard_map/ppermute | solution.py:425
  522.1 6.7 %collective-permute-start.78 = (bf16[96,576]{0,1:T(8,128)(2,1)S(1)}, bf16[96,576]{0,1:T(8,128)(2,1)S(1)}, u32[]{:S(2)}, u32[]{:S(2)}) collective-permute-start(bf16[96,576]{0,1:T(8,128)(2,1)S(1)} %fusion.66), channel_id=1, source_target_pairs={{0,4},{4,0},{8,12},{12,8},{1,5},{5,1},{9,13},{13,9},{2,6},{6,2},{1... | collective-permute-start | bytes 331784 | tf_op jit(solution)/shard_map/ppermute | solution.py:425
  533.1 7.3 %collective-permute-done.78 = bf16[96,576]{0,1:T(8,128)(2,1)S(1)} collective-permute-done((bf16[96,576]{0,1:T(8,128)(2,1)S(1)}, bf16[96,576]{0,1:T(8,128)(2,1)S(1)}, u32[]{:S(2)}, u32[]{:S(2)}) %collective-permute-start.78) | collective-permute-done | bytes 110624 | tf_op jit(solution)/shard_map/ppermute | solution.py:425
  541.7 10.1 %collective-permute-done.70 = bf16[144,768]{1,0:T(8,128)(2,1)S(1)} collective-permute-done((bf16[144,768]{1,0:T(8,128)(2,1)S(1)}, bf16[144,768]{1,0:T(8,128)(2,1)S(1)}, u32[]{:S(2)}, u32[]{:S(2)}) %collective-permute-start.70) | collective-permute-done | bytes 221216 | tf_op jit(solution)/shard_map/ppermute | solution.py:425
  557.0 10.0 %collective-permute-done.57 = bf16[144,2048]{1,0:T(8,128)(2,1)S(1)} collective-permute-done((bf16[144,2048]{1,0:T(8,128)(2,1)S(1)}, bf16[144,2048]{1,0:T(8,128)(2,1)S(1)}, u32[]{:S(2)}, u32[]{:S(2)}) %collective-permute-start.57) | collective-permute-done | bytes 589856 | tf_op jit(solution)/shard_map/ppermute | solution.py:425
  567.3 2.6 collective-permute-start.59
  574.5 5.4 collective-permute-done.59
  581.5 7.3 %collective-permute-done.61 = bf16[144,512]{1,0:T(8,128)(2,1)S(1)} collective-permute-done((bf16[144,512]{1,0:T(8,128)(2,1)S(1)}, bf16[144,512]{1,0:T(8,128)(2,1)S(1)}, u32[]{:S(2)}, u32[]{:S(2)}) %collective-permute-start.61) | collective-permute-done | bytes 147488 | tf_op jit(solution)/shard_map/ppermute | solution.py:490
  597.0 4.5 collective-permute-done.63
  (479 shorter events, 190.3 us)
Async XLA Ops:
  3.6 14.9 %collective-permute-start.1 = (bf16[144,1538]{1,0:T(8,128)(2,1)S(1)}, bf16[144,1538]{1,0:T(8,128)(2,1)}, u32[]{:S(2)}, u32[]{:S(2)}) collective-permute-start(bf16[144,1538]{1,0:T(8,128)(2,1)S(1)} %concatenate.142), channel_id=1, source_target_pairs={{0,16},{16,0},{1,17},{17,1},{2,18},{18,2},{3,19},{19,3},{4,20},{20... | collective-permute-start | bytes 1328840 | tf_op jit(solution)/shard_map/ppermute | solution.py:425
  8.5 22.5 %collective-permute-start = (bf16[512,576]{0,1:T(8,128)(2,1)}, bf16[512,576]{0,1:T(8,128)(2,1)S(1)}, u32[]{:S(2)}, u32[]{:S(2)}) collective-permute-start(bf16[512,576]{0,1:T(8,128)(2,1)} %dynamic-slice_bitcast_fusion.8), channel_id=1, source_target_pairs={{0,16},{16,0},{1,17},{17,1},{2,18},{18,2},{3,19},{19,3},{4,20},{20... | collective-permute-start | bytes 1769480 | tf_op jit(solution)/shard_map/ppermute | solution.py:425
  18.6 11.4 %collective-permute-start.2 = (bf16[144,1538]{1,0:T(8,128)(2,1)S(1)}, bf16[144,1538]{1,0:T(8,128)(2,1)S(1)}, u32[]{:S(2)}, u32[]{:S(2)}) collective-permute-start(bf16[144,1538]{1,0:T(8,128)(2,1)S(1)} %broadcast_select_fusion.19), channel_id=1, source_target_pairs={{0,2},{1,3},{2,0},{3,1},{4,6},{5,7},{6,4},{7,5},{8,10},{9,11},{10,... | collective-permute-start | bytes 1328840 | tf_op jit(solution)/shard_map/ppermute | solution.py:425
  21.1 19.5 %collective-permute-start.6 = (bf16[384,576]{0,1:T(8,128)(2,1)}, bf16[384,576]{0,1:T(8,128)(2,1)}, u32[]{:S(2)}, u32[]{:S(2)}) collective-permute-start(bf16[384,576]{0,1:T(8,128)(2,1)} %bitcast.196), channel_id=1, source_target_pairs={{0,16},{16,0},{1,17},{17,1},{2,18},{18,2},{3,19},{19,3},{4,20},{20... | collective-permute-start | bytes 1327112 | tf_op jit(solution)/shard_map/ppermute | solution.py:425
  23.7 35.0 %collective-permute-start.5 = (bf16[144,3072]{1,0:T(8,128)(2,1)S(1)}, bf16[144,3072]{1,0:T(8,128)(2,1)}, u32[]{:S(2)}, u32[]{:S(2)}) collective-permute-start(bf16[144,3072]{1,0:T(8,128)(2,1)S(1)} %pad_maximum_fusion.16), channel_id=1, source_target_pairs={{0,16},{16,0},{1,17},{17,1},{2,18},{18,2},{3,19},{19,3},{4,20},{20... | collective-permute-start | bytes 2654216 | tf_op jit(solution)/shard_map/ppermute | solution.py:425
  35.5 11.2 %collective-permute-start.8 = (bf16[512,384]{1,0:T(8,128)(2,1)S(1)}, bf16[512,384]{1,0:T(8,128)(2,1)S(1)}, u32[]{:S(2)}, u32[]{:S(2)}) collective-permute-start(bf16[512,384]{1,0:T(8,128)(2,1)S(1)} %pad_maximum_fusion.27), channel_id=1, source_target_pairs={{0,2},{1,3},{2,0},{3,1},{4,6},{5,7},{6,4},{7,5},{8,10},{9,11},{10,... | collective-permute-start | bytes 1179656 | tf_op jit(solution)/shard_map/ppermute | solution.py:425
  41.4 18.5 %collective-permute-start.7 = (bf16[512,384]{1,0:T(8,128)(2,1)S(1)}, bf16[512,384]{1,0:T(8,128)(2,1)S(1)}, u32[]{:S(2)}, u32[]{:S(2)}) collective-permute-start(bf16[512,384]{1,0:T(8,128)(2,1)S(1)} %pad_maximum_fusion.27), channel_id=1, source_target_pairs={{0,1},{1,0},{2,3},{3,2},{4,5},{5,4},{6,7},{7,6},{8,9},{9,8},{10,11... | collective-permute-start | bytes 1179656 | tf_op jit(solution)/shard_map/ppermute | solution.py:425
  46.6 13.3 %collective-permute-start.9 = (bf16[512,384]{1,0:T(8,128)(2,1)S(1)}, bf16[512,384]{1,0:T(8,128)(2,1)S(1)}, u32[]{:S(2)}, u32[]{:S(2)}) collective-permute-start(bf16[512,384]{1,0:T(8,128)(2,1)S(1)} %collective-permute-done.8), channel_id=1, source_target_pairs={{0,1},{1,0},{2,3},{3,2},{4,5},{5,4},{6,7},{7,6},{8,9},{9,8},{10,11... | collective-permute-start | bytes 1179656 | tf_op jit(solution)/shard_map/ppermute | solution.py:425
  61.4 30.6 %collective-permute-start.10 = (bf16[144,3072]{1,0:T(8,128)(2,1)}, bf16[144,3072]{1,0:T(8,128)(2,1)}, u32[]{:S(2)}, u32[]{:S(2)}) collective-permute-start(bf16[144,3072]{1,0:T(8,128)(2,1)} %broadcast_select_fusion.17), channel_id=1, source_target_pairs={{0,2},{1,3},{2,0},{3,1},{4,6},{5,7},{6,4},{7,5},{8,10},{9,11},{10,... | collective-permute-start | bytes 2654216 | tf_op jit(solution)/shard_map/ppermute | solution.py:425
  64.5 27.5 %collective-permute-start.13 = (bf16[384,576]{0,1:T(8,128)(2,1)}, bf16[384,576]{0,1:T(8,128)(2,1)}, u32[]{:S(2)}, u32[]{:S(2)}) collective-permute-start(bf16[384,576]{0,1:T(8,128)(2,1)} %broadcast_select_fusion.53), channel_id=1, source_target_pairs={{0,2},{1,3},{2,0},{3,1},{4,6},{5,7},{6,4},{7,5},{8,10},{9,11},{10,... | collective-permute-start | bytes 1327112 | tf_op jit(solution)/shard_map/ppermute | solution.py:425
  65.4 29.5 %collective-permute-start.15 = (bf16[384,576]{0,1:T(8,128)(2,1)}, bf16[384,576]{0,1:T(8,128)(2,1)S(1)}, u32[]{:S(2)}, u32[]{:S(2)}) collective-permute-start(bf16[384,576]{0,1:T(8,128)(2,1)} %broadcast_select_fusion.53), channel_id=1, source_target_pairs={{0,1},{1,0},{2,3},{3,2},{4,5},{5,4},{6,7},{7,6},{8,9},{9,8},{10,11... | collective-permute-start | bytes 1327112 | tf_op jit(solution)/shard_map/ppermute | solution.py:425
  65.4 31.4 %collective-permute-start.12 = (bf16[144,3072]{1,0:T(8,128)(2,1)}, bf16[144,3072]{1,0:T(8,128)(2,1)S(1)}, u32[]{:S(2)}, u32[]{:S(2)}) collective-permute-start(bf16[144,3072]{1,0:T(8,128)(2,1)} %broadcast_select_fusion.17), channel_id=1, source_target_pairs={{0,1},{1,0},{2,3},{3,2},{4,5},{5,4},{6,7},{7,6},{8,9},{9,8},{10,11... | collective-permute-start | bytes 2654216 | tf_op jit(solution)/shard_map/ppermute | solution.py:425
  102.4 24.7 %collective-permute-start.22 = (bf16[384,576]{0,1:T(8,128)(2,1)}, bf16[384,576]{0,1:T(8,128)(2,1)}, u32[]{:S(2)}, u32[]{:S(2)}) collective-permute-start(bf16[384,576]{0,1:T(8,128)(2,1)} %broadcast_select_fusion.36), channel_id=1, source_target_pairs={{0,2},{1,3},{2,0},{3,1},{4,6},{5,7},{6,4},{7,5},{8,10},{9,11},{10,... | collective-permute-start | bytes 1327112 | tf_op jit(solution)/shard_map/ppermute | solution.py:425
  103.8 41.1 %collective-permute-start.24 = (bf16[384,576]{0,1:T(8,128)(2,1)}, bf16[384,576]{0,1:T(8,128)(2,1)}, u32[]{:S(2)}, u32[]{:S(2)}) collective-permute-start(bf16[384,576]{0,1:T(8,128)(2,1)} %broadcast_select_fusion.36), channel_id=1, source_target_pairs={{0,1},{1,0},{2,3},{3,2},{4,5},{5,4},{6,7},{7,6},{8,9},{9,8},{10,11... | collective-permute-start | bytes 1327112 | tf_op jit(solution)/shard_map/ppermute | solution.py:425
  104.9 21.0 %collective-permute-start.16 = (bf16[144,1538]{1,0:T(8,128)(2,1)S(1)}, bf16[144,1538]{1,0:T(8,128)(2,1)S(1)}, u32[]{:S(2)}, u32[]{:S(2)}) collective-permute-start(bf16[144,1538]{1,0:T(8,128)(2,1)S(1)} %broadcast_select_fusion.18), channel_id=1, source_target_pairs={{0,2},{1,3},{2,0},{3,1},{4,6},{5,7},{6,4},{7,5},{8,10},{9,11},{10,... | collective-permute-start | bytes 1328840 | tf_op jit(solution)/shard_map/ppermute | solution.py:425
  105.6 22.1 %collective-permute-start.18 = (bf16[144,1538]{1,0:T(8,128)(2,1)S(1)}, bf16[144,1538]{1,0:T(8,128)(2,1)S(1)}, u32[]{:S(2)}, u32[]{:S(2)}) collective-permute-start(bf16[144,1538]{1,0:T(8,128)(2,1)S(1)} %broadcast_select_fusion.18), channel_id=1, source_target_pairs={{0,1},{1,0},{2,3},{3,2},{4,5},{5,4},{6,7},{7,6},{8,9},{9,8},{10,11... | collective-permute-start | bytes 1328840 | tf_op jit(solution)/shard_map/ppermute | solution.py:425
  108.0 37.0 %collective-permute-start.25 = (bf16[144,3072]{1,0:T(8,128)(2,1)}, bf16[144,3072]{1,0:T(8,128)(2,1)}, u32[]{:S(2)}, u32[]{:S(2)}) collective-permute-start(bf16[144,3072]{1,0:T(8,128)(2,1)} %broadcast_select_fusion), channel_id=1, source_target_pairs={{0,2},{1,3},{2,0},{3,1},{4,6},{5,7},{6,4},{7,5},{8,10},{9,11},{10,... | collective-permute-start | bytes 2654216 | tf_op jit(solution)/shard_map/ppermute | solution.py:425
  127.1 17.9 %collective-permute-start.23 = (bf16[384,576]{0,1:T(8,128)(2,1)}, bf16[384,576]{0,1:T(8,128)(2,1)}, u32[]{:S(2)}, u32[]{:S(2)}) collective-permute-start(bf16[384,576]{0,1:T(8,128)(2,1)} %collective-permute-done.22), channel_id=1, source_target_pairs={{0,1},{1,0},{2,3},{3,2},{4,5},{5,4},{6,7},{7,6},{8,9},{9,8},{10,11... | collective-permute-start | bytes 1327112 | tf_op jit(solution)/shard_map/ppermute | solution.py:425
  133.9 18.6 %collective-permute-start.20 = (bf16[512,384]{1,0:T(8,128)(2,1)}, bf16[512,384]{1,0:T(8,128)(2,1)}, u32[]{:S(2)}, u32[]{:S(2)}) collective-permute-start(bf16[512,384]{1,0:T(8,128)(2,1)} %pad_maximum_fusion.28), channel_id=1, source_target_pairs={{0,2},{1,3},{2,0},{3,1},{4,6},{5,7},{6,4},{7,5},{8,10},{9,11},{10,... | collective-permute-start | bytes 1179656 | tf_op jit(solution)/shard_map/ppermute | solution.py:425
  137.3 27.2 %collective-permute-start.27 = (bf16[144,3072]{1,0:T(8,128)(2,1)}, bf16[144,3072]{1,0:T(8,128)(2,1)}, u32[]{:S(2)}, u32[]{:S(2)}) collective-permute-start(bf16[144,3072]{1,0:T(8,128)(2,1)} %broadcast_select_fusion), channel_id=1, source_target_pairs={{0,1},{1,0},{2,3},{3,2},{4,5},{5,4},{6,7},{7,6},{8,9},{9,8},{10,11... | collective-permute-start | bytes 2654216 | tf_op jit(solution)/shard_map/ppermute | solution.py:425
  145.0 19.5 %collective-permute-start.26 = (bf16[144,3072]{1,0:T(8,128)(2,1)}, bf16[144,3072]{1,0:T(8,128)(2,1)}, u32[]{:S(2)}, u32[]{:S(2)}) collective-permute-start(bf16[144,3072]{1,0:T(8,128)(2,1)} %collective-permute-done.25), channel_id=1, source_target_pairs={{0,1},{1,0},{2,3},{3,2},{4,5},{5,4},{6,7},{7,6},{8,9},{9,8},{10,11... | collective-permute-start | bytes 2654216 | tf_op jit(solution)/shard_map/ppermute | solution.py:425
  199.6 37.3 %collective-permute-start.28 = (bf16[2,512,384]{2,1,0:T(8,128)(2,1)}, bf16[2,512,384]{2,1,0:T(8,128)(2,1)}, u32[]{:S(2)}, u32[]{:S(2)}) collective-permute-start(bf16[2,512,384]{2,1,0:T(8,128)(2,1)} %slice.193), channel_id=1, source_target_pairs={{0,1},{1,0},{2,3},{3,2},{4,5},{5,4},{6,7},{7,6},{8,9},{9,8},{10,11... | collective-permute-start | bytes 2359304 | tf_op jit(solution)/shard_map/ppermute | solution.py:425
  232.4 31.5 %collective-permute-start.32 = (bf16[2,384,576]{1,2,0:T(8,128)(2,1)S(1)}, bf16[2,384,576]{1,2,0:T(8,128)(2,1)S(1)}, u32[]{:S(2)}, u32[]{:S(2)}) collective-permute-start(bf16[2,384,576]{1,2,0:T(8,128)(2,1)S(1)} %bitcast.205), channel_id=1, source_target_pairs={{0,1},{1,0},{2,3},{3,2},{4,5},{5,4},{6,7},{7,6},{8,9},{9,8},{10,11... | collective-permute-start | bytes 2654216 | tf_op jit(solution)/shard_map/ppermute | solution.py:425
  235.4 56.2 %collective-permute-start.30 = (bf16[2,144,3072]{2,1,0:T(8,128)(2,1)}, bf16[2,144,3072]{2,1,0:T(8,128)(2,1)}, u32[]{:S(2)}, u32[]{:S(2)}) collective-permute-start(bf16[2,144,3072]{2,1,0:T(8,128)(2,1)} %dynamic-slice_bitcast_fusion.1), channel_id=1, source_target_pairs={{0,1},{1,0},{2,3},{3,2},{4,5},{5,4},{6,7},{7,6},{8,9},{9,8},{10,11... | collective-permute-start | bytes 5308424 | tf_op jit(solution)/shard_map/ppermute | solution.py:425
  238.1 35.8 %collective-permute-start.29 = (bf16[512,384]{1,0:T(8,128)(2,1)S(1)}, bf16[512,384]{1,0:T(8,128)(2,1)S(1)}, u32[]{:S(2)}, u32[]{:S(2)}) collective-permute-start(bf16[512,384]{1,0:T(8,128)(2,1)S(1)} %fusion.52), channel_id=1, source_target_pairs={{0,2},{1,3},{2,0},{3,1},{4,6},{5,7},{6,4},{7,5},{8,10},{9,11},{10,... | collective-permute-start | bytes 1179656 | tf_op jit(solution)/shard_map/ppermute | solution.py:425
  265.0 31.6 %collective-permute-start.33 = (bf16[384,576]{0,1:T(8,128)(2,1)}, bf16[384,576]{0,1:T(8,128)(2,1)}, u32[]{:S(2)}, u32[]{:S(2)}) collective-permute-start(bf16[384,576]{0,1:T(8,128)(2,1)} %dynamic-slice_bitcast_fusion.10), channel_id=1, source_target_pairs={{0,2},{1,3},{2,0},{3,1},{4,6},{5,7},{6,4},{7,5},{8,10},{9,11},{10,... | collective-permute-start | bytes 1327112 | tf_op jit(solution)/shard_map/ppermute | solution.py:425
  294.6 22.5 %collective-permute-start.31 = (bf16[144,3072]{1,0:T(8,128)(2,1)S(1)}, bf16[144,3072]{1,0:T(8,128)(2,1)S(1)}, u32[]{:S(2)}, u32[]{:S(2)}) collective-permute-start(bf16[144,3072]{1,0:T(8,128)(2,1)S(1)} %dynamic-slice_bitcast_fusion.5), channel_id=1, source_target_pairs={{0,2},{1,3},{2,0},{3,1},{4,6},{5,7},{6,4},{7,5},{8,10},{9,11},{10,... | collective-permute-start | bytes 2654216 | tf_op jit(solution)/shard_map/ppermute | solution.py:425
  300.1 71.5 %collective-permute-start.41 = (bf16[144,2048]{1,0:T(8,128)(2,1)}, bf16[144,2048]{1,0:T(8,128)(2,1)}, u32[]{:S(2)}, u32[]{:S(2)}) collective-permute-start(bf16[144,2048]{1,0:T(8,128)(2,1)} %dynamic-slice_bitcast_fusion.7), channel_id=1, source_target_pairs={{0,2},{1,3},{2,0},{3,1},{4,6},{5,7},{6,4},{7,5},{8,10},{9,11},{10,... | collective-permute-start | bytes 1769480 | tf_op jit(solution)/shard_map/ppermute | solution.py:425
  331.4 21.3 %collective-permute-start.37 = (bf16[96,576]{0,1:T(8,128)(2,1)}, bf16[96,576]{0,1:T(8,128)(2,1)S(1)}, u32[]{:S(2)}, u32[]{:S(2)}) collective-permute-start(bf16[96,576]{0,1:T(8,128)(2,1)} %get-tuple-element.212), channel_id=1, source_target_pairs={{0,4},{4,0},{8,12},{12,8},{1,5},{5,1},{9,13},{13,9},{2,6},{6,2},{1... | collective-permute-start | bytes 331784 | tf_op jit(solution)/shard_map/ppermute | solution.py:425
  333.0 23.3 %collective-permute-start.38 = (bf16[96,576]{0,1:T(8,128)(2,1)}, bf16[96,576]{0,1:T(8,128)(2,1)}, u32[]{:S(2)}, u32[]{:S(2)}) collective-permute-start(bf16[96,576]{0,1:T(8,128)(2,1)} %get-tuple-element.214), channel_id=1, source_target_pairs={{0,8},{4,12},{8,0},{12,4},{1,9},{5,13},{9,1},{13,5},{2,10},{6,14},... | collective-permute-start | bytes 331784 | tf_op jit(solution)/shard_map/ppermute | solution.py:425
  335.6 20.9 %collective-permute-start.39 = (bf16[96,576]{0,1:T(8,128)(2,1)}, bf16[96,576]{0,1:T(8,128)(2,1)}, u32[]{:S(2)}, u32[]{:S(2)}) collective-permute-start(bf16[96,576]{0,1:T(8,128)(2,1)} %get-tuple-element.213), channel_id=1, source_target_pairs={{0,12},{4,8},{8,4},{12,0},{1,13},{5,9},{9,5},{13,1},{2,14},{6,10},... | collective-permute-start | bytes 331784 | tf_op jit(solution)/shard_map/ppermute | solution.py:425
  336.6 21.6 %collective-permute-start.34 = (bf16[144,768]{1,0:T(8,128)(2,1)}, bf16[144,768]{1,0:T(8,128)(2,1)}, u32[]{:S(2)}, u32[]{:S(2)}) collective-permute-start(bf16[144,768]{1,0:T(8,128)(2,1)} %get-tuple-element.182), channel_id=1, source_target_pairs={{0,4},{4,0},{8,12},{12,8},{1,5},{5,1},{9,13},{13,9},{2,6},{6,2},{1... | collective-permute-start | bytes 663560 | tf_op jit(solution)/shard_map/ppermute | solution.py:425
  352.8 16.9 %collective-permute-start.35 = (bf16[144,768]{1,0:T(8,128)(2,1)S(1)}, bf16[144,768]{1,0:T(8,128)(2,1)S(1)}, u32[]{:S(2)}, u32[]{:S(2)}) collective-permute-start(bf16[144,768]{1,0:T(8,128)(2,1)S(1)} %copy-done.87), channel_id=1, source_target_pairs={{0,8},{4,12},{8,0},{12,4},{1,9},{5,13},{9,1},{13,5},{2,10},{6,14},... | collective-permute-start | bytes 663560 | tf_op jit(solution)/shard_map/ppermute | solution.py:425
  356.3 13.4 %collective-permute-start.36 = (bf16[144,768]{1,0:T(8,128)(2,1)S(1)}, bf16[144,768]{1,0:T(8,128)(2,1)S(1)}, u32[]{:S(2)}, u32[]{:S(2)}) collective-permute-start(bf16[144,768]{1,0:T(8,128)(2,1)S(1)} %copy-done.86), channel_id=1, source_target_pairs={{0,12},{4,8},{8,4},{12,0},{1,13},{5,9},{9,5},{13,1},{2,14},{6,10},... | collective-permute-start | bytes 663560 | tf_op jit(solution)/shard_map/ppermute | solution.py:425
  356.5 68.1 %collective-permute-start.44 = (bf16[2,384,576]{1,2,0:T(8,128)(2,1)}, bf16[2,384,576]{1,2,0:T(8,128)(2,1)}, u32[]{:S(2)}, u32[]{:S(2)}) collective-permute-start(bf16[2,384,576]{1,2,0:T(8,128)(2,1)} %bitcast.180), channel_id=1, source_target_pairs={{0,1},{1,0},{2,3},{3,2},{4,5},{5,4},{6,7},{7,6},{8,9},{9,8},{10,11... | collective-permute-start | bytes 2654216 | tf_op jit(solution)/shard_map/ppermute | solution.py:425
  358.3 48.3 %collective-permute-start.42 = (bf16[2,144,3072]{2,1,0:T(8,128)(2,1)}, bf16[2,144,3072]{2,1,0:T(8,128)(2,1)}, u32[]{:S(2)}, u32[]{:S(2)}) collective-permute-start(bf16[2,144,3072]{2,1,0:T(8,128)(2,1)} %dynamic-slice_bitcast_fusion), channel_id=1, source_target_pairs={{0,1},{1,0},{2,3},{3,2},{4,5},{5,4},{6,7},{7,6},{8,9},{9,8},{10,11... | collective-permute-start | bytes 5308424 | tf_op jit(solution)/shard_map/ppermute | solution.py:425
  373.7 26.5 %collective-permute-start.48 = (bf16[144,512]{1,0:T(8,128)(2,1)}, bf16[144,512]{1,0:T(8,128)(2,1)}, u32[]{:S(2)}, u32[]{:S(2)}) collective-permute-start(bf16[144,512]{1,0:T(8,128)(2,1)} %get-tuple-element.198), channel_id=1, source_target_pairs={{0,4},{4,0},{8,12},{12,8},{1,5},{5,1},{9,13},{13,9},{2,6},{6,2},{1... | collective-permute-start | bytes 442376 | tf_op jit(solution)/shard_map/ppermute | solution.py:425
  378.5 23.0 %collective-permute-start.49 = (bf16[144,512]{1,0:T(8,128)(2,1)}, bf16[144,512]{1,0:T(8,128)(2,1)}, u32[]{:S(2)}, u32[]{:S(2)}) collective-permute-start(bf16[144,512]{1,0:T(8,128)(2,1)} %get-tuple-element.200), channel_id=1, source_target_pairs={{0,8},{4,12},{8,0},{12,4},{1,9},{5,13},{9,1},{13,5},{2,10},{6,14},... | collective-permute-start | bytes 442376 | tf_op jit(solution)/shard_map/ppermute | solution.py:425
  379.4 17.7 %collective-permute-start.47 = (bf16[96,576]{0,1:T(8,128)(2,1)}, bf16[96,576]{0,1:T(8,128)(2,1)}, u32[]{:S(2)}, u32[]{:S(2)}) collective-permute-start(bf16[96,576]{0,1:T(8,128)(2,1)} %add_convert_fusion.19), channel_id=1, source_target_pairs={{0,16},{1,17},{2,18},{3,19},{4,20},{5,21},{6,22},{7,23},{8,24},{9,... | collective-permute-start | bytes 331784 | tf_op jit(solution)/shard_map/ppermute | solution.py:490
  400.2 27.2 %collective-permute-start.46 = (bf16[144,768]{1,0:T(8,128)(2,1)S(1)}, bf16[144,768]{1,0:T(8,128)(2,1)S(1)}, u32[]{:S(2)}, u32[]{:S(2)}) collective-permute-start(bf16[144,768]{1,0:T(8,128)(2,1)S(1)} %copy-done.69), channel_id=1, source_target_pairs={{0,16},{1,17},{2,18},{3,19},{4,20},{5,21},{6,22},{7,23},{8,24},{9,... | collective-permute-start | bytes 663560 | tf_op jit(solution)/shard_map/ppermute | solution.py:490
  405.2 22.9 %collective-permute-start.51 = (bf16[144,512]{1,0:T(8,128)(2,1)S(1)}, bf16[144,512]{1,0:T(8,128)(2,1)S(1)}, u32[]{:S(2)}, u32[]{:S(2)}) collective-permute-start(bf16[144,512]{1,0:T(8,128)(2,1)S(1)} %add_convert_fusion.17), channel_id=1, source_target_pairs={{0,16},{1,17},{2,18},{3,19},{4,20},{5,21},{6,22},{7,23},{8,24},{9,... | collective-permute-start | bytes 442376 | tf_op jit(solution)/shard_map/ppermute | solution.py:490
  408.8 43.1 %collective-permute-start.43 = (bf16[144,3072]{1,0:T(8,128)(2,1)S(1)}, bf16[144,3072]{1,0:T(8,128)(2,1)S(1)}, u32[]{:S(2)}, u32[]{:S(2)}) collective-permute-start(bf16[144,3072]{1,0:T(8,128)(2,1)S(1)} %dynamic-slice_bitcast_fusion.4), channel_id=1, source_target_pairs={{0,2},{1,3},{2,0},{3,1},{4,6},{5,7},{6,4},{7,5},{8,10},{9,11},{10,... | collective-permute-start | bytes 2654216 | tf_op jit(solution)/shard_map/ppermute | solution.py:425
  426.0 25.0 %collective-permute-start.45 = (bf16[384,576]{0,1:T(8,128)(2,1)S(1)}, bf16[384,576]{0,1:T(8,128)(2,1)S(1)}, u32[]{:S(2)}, u32[]{:S(2)}) collective-permute-start(bf16[384,576]{0,1:T(8,128)(2,1)S(1)} %dynamic-slice_bitcast_fusion.9), channel_id=1, source_target_pairs={{0,2},{1,3},{2,0},{3,1},{4,6},{5,7},{6,4},{7,5},{8,10},{9,11},{10,... | collective-permute-start | bytes 1327112 | tf_op jit(solution)/shard_map/ppermute | solution.py:425
  454.1 13.7 %collective-permute-start.52 = (bf16[2,512,384]{2,1,0:T(8,128)(2,1)}, bf16[2,512,384]{2,1,0:T(8,128)(2,1)}, u32[]{:S(2)}, u32[]{:S(2)}) collective-permute-start(bf16[2,512,384]{2,1,0:T(8,128)(2,1)} %slice.204), channel_id=1, source_target_pairs={{0,1},{1,0},{2,3},{3,2},{4,5},{5,4},{6,7},{7,6},{8,9},{9,8},{10,11... | collective-permute-start | bytes 2359304 | tf_op jit(solution)/shard_map/ppermute | solution.py:425
  459.8 93.2 %collective-permute-start.54 = (bf16[512,576]{0,1:T(8,128)(2,1)}, bf16[512,576]{0,1:T(8,128)(2,1)}, u32[]{:S(2)}, u32[]{:S(2)}) collective-permute-start(bf16[512,576]{0,1:T(8,128)(2,1)} %get-tuple-element.223), channel_id=1, source_target_pairs={{0,16},{1,17},{2,18},{3,19},{4,20},{5,21},{6,22},{7,23},{8,24},{9,... | collective-permute-start | bytes 1769480 | tf_op jit(solution)/shard_map/ppermute | solution.py:819
  468.8 20.4 %collective-permute-start.53 = (bf16[512,384]{1,0:T(8,128)(2,1)S(1)}, bf16[512,384]{1,0:T(8,128)(2,1)S(1)}, u32[]{:S(2)}, u32[]{:S(2)}) collective-permute-start(bf16[512,384]{1,0:T(8,128)(2,1)S(1)} %fusion.54), channel_id=1, source_target_pairs={{0,2},{1,3},{2,0},{3,1},{4,6},{5,7},{6,4},{7,5},{8,10},{9,11},{10,... | collective-permute-start | bytes 1179656 | tf_op jit(solution)/shard_map/ppermute | solution.py:425
  472.9 13.6 %collective-permute-start.73 = (bf16[96,576]{0,1:T(8,128)(2,1)S(1)}, bf16[96,576]{0,1:T(8,128)(2,1)S(1)}, u32[]{:S(2)}, u32[]{:S(2)}) collective-permute-start(bf16[96,576]{0,1:T(8,128)(2,1)S(1)} %get-tuple-element.211), channel_id=1, source_target_pairs={{0,8},{4,12},{8,0},{12,4},{1,9},{5,13},{9,1},{13,5},{2,10},{6,14},... | collective-permute-start | bytes 331784 | tf_op jit(solution)/shard_map/ppermute | solution.py:425
  473.2 13.3 %collective-permute-start.74 = (bf16[96,576]{0,1:T(8,128)(2,1)S(1)}, bf16[96,576]{0,1:T(8,128)(2,1)S(1)}, u32[]{:S(2)}, u32[]{:S(2)}) collective-permute-start(bf16[96,576]{0,1:T(8,128)(2,1)S(1)} %get-tuple-element.210), channel_id=1, source_target_pairs={{0,12},{4,8},{8,4},{12,0},{1,13},{5,9},{9,5},{13,1},{2,14},{6,10},... | collective-permute-start | bytes 331784 | tf_op jit(solution)/shard_map/ppermute | solution.py:425
  478.2 26.2 %collective-permute-start.65 = (bf16[144,768]{1,0:T(8,128)(2,1)}, bf16[144,768]{1,0:T(8,128)(2,1)}, u32[]{:S(2)}, u32[]{:S(2)}) collective-permute-start(bf16[144,768]{1,0:T(8,128)(2,1)} %get-tuple-element.179), channel_id=1, source_target_pairs={{0,4},{4,0},{8,12},{12,8},{1,5},{5,1},{9,13},{13,9},{2,6},{6,2},{1... | collective-permute-start | bytes 663560 | tf_op jit(solution)/shard_map/ppermute | solution.py:425
  486.5 18.0 %collective-permute-start.66 = (bf16[144,768]{1,0:T(8,128)(2,1)}, bf16[144,768]{1,0:T(8,128)(2,1)}, u32[]{:S(2)}, u32[]{:S(2)}) collective-permute-start(bf16[144,768]{1,0:T(8,128)(2,1)} %get-tuple-element.181), channel_id=1, source_target_pairs={{0,8},{4,12},{8,0},{12,4},{1,9},{5,13},{9,1},{13,5},{2,10},{6,14},... | collective-permute-start | bytes 663560 | tf_op jit(solution)/shard_map/ppermute | solution.py:425
  486.5 18.0 %collective-permute-start.67 = (bf16[144,768]{1,0:T(8,128)(2,1)}, bf16[144,768]{1,0:T(8,128)(2,1)}, u32[]{:S(2)}, u32[]{:S(2)}) collective-permute-start(bf16[144,768]{1,0:T(8,128)(2,1)} %get-tuple-element.180), channel_id=1, source_target_pairs={{0,12},{4,8},{8,4},{12,0},{1,13},{5,9},{9,5},{13,1},{2,14},{6,10},... | collective-permute-start | bytes 663560 | tf_op jit(solution)/shard_map/ppermute | solution.py:425
  489.2 18.1 %collective-permute-start.75 = (bf16[96,576]{0,1:T(8,128)(2,1)}, bf16[96,576]{0,1:T(8,128)(2,1)}, u32[]{:S(2)}, u32[]{:S(2)}) collective-permute-start(bf16[96,576]{0,1:T(8,128)(2,1)} %add_convert_fusion.13), channel_id=1, source_target_pairs={{16,0},{17,1},{18,2},{19,3},{20,4},{21,5},{22,6},{23,7},{24,8},{25... | collective-permute-start | bytes 331784 | tf_op jit(solution)/shard_map/ppermute | solution.py:490
  504.5 47.8 %collective-permute-start.56 = (bf16[2,144,2048]{2,1,0:T(8,128)(2,1)S(1)}, bf16[2,144,2048]{2,1,0:T(8,128)(2,1)S(1)}, u32[]{:S(2)}, u32[]{:S(2)}) collective-permute-start(bf16[2,144,2048]{2,1,0:T(8,128)(2,1)S(1)} %dynamic-slice_bitcast_fusion.2), channel_id=1, source_target_pairs={{0,1},{1,0},{2,3},{3,2},{4,5},{5,4},{6,7},{7,6},{8,9},{9,8},{10,11... | collective-permute-start | bytes 3538952 | tf_op jit(solution)/shard_map/ppermute | solution.py:425
  505.9 16.2 %collective-permute-start.68 = (bf16[144,768]{1,0:T(8,128)(2,1)S(1)}, bf16[144,768]{1,0:T(8,128)(2,1)S(1)}, u32[]{:S(2)}, u32[]{:S(2)}) collective-permute-start(bf16[144,768]{1,0:T(8,128)(2,1)S(1)} %add_convert_fusion.9), channel_id=1, source_target_pairs={{16,0},{17,1},{18,2},{19,3},{20,4},{21,5},{22,6},{23,7},{24,8},{25... | collective-permute-start | bytes 663560 | tf_op jit(solution)/shard_map/ppermute | solution.py:490
  508.3 20.7 %collective-permute-start.76 = (bf16[96,576]{0,1:T(8,128)(2,1)S(1)}, bf16[96,576]{0,1:T(8,128)(2,1)S(1)}, u32[]{:S(2)}, u32[]{:S(2)}) collective-permute-start(bf16[96,576]{0,1:T(8,128)(2,1)S(1)} %fusion.66), channel_id=1, source_target_pairs={{0,12},{4,8},{8,4},{12,0},{1,13},{5,9},{9,5},{13,1},{2,14},{6,10},... | collective-permute-start | bytes 331784 | tf_op jit(solution)/shard_map/ppermute | solution.py:425
  510.3 22.8 %collective-permute-start.77 = (bf16[96,576]{0,1:T(8,128)(2,1)S(1)}, bf16[96,576]{0,1:T(8,128)(2,1)S(1)}, u32[]{:S(2)}, u32[]{:S(2)}) collective-permute-start(bf16[96,576]{0,1:T(8,128)(2,1)S(1)} %fusion.66), channel_id=1, source_target_pairs={{0,8},{4,12},{8,0},{12,4},{1,9},{5,13},{9,1},{13,5},{2,10},{6,14},... | collective-permute-start | bytes 331784 | tf_op jit(solution)/shard_map/ppermute | solution.py:425
  522.1 18.3 %collective-permute-start.78 = (bf16[96,576]{0,1:T(8,128)(2,1)S(1)}, bf16[96,576]{0,1:T(8,128)(2,1)S(1)}, u32[]{:S(2)}, u32[]{:S(2)}) collective-permute-start(bf16[96,576]{0,1:T(8,128)(2,1)S(1)} %fusion.66), channel_id=1, source_target_pairs={{0,4},{4,0},{8,12},{12,8},{1,5},{5,1},{9,13},{13,9},{2,6},{6,2},{1... | collective-permute-start | bytes 331784 | tf_op jit(solution)/shard_map/ppermute | solution.py:425
  529.0 12.7 %collective-permute-start.69 = (bf16[144,768]{1,0:T(8,128)(2,1)S(1)}, bf16[144,768]{1,0:T(8,128)(2,1)S(1)}, u32[]{:S(2)}, u32[]{:S(2)}) collective-permute-start(bf16[144,768]{1,0:T(8,128)(2,1)S(1)} %fusion.60), channel_id=1, source_target_pairs={{0,12},{4,8},{8,4},{12,0},{1,13},{5,9},{9,5},{13,1},{2,14},{6,10},... | collective-permute-start | bytes 663560 | tf_op jit(solution)/shard_map/ppermute | solution.py:425
  533.1 18.6 %collective-permute-start.70 = (bf16[144,768]{1,0:T(8,128)(2,1)S(1)}, bf16[144,768]{1,0:T(8,128)(2,1)S(1)}, u32[]{:S(2)}, u32[]{:S(2)}) collective-permute-start(bf16[144,768]{1,0:T(8,128)(2,1)S(1)} %fusion.60), channel_id=1, source_target_pairs={{0,8},{4,12},{8,0},{12,4},{1,9},{5,13},{9,1},{13,5},{2,10},{6,14},... | collective-permute-start | bytes 663560 | tf_op jit(solution)/shard_map/ppermute | solution.py:425
  540.4 11.7 %collective-permute-start.71 = (bf16[144,768]{1,0:T(8,128)(2,1)S(1)}, bf16[144,768]{1,0:T(8,128)(2,1)S(1)}, u32[]{:S(2)}, u32[]{:S(2)}) collective-permute-start(bf16[144,768]{1,0:T(8,128)(2,1)S(1)} %fusion.60), channel_id=1, source_target_pairs={{0,4},{4,0},{8,12},{12,8},{1,5},{5,1},{9,13},{13,9},{2,6},{6,2},{1... | collective-permute-start | bytes 663560 | tf_op jit(solution)/shard_map/ppermute | solution.py:425
  552.8 14.2 %collective-permute-start.57 = (bf16[144,2048]{1,0:T(8,128)(2,1)S(1)}, bf16[144,2048]{1,0:T(8,128)(2,1)S(1)}, u32[]{:S(2)}, u32[]{:S(2)}) collective-permute-start(bf16[144,2048]{1,0:T(8,128)(2,1)S(1)} %dynamic-slice_bitcast_fusion.6), channel_id=1, source_target_pairs={{0,2},{1,3},{2,0},{3,1},{4,6},{5,7},{6,4},{7,5},{8,10},{9,11},{10,... | collective-permute-start | bytes 1769480 | tf_op jit(solution)/shard_map/ppermute | solution.py:425
  555.7 25.6 %collective-permute-start.55 = (bf16[512,576]{0,1:T(8,128)(2,1)S(1)}, bf16[512,576]{0,1:T(8,128)(2,1)S(1)}, u32[]{:S(2)}, u32[]{:S(2)}) collective-permute-start(bf16[512,576]{0,1:T(8,128)(2,1)S(1)} %get-tuple-element.144), channel_id=1, source_target_pairs={{16,0},{17,1},{18,2},{19,3},{20,4},{21,5},{22,6},{23,7},{24,8},{25... | collective-permute-start | bytes 1769480 | tf_op jit(solution)/shard_map/ppermute | solution.py:858
  567.3 12.6 %collective-permute-start.59 = (bf16[144,512]{1,0:T(8,128)(2,1)S(1)}, bf16[144,512]{1,0:T(8,128)(2,1)S(1)}, u32[]{:S(2)}, u32[]{:S(2)}) collective-permute-start(bf16[144,512]{1,0:T(8,128)(2,1)S(1)} %get-tuple-element.197), channel_id=1, source_target_pairs={{0,8},{4,12},{8,0},{12,4},{1,9},{5,13},{9,1},{13,5},{2,10},{6,14},... | collective-permute-start | bytes 442376 | tf_op jit(solution)/shard_map/ppermute | solution.py:425
  590.9 10.6 %collective-permute-start.63 = (bf16[144,512]{1,0:T(8,128)(2,1)S(1)}, bf16[144,512]{1,0:T(8,128)(2,1)S(1)}, u32[]{:S(2)}, u32[]{:S(2)}) collective-permute-start(bf16[144,512]{1,0:T(8,128)(2,1)S(1)} %fusion.65), channel_id=1, source_target_pairs={{0,8},{4,12},{8,0},{12,4},{1,9},{5,13},{9,1},{13,5},{2,10},{6,14},... | collective-permute-start | bytes 442376 | tf_op jit(solution)/shard_map/ppermute | solution.py:425
  (110 other events, 907.8 us)

commit v3 on v2

--- a/solution.py
+++ b/solution.py
@@ -459,14 +459,58 @@
 
 def reduce_to_owner(partial, index):
     rows = partial.shape[0] // 4
-    blocks = partial.reshape(2, 2, rows, partial.shape[1])
     core, chip = index & 1, index >> 1
-    kept = lax.dynamic_index_in_dim(blocks, core, 1, keepdims=False)
-    sent = lax.dynamic_index_in_dim(blocks, core ^ 1, 1, keepdims=False)
-    halves = add_low(kept, xor_send(sent, "shard", 1))
-    kept = lax.dynamic_index_in_dim(halves, chip, 0, keepdims=False)
-    sent = lax.dynamic_index_in_dim(halves, chip ^ 1, 0, keepdims=False)
-    return add_low(kept, xor_send(sent, "shard", 2))
+
+    def block(number):
+        return lax.dynamic_slice_in_dim(partial, number * rows, rows, 0)
+
+    far, near = [
+        add_low(block(2 * owner + core), xor_send(block(2 * owner + (core ^ 1)), "shard", 1))
+        for owner in (chip ^ 1, chip)
+    ]
+    return add_low(near, xor_send(far, "shard", 2))
+
+
+FOLD = ((0, 2, 3, 1), (1, 3, 2, 0))
+
+
+def section_pairs(half, moves, back):
+    pairs = []
+    for start, end in moves:
+        for held, folded in enumerate(FOLD[half]):
+            ends = (start * 4 + held, end * 4 + folded)
+            if back:
+                ends = (start * 4 + folded, end * 4 + held)
+            pairs.append(ends)
+    return pairs
+
+
+def fold_rows(rows, index, moves):
+    size = rows.shape[0] // 2
+    first, second = [
+        lax.ppermute(
+            rows[half * size : (half + 1) * size],
+            ("section", "shard"),
+            section_pairs(half, moves, False),
+        )
+        for half in (0, 1)
+    ]
+    odd = (index & 1) == 1
+    return jnp.concatenate([jnp.where(odd, second, first), jnp.where(odd, first, second)], axis=0)
+
+
+def unfold_rows(rows, index, moves):
+    size = rows.shape[0] // 2
+    low, high = rows[:size], rows[size:]
+    odd = (index & 1) == 1
+    parts = (jnp.where(odd, high, low), jnp.where(odd, low, high))
+    return jnp.concatenate(
+        [
+            lax.ppermute(parts[half], ("section", "shard"), section_pairs(half, moves, True))
+            for half in (0, 1)
+        ],
+        axis=0,
+    )
 
 
 def reduce_replicas(value, replica, axis):
@@ -509,13 +553,20 @@
     return slice(start + head * HEAD, start + (head + 1) * HEAD)
 
 
-def over_blocks(index, update):
-    update(0, True)
+def over_blocks(index, rows, update):
+    every, early, late = slice(0, rows), slice(0, rows // 2), slice(rows // 2, rows)
+    update(0, True, every, every)
 
     def other(j, carry):
-        @pl.when((index ^ j) < index)
+        before = (index ^ j) < index
+
+        @pl.when(before)
         def _():
-            update(j, False)
+            update(j, False, early, every)
+
+        @pl.when(jnp.logical_not(before))
+        def _():
+            update(j, False, every, late)
 
         return carry
 
@@ -532,30 +583,30 @@
     rows = q_ref.shape[0]
     group = HEADS // KV_HEADS
 
-    def update(j, own):
+    def update(j, own, met, asked):
         for kv in range(KV_HEADS):
-            keys = blocks_ref[j, :, head_columns(kv)]
-            values = blocks_ref[j, :, head_columns(kv, KV_HEADS * HEAD)]
+            keys = blocks_ref[j, met, head_columns(kv)]
+            values = blocks_ref[j, met, head_columns(kv, KV_HEADS * HEAD)]
             for head in range(kv * group, (kv + 1) * group):
                 line = slice(head, head + 1)
-                scores = nt_dot(keys, q_ref[:, head_columns(head)] * HEAD ** (-0.5))
+                scores = nt_dot(keys, q_ref[asked, head_columns(head)] * HEAD ** (-0.5))
                 if own:
                     scores = jnp.where(causal(rows), scores, neg_large)
                     new_top = jnp.max(scores, axis=0, keepdims=True)
                 else:
-                    new_top = jnp.maximum(top[line, :], jnp.max(scores, axis=0, keepdims=True))
+                    new_top = jnp.maximum(top[line, asked], jnp.max(scores, axis=0, keepdims=True))
                 weights_now = jnp.exp(scores - new_top)
                 sums = jnp.sum(weights_now, axis=0, keepdims=True)
                 mixed = tn_dot(values, weights_now.astype(jnp.bfloat16))
                 if not own:
-                    factor = jnp.exp(top[line, :] - new_top)
-                    sums = sums + total[line, :] * factor
-                    mixed = mixed + acc[head_columns(head), :] * factor
-                top[line, :] = new_top
-                total[line, :] = sums
-                acc[head_columns(head), :] = mixed
-
-    over_blocks(index_ref[0], update)
+                    factor = jnp.exp(top[line, asked] - new_top)
+                    sums = sums + total[line, asked] * factor
+                    mixed = mixed + acc[head_columns(head), asked] * factor
+                top[line, asked] = new_top
+                total[line, asked] = sums
+                acc[head_columns(head), asked] = mixed
+
+    over_blocks(index_ref[0], rows, update)
     log_ref[...] = jnp.zeros_like(log_ref)
     for head in range(HEADS):
         line = slice(head, head + 1)
@@ -578,33 +629,33 @@
         delta[head : head + 1, :] = jnp.sum(acc[head_columns(head), :], axis=0, keepdims=True)
     acc[...] = jnp.zeros_like(acc)
 
-    def update(j, own):
+    def update(j, own, met, asked):
         for kv in range(KV_HEADS):
-            keys = blocks_ref[j, :, head_columns(kv)]
-            values = blocks_ref[j, :, head_columns(kv, width)]
-            key_sum = jnp.zeros((rows, HEAD), jnp.float32)
-            value_sum = jnp.zeros((rows, HEAD), jnp.float32)
+            keys = blocks_ref[j, met, head_columns(kv)]
+            values = blocks_ref[j, met, head_columns(kv, width)]
+            key_sum = jnp.zeros((met.stop - met.start, HEAD), jnp.float32)
+            value_sum = jnp.zeros((met.stop - met.start, HEAD), jnp.float32)
             for head in range(kv * group, (kv + 1) * group):
                 line = slice(head, head + 1)
-                query = q_ref[:, head_columns(head)]
-                grads = grads_ref[:, head_columns(head)]
+                query = q_ref[asked, head_columns(head)]
+                grads = grads_ref[asked, head_columns(head)]
                 scores = nt_dot(keys, query * HEAD ** (-0.5))
                 if own:
                     scores = jnp.where(causal(rows), scores, neg_large)
-                probabilities = jnp.exp(scores - log_ref[line, :])
+                probabilities = jnp.exp(scores - log_ref[line, asked])
                 grad_probs = nt_dot(values, grads)
                 grad_scores = (
-                    probabilities * (grad_probs - delta[line, :]) * HEAD ** (-0.5)
+                    probabilities * (grad_probs - delta[line, asked]) * HEAD ** (-0.5)
                 ).astype(jnp.bfloat16)
-                acc[head_columns(head), :] += tn_dot(keys, grad_scores)
+                acc[head_columns(head), asked] += tn_dot(keys, grad_scores)
                 key_sum += jnp.dot(grad_scores, query, preferred_element_type=jnp.float32)
                 value_sum += jnp.dot(
                     probabilities.astype(jnp.bfloat16), grads, preferred_element_type=jnp.float32
                 )
-            parts_ref[j, :, head_columns(kv)] = key_sum.astype(jnp.bfloat16)
-            parts_ref[j, :, head_columns(kv, width)] = value_sum.astype(jnp.bfloat16)
-
-    over_blocks(index_ref[0], update)
+            parts_ref[j, met, head_columns(kv)] = key_sum.astype(jnp.bfloat16)
+            parts_ref[j, met, head_columns(kv, width)] = value_sum.astype(jnp.bfloat16)
+
+    over_blocks(index_ref[0], rows, update)
     query_ref[...] = acc[...].T
 
 
@@ -765,10 +816,14 @@
     local = ends[0]
     tok_count, model_width = local.shape[-2:]
     own_pair = local.reshape(2, tok_count, model_width)
-    moved = xor_send(
-        lax.dynamic_index_in_dim(own_pair, 1 - section, 0, keepdims=False), "section", 1
-    )
-    stayed = lax.dynamic_index_in_dim(own_pair, section, 0, keepdims=False)
+    moved = fold_rows(
+        lax.dynamic_index_in_dim(own_pair, 1 - section, 0, keepdims=False),
+        index,
+        ((0, 1), (1, 0)),
+    )
+    stayed = fold_rows(
+        lax.dynamic_index_in_dim(own_pair, section, 0, keepdims=False), index, ((0, 0), (1, 1))
+    )
     tokens = jnp.where(leading, stayed, moved)
     cotangent = jnp.where(leading, moved, stayed)
 
@@ -780,7 +835,10 @@
         jnp.concatenate([w_gate[0], w_up[0]], axis=1),
         w_down[0],
     )
-    positions = index * tok_count + jnp.arange(tok_count, dtype=jnp.int32)
+    chunk = jnp.arange(tok_count // 2, dtype=jnp.int32)
+    positions = jnp.concatenate(
+        [index * chunk.shape[0] + chunk, (7 - index) * chunk.shape[0] + chunk]
+    )
     tables = rotation_tables(positions)
     other_attn = xor_send(groups[0], "section", 1)
     own_rest, other_attn = tied(groups[1:], other_attn)
@@ -816,13 +874,14 @@
     )
     weights_second = attn_second + second_rest
     final, kept_second = forward_rest(*second_state, weights_second, index)
-    final_arrived = lax.ppermute(final.astype(jnp.bfloat16), "section", [(0, 1)])
+    final_low = final.astype(jnp.bfloat16)
+    final_arrived = unfold_rows(final_low, index, ((0, 1),))
+    final_stayed = unfold_rows(final_low, index, ((1, 1),))
 
     def pack(g_in, g_out, g_gain_attn, g_gain_ffn):
         pad = jnp.zeros((model_width, 2048 - attn_width - 2), jnp.float32)
-        return jnp.concatenate(
-            [g_in, g_out, g_gain_attn[:, None], g_gain_ffn[:, None], pad], axis=1
-        ).astype(jnp.bfloat16)
+        parts = [g_in, g_out, g_gain_attn[:, None], g_gain_ffn[:, None], pad]
+        return jnp.concatenate([part.astype(jnp.bfloat16) for part in parts], axis=1)
 
     def over_shards(*partials):
         return tuple(reduce_to_owner(partial, index) for partial in partials)
@@ -855,15 +914,17 @@
     (attn_first_sum,) = over_shards(pack(g_in, g_out, g_gain_attn, g_gain_ffn))
     attn_first_sum = reduce_sections(reduce_replicas(attn_first_sum, replica, 1), 0)
     quarters = ((attn_second_sum,) + ffn_second, (attn_first_sum,) + ffn_first)
-    grad_arrived = lax.ppermute(grad.astype(jnp.bfloat16), "section", [(1, 0)])
+    grad_low = grad.astype(jnp.bfloat16)
+    grad_stayed = unfold_rows(grad_low, index, ((0, 0),))
+    grad_arrived = unfold_rows(grad_low, index, ((1, 0),))
     attn_sum, gate_up_sum, down_sum = [
         gather_replicas(jnp.where(leading, first, second), replica, axis).astype(jnp.float32)
         for first, second, axis in zip(quarters[1], quarters[0], (1, 1, 0))
     ]
     ends_out = jnp.stack(
         [
-            jnp.where(leading, grad, final_arrived.astype(jnp.float32)),
-            jnp.where(leading, grad_arrived.astype(jnp.float32), final),
+            jnp.where(leading, grad_stayed, final_arrived).astype(jnp.float32),
+            jnp.where(leading, grad_arrived, final_stayed).astype(jnp.float32),
         ]
     ).reshape(1, 2, 1, tok_count, model_width)
     cuts = [w_query.shape[2], w_query.shape[2] + w_key.shape[2], in_width, attn_width]

time: 614 us -> 574 us (0.935)
  Pallas kernels: 33 us -> 80.1 us
  local copies, waits for them, and re-layouts: 93.2 us -> 52 us
  starting transfers between devices: 153 us -> 122 us
  waiting for transfers between devices: 201 us -> 192 us
  other arithmetic: 70.8 us -> 63.9 us
    ppermute x71 -> x76, starting transfers between devices: 139 us -> 86 us  [xor_send(): return lax.ppermute(value, axis, [(i, i ^ bits) for i in range(peers)])]
    ppermute x71 -> x76, waiting for transfers between devices: 193 us -> 164 us  [xor_send(): return lax.ppermute(value, axis, [(i, i ^ bits) for i in range(peers)])]
    pallas_call x2, Pallas kernels: 20.7 us -> 44.9 us  [attend_backward(): pl.pallas_call(attend_backward_kernel, out_shape=(jax.ShapeDtypeStruct((r...]
    pallas_call x2, Pallas kernels: 12.3 us -> 35.3 us  [attend_forward(): pl.pallas_call(attend_forward_kernel, out_shape=(jax.ShapeDtypeStruct((ro...]
    ppermute x2 -> x12, starting transfers between devices: 3.42 us -> 22.9 us  [the longest x8 16.3 us: unfold_rows(): lax.ppermute(parts[half], ('section', 'shard'), section_pairs(half, moves...]
    ppermute x2 -> x12, waiting for transfers between devices: 0.01 us -> 15.8 us  [the longest x4 8.6 us: fold_rows(): lax.ppermute(rows[half * size:(half + 1) * size], ('section', 'shard'), s...]
    squeeze x11 -> x0, local copies, waits for them, and re-layouts: 11.1 us -> none  [the longest x4 7.22 us: reduce_to_owner(): sent = lax.dynamic_index_in_dim(blocks, core ^ 1, 1, keepdims=False)]
    dynamic_slice x4 -> x6, local copies, waits for them, and re-layouts: 17.3 us -> 6.25 us  [block(): return lax.dynamic_slice_in_dim(partial, number * rows, rows, 0)]
  transfers between devices with their start and end apart: 79 -> 94, of which waited for: 29 -> 39; matrix products, arithmetic and copies ran while one was open for 27% -> 21% of each run, Pallas kernels for 4% -> 10%
where the time goes in v3:
time: 574 us; the launch traced here: 566 us
  waiting for transfers between devices  192 us (33%)
  starting transfers between devices  122 us (21%)
  Pallas kernels  80.1 us (14%)
  other arithmetic  63.9 us (11%)
  matrix products  52.9 us (9%)
  local copies, waits for them, and re-layouts  52 us (9%)
    ppermute x76, waiting for transfers between devices, xor_send(): return lax.ppermute(value, axis, [(i, i ^ bits) for i in range(peers)])  164 us
    ppermute x76, starting transfers between devices, xor_send(): return lax.ppermute(value, axis, [(i, i ^ bits) for i in range(peers)])  86 us
    pallas_call x2, Pallas kernels, attend_backward(): pl.pallas_call(attend_backward_kernel, out_shape=(jax.ShapeDtypeStruct((r...  44.9 us
    pallas_call x2, Pallas kernels, attend_forward(): pl.pallas_call(attend_forward_kernel, out_shape=(jax.ShapeDtypeStruct((ro...  35.3 us
    dot_general x8, matrix products, input_grad(): jnp.einsum('rf,df->rd', gradient, weight, preferred_element_type=jnp.floa...  21.2 us
    dot_general x8, matrix products, weight_grad(): jnp.einsum('rd,rf->df', left_side, right_side, preferred_element_type=jnp...  17.6 us
    ppermute x8, starting transfers between devices, unfold_rows(): lax.ppermute(parts[half], ('section', 'shard'), section_pairs(half, moves...  16.3 us
    unnamed x184, local copies, waits for them, and re-layouts  15.4 us
  transfers between devices with their start and end apart: 94, of which 39 were waited for; matrix products, arithmetic and copies ran while one was open for 21% of the time, Pallas kernels for 10%

profile of v3, /device:TPU:0, one launch (start us, length us, event | category | flops | bytes accessed | tf_op | source)
XLA Modules:
  0.0 565.9 jit_solution(6281521287428056465)
XLA Ops:
  3.8 3.0 collective-permute-start.4
  9.0 3.8 collective-permute-start.2
  15.6 3.0 collective-permute-done.4
  21.9 2.7 collective-permute-done
  24.6 5.9 %collective-permute-done.1 = bf16[256,576]{0,1:T(8,128)(2,1)} collective-permute-done((bf16[256,576]{0,1:T(8,128)(2,1)}, bf16[256,576]{0,1:T(8,128)(2,1)}, u32[]{:S(2)}, u32[]{:S(2)}) %collective-permute-start.1) | collective-permute-done | bytes 294944 | tf_op jit(solution)/shard_map/ppermute | solution.py:491
  31.6 5.7 collective-permute-done.5
  49.6 19.8 %collective-permute-done.9 = bf16[384,576]{0,1:T(8,128)(2,1)} collective-permute-done((bf16[384,576]{0,1:T(8,128)(2,1)}, bf16[384,576]{0,1:T(8,128)(2,1)}, u32[]{:S(2)}, u32[]{:S(2)}) %collective-permute-start.9) | collective-permute-done | bytes 442400 | tf_op jit(solution)/shard_map/ppermute | solution.py:425
  78.1 17.8 %shard_map.177 = (bf16[512,576]{1,0:T(8,128)(2,1)S(1)}, f32[512,576]{1,0:T(8,128)S(1)}, f32[16,512]{1,0:T(8,128)S(1)}) custom-call(s32[1]{0:T(128)} %bitcast.4.index_ref, bf16[512,576]{1,0:T(8,128)(2,1)S(1)} %copy.60.q_ref, bf16[4,512,384]{2,1,0:T(8,128)(2,1)} %pad_maximum_fusion.12.blocks_ref), custom_call_target="tpu_custom_call" | custom-call | flops 2415919104 | bytes 4194304 | tf_op jit(solution)/shard_map/pallas_call | solution.py:668
  95.9 10.6 %collective-permute-done.16 = bf16[384,576]{0,1:T(8,128)(2,1)} collective-permute-done((bf16[384,576]{0,1:T(8,128)(2,1)}, bf16[384,576]{0,1:T(8,128)(2,1)}, u32[]{:S(2)}, u32[]{:S(2)}) %collective-permute-start.16) | collective-permute-done | bytes 442400 | tf_op jit(solution)/shard_map/ppermute | solution.py:425
  107.0 2.3 multiply_reduce_fusion.5
  111.3 2.4 broadcast_select_fusion.16
  114.2 2.3 broadcast_select_fusion.38
  121.2 2.7 fusion.69
  126.6 13.4 %collective-permute-done.19 = bf16[144,1538]{1,0:T(8,128)(2,1)S(1)} collective-permute-done((bf16[144,1538]{1,0:T(8,128)(2,1)S(1)}, bf16[144,1538]{1,0:T(8,128)(2,1)S(1)}, u32[]{:S(2)}, u32[]{:S(2)}) %collective-permute-start.19) | collective-permute-done | bytes 442976 | tf_op jit(solution)/shard_map/ppermute | solution.py:425
  148.8 10.2 %collective-permute-done.28 = bf16[144,3072]{1,0:T(8,128)(2,1)} collective-permute-done((bf16[144,3072]{1,0:T(8,128)(2,1)}, bf16[144,3072]{1,0:T(8,128)(2,1)}, u32[]{:S(2)}, u32[]{:S(2)}) %collective-permute-start.28) | collective-permute-done | bytes 884768 | tf_op jit(solution)/shard_map/ppermute | solution.py:425
  159.1 2.9 broadcast_select_fusion.50
  162.6 4.0 collective-permute-done.23
  168.6 2.7 pad_maximum_fusion.13.blocks_ref
  171.3 17.5 %shard_map.178 = (bf16[512,576]{1,0:T(8,128)(2,1)S(1)}, f32[512,576]{1,0:T(8,128)S(1)}, f32[16,512]{1,0:T(8,128)S(1)}) custom-call(s32[1]{0:T(128)} %bitcast.4.index_ref, bf16[512,576]{1,0:T(8,128)(2,1)S(1)} %copy.63.q_ref, bf16[4,512,384]{2,1,0:T(8,128)(2,1)} %pad_maximum_fusion.13.blocks_ref), custom_call_target="tpu_custom_call" | custom-call | flops 2415919104 | bytes 4194304 | tf_op jit(solution)/shard_map/pallas_call | solution.py:668
  190.1 2.3 broadcast_select_fusion.12
  192.4 2.8 fusion.41
  195.2 4.1 multiply_convert_fusion.4
  201.6 3.8 convolution_convert_fusion.1
  205.4 2.3 convolution_convert_fusion.3
  216.3 22.4 %shard_map.179 = (f32[512,576]{1,0:T(8,128)S(1)}, bf16[4,512,384]{2,1,0:T(8,128)(2,1)}) custom-call(s32[1]{0:T(128)} %bitcast.4.index_ref, bf16[512,576]{1,0:T(8,128)(2,1)S(1)} %copy-done.1, bf16[4,512,384]{2,1,0:T(8,128)(2,1)} %pad_maximum_fusion.13.blocks_ref, bf16[512,576]{1,0:T(8,128)(2,1)S(1)} %copy-done.2, f32[512,576]{1,0:T(8,128)S(1)} %copy-done.6, ...), custom_call_target="tpu_custom_call" | custom-call | flops 6039797760 | bytes 8388608 | tf_op jit(solution)/shard_map/pallas_call | solution.py:691
  253.1 9.1 %collective-permute-done.38 = bf16[384,576]{0,1:T(8,128)(2,1)S(1)} collective-permute-done((bf16[384,576]{0,1:T(8,128)(2,1)S(1)}, bf16[384,576]{0,1:T(8,128)(2,1)S(1)}, u32[]{:S(2)}, u32[]{:S(2)}) %collective-permute-start.38) | collective-permute-done | bytes 442400 | tf_op jit(solution)/shard_map/ppermute | solution.py:425
  263.1 7.5 %collective-permute-done.32 = bf16[512,384]{1,0:T(8,128)(2,1)S(1)} collective-permute-done((bf16[512,384]{1,0:T(8,128)(2,1)S(1)}, bf16[512,384]{1,0:T(8,128)(2,1)S(1)}, u32[]{:S(2)}, u32[]{:S(2)}) %collective-permute-start.32) | collective-permute-done | bytes 393248 | tf_op jit(solution)/shard_map/ppermute | solution.py:425
  277.1 3.5 fusion.26
  283.3 5.6 concatenate.211
  291.5 2.2 add_convert_fusion.3
  293.7 4.7 multiply_convert_fusion.1
  307.7 2.6 collective-permute-start.43
  315.1 3.4 collective-permute-start.40
  318.5 3.2 collective-permute-done.43
  321.7 2.4 collective-permute-start.41
  327.0 12.1 %collective-permute-done.40 = bf16[144,768]{1,0:T(8,128)(2,1)S(1)} collective-permute-done((bf16[144,768]{1,0:T(8,128)(2,1)S(1)}, bf16[144,768]{1,0:T(8,128)(2,1)S(1)}, u32[]{:S(2)}, u32[]{:S(2)}) %collective-permute-start.40) | collective-permute-done | bytes 221216 | tf_op jit(solution)/shard_map/ppermute | solution.py:425
  342.5 8.2 %collective-permute-start.56 = (bf16[144,512]{1,0:T(8,128)(2,1)}, bf16[144,512]{1,0:T(8,128)(2,1)}, u32[]{:S(2)}, u32[]{:S(2)}) collective-permute-start(bf16[144,512]{1,0:T(8,128)(2,1)} %get-tuple-element.212), channel_id=1, source_target_pairs={{0,4},{4,0},{8,12},{12,8},{1,5},{5,1},{9,13},{13,9},{2,6},{6,2},{1... | collective-permute-start | bytes 442376 | tf_op jit(solution)/shard_map/ppermute | solution.py:425
  350.7 3.5 collective-permute-start.55
  357.7 22.4 %shard_map.180 = (f32[512,576]{1,0:T(8,128)S(1)}, bf16[4,512,384]{2,1,0:T(8,128)(2,1)}) custom-call(s32[1]{0:T(128)} %bitcast.4.index_ref, bf16[512,576]{1,0:T(8,128)(2,1)S(1)} %copy.60.q_ref, bf16[4,512,384]{2,1,0:T(8,128)(2,1)} %pad_maximum_fusion.12.blocks_ref, bf16[512,576]{1,0:T(8,128)(2,1)S(1)} %copy.72.grads_ref, f32[512,576]{1,0:T(8,128)S(1)} %copy-done.4, ...), custom_call_target="tpu_custom_call" | custom-call | flops 6039797760 | bytes 8388608 | tf_op jit(solution)/shard_map/pallas_call | solution.py:691
  381.6 3.0 convolution_convert_fusion.6
  392.0 6.1 %collective-permute-done.57 = bf16[144,512]{1,0:T(8,128)(2,1)S(1)} collective-permute-done((bf16[144,512]{1,0:T(8,128)(2,1)S(1)}, bf16[144,512]{1,0:T(8,128)(2,1)S(1)}, u32[]{:S(2)}, u32[]{:S(2)}) %collective-permute-start.57) | collective-permute-done | bytes 147488 | tf_op jit(solution)/shard_map/ppermute | solution.py:425
  402.9 4.4 collective-permute-start.59
  407.3 2.6 collective-permute-done.59
  409.9 5.1 collective-permute-start.64
  417.1 4.0 collective-permute-done.50
  429.9 8.1 %collective-permute-done.88 = bf16[96,576]{0,1:T(8,128)(2,1)S(1)} collective-permute-done((bf16[96,576]{0,1:T(8,128)(2,1)S(1)}, bf16[96,576]{0,1:T(8,128)(2,1)S(1)}, u32[]{:S(2)}, u32[]{:S(2)}) %collective-permute-start.88) | collective-permute-done | bytes 110624 | tf_op jit(solution)/shard_map/ppermute | solution.py:425
  439.5 2.3 collective-permute-start.80
  445.2 2.4 collective-permute-start.82
  447.7 2.4 collective-permute-done.80
  452.3 7.1 %collective-permute-done.81 = bf16[144,768]{1,0:T(8,128)(2,1)S(1)} collective-permute-done((bf16[144,768]{1,0:T(8,128)(2,1)S(1)}, bf16[144,768]{1,0:T(8,128)(2,1)S(1)}, u32[]{:S(2)}, u32[]{:S(2)}) %collective-permute-start.81) | collective-permute-done | bytes 221216 | tf_op jit(solution)/shard_map/ppermute | solution.py:425
  459.4 3.0 collective-permute-start.91
  462.5 8.6 %collective-permute-start.92 = (bf16[96,576]{0,1:T(8,128)(2,1)S(1)}, bf16[96,576]{0,1:T(8,128)(2,1)S(1)}, u32[]{:S(2)}, u32[]{:S(2)}) collective-permute-start(bf16[96,576]{0,1:T(8,128)(2,1)S(1)} %fusion.57), channel_id=1, source_target_pairs={{0,8},{4,12},{8,0},{12,4},{1,9},{5,13},{9,1},{13,5},{2,10},{6,14},... | collective-permute-start | bytes 331784 | tf_op jit(solution)/shard_map/ppermute | solution.py:425
  472.7 3.2 collective-permute-done.92
  489.6 3.9 concatenate.227
  493.8 3.9 collective-permute-done.85
  501.8 4.4 collective-permute-start.63
  506.2 9.4 %collective-permute-done.72 = bf16[144,2048]{1,0:T(8,128)(2,1)S(1)} collective-permute-done((bf16[144,2048]{1,0:T(8,128)(2,1)S(1)}, bf16[144,2048]{1,0:T(8,128)(2,1)S(1)}, u32[]{:S(2)}, u32[]{:S(2)}) %collective-permute-start.72) | collective-permute-done | bytes 589856 | tf_op jit(solution)/shard_map/ppermute | solution.py:425
  516.3 3.5 collective-permute-start.74
  523.8 6.9 %collective-permute-done.74 = bf16[144,512]{1,0:T(8,128)(2,1)S(1)} collective-permute-done((bf16[144,512]{1,0:T(8,128)(2,1)S(1)}, bf16[144,512]{1,0:T(8,128)(2,1)S(1)}, u32[]{:S(2)}, u32[]{:S(2)}) %collective-permute-start.74) | collective-permute-done | bytes 147488 | tf_op jit(solution)/shard_map/ppermute | solution.py:425
  536.0 5.8 %collective-permute-done.66 = bf16[256,576]{0,1:T(8,128)(2,1)S(1)} collective-permute-done((bf16[256,576]{0,1:T(8,128)(2,1)S(1)}, bf16[256,576]{0,1:T(8,128)(2,1)S(1)}, u32[]{:S(2)}, u32[]{:S(2)}) %collective-permute-start.66) | collective-permute-done | bytes 294944 | tf_op jit(solution)/shard_map/ppermute | solution.py:509
  543.3 5.5 collective-permute-done.76
  551.1 2.3 collective-permute-start.79
  554.9 2.6 collective-permute-done.77
  557.5 4.8 collective-permute-done.78
  (490 shorter events, 187.0 us)
Async XLA Ops:
  3.8 14.8 %collective-permute-start.4 = (bf16[144,1538]{1,0:T(8,128)(2,1)S(1)}, bf16[144,1538]{1,0:T(8,128)(2,1)S(1)}, u32[]{:S(2)}, u32[]{:S(2)}) collective-permute-start(bf16[144,1538]{1,0:T(8,128)(2,1)S(1)} %concatenate.191), channel_id=1, source_target_pairs={{0,16},{16,0},{1,17},{17,1},{2,18},{18,2},{3,19},{19,3},{4,20},{20... | collective-permute-start | bytes 1328840 | tf_op jit(solution)/shard_map/ppermute | solution.py:425
  7.8 16.8 %collective-permute-start = (bf16[256,576]{0,1:T(8,128)(2,1)}, bf16[256,576]{0,1:T(8,128)(2,1)}, u32[]{:S(2)}, u32[]{:S(2)}) collective-permute-start(bf16[256,576]{0,1:T(8,128)(2,1)} %get-tuple-element.181), channel_id=1, source_target_pairs={{0,17},{1,19},{2,18},{3,16},{16,1},{17,3},{18,2},{19,0},{4,21},{5,... | collective-permute-start | bytes 884744 | tf_op jit(solution)/shard_map/ppermute | solution.py:491
  7.8 22.7 %collective-permute-start.1 = (bf16[256,576]{0,1:T(8,128)(2,1)}, bf16[256,576]{0,1:T(8,128)(2,1)}, u32[]{:S(2)}, u32[]{:S(2)}) collective-permute-start(bf16[256,576]{0,1:T(8,128)(2,1)} %get-tuple-element.184), channel_id=1, source_target_pairs={{0,16},{1,18},{2,19},{3,17},{16,0},{17,2},{18,3},{19,1},{4,20},{5,... | collective-permute-start | bytes 884744 | tf_op jit(solution)/shard_map/ppermute | solution.py:491
  9.0 28.4 %collective-permute-start.2 = (bf16[256,576]{0,1:T(8,128)(2,1)}, bf16[256,576]{0,1:T(8,128)(2,1)S(1)}, u32[]{:S(2)}, u32[]{:S(2)}) collective-permute-start(bf16[256,576]{0,1:T(8,128)(2,1)} %get-tuple-element.182), channel_id=1, source_target_pairs={{0,1},{1,3},{2,2},{3,0},{16,17},{17,19},{18,18},{19,16},{4,5},{5,7... | collective-permute-start | bytes 884744 | tf_op jit(solution)/shard_map/ppermute | solution.py:491
  12.8 24.6 %collective-permute-start.3 = (bf16[256,576]{0,1:T(8,128)(2,1)}, bf16[256,576]{0,1:T(8,128)(2,1)S(1)}, u32[]{:S(2)}, u32[]{:S(2)}) collective-permute-start(bf16[256,576]{0,1:T(8,128)(2,1)} %get-tuple-element.183), channel_id=1, source_target_pairs={{0,0},{1,2},{2,3},{3,1},{16,16},{17,18},{18,19},{19,17},{4,4},{5,6... | collective-permute-start | bytes 884744 | tf_op jit(solution)/shard_map/ppermute | solution.py:491
  19.5 17.8 %collective-permute-start.5 = (bf16[144,1538]{1,0:T(8,128)(2,1)}, bf16[144,1538]{1,0:T(8,128)(2,1)}, u32[]{:S(2)}, u32[]{:S(2)}) collective-permute-start(bf16[144,1538]{1,0:T(8,128)(2,1)} %broadcast_select_fusion.21), channel_id=1, source_target_pairs={{0,2},{1,3},{2,0},{3,1},{4,6},{5,7},{6,4},{7,5},{8,10},{9,11},{10,... | collective-permute-start | bytes 1328840 | tf_op jit(solution)/shard_map/ppermute | solution.py:425
  37.8 34.0 %collective-permute-start.8 = (bf16[144,3072]{1,0:T(8,128)(2,1)S(1)}, bf16[144,3072]{1,0:T(8,128)(2,1)S(1)}, u32[]{:S(2)}, u32[]{:S(2)}) collective-permute-start(bf16[144,3072]{1,0:T(8,128)(2,1)S(1)} %pad_maximum_fusion.16), channel_id=1, source_target_pairs={{0,16},{16,0},{1,17},{17,1},{2,18},{18,2},{3,19},{19,3},{4,20},{20... | collective-permute-start | bytes 2654216 | tf_op jit(solution)/shard_map/ppermute | solution.py:425
  38.4 31.0 %collective-permute-start.9 = (bf16[384,576]{0,1:T(8,128)(2,1)}, bf16[384,576]{0,1:T(8,128)(2,1)}, u32[]{:S(2)}, u32[]{:S(2)}) collective-permute-start(bf16[384,576]{0,1:T(8,128)(2,1)} %bitcast.13), channel_id=1, source_target_pairs={{0,16},{16,0},{1,17},{17,1},{2,18},{18,2},{3,19},{19,3},{4,20},{20... | collective-permute-start | bytes 1327112 | tf_op jit(solution)/shard_map/ppermute | solution.py:425
  48.3 23.0 %collective-permute-start.11 = (bf16[512,384]{1,0:T(8,128)(2,1)S(1)}, bf16[512,384]{1,0:T(8,128)(2,1)S(1)}, u32[]{:S(2)}, u32[]{:S(2)}) collective-permute-start(bf16[512,384]{1,0:T(8,128)(2,1)S(1)} %pad_maximum_fusion.29), channel_id=1, source_target_pairs={{0,2},{1,3},{2,0},{3,1},{4,6},{5,7},{6,4},{7,5},{8,10},{9,11},{10,... | collective-permute-start | bytes 1179656 | tf_op jit(solution)/shard_map/ppermute | solution.py:425
  75.0 31.5 %collective-permute-start.13 = (bf16[144,3072]{1,0:T(8,128)(2,1)}, bf16[144,3072]{1,0:T(8,128)(2,1)}, u32[]{:S(2)}, u32[]{:S(2)}) collective-permute-start(bf16[144,3072]{1,0:T(8,128)(2,1)} %broadcast_select_fusion.17), channel_id=1, source_target_pairs={{0,2},{1,3},{2,0},{3,1},{4,6},{5,7},{6,4},{7,5},{8,10},{9,11},{10,... | collective-permute-start | bytes 2654216 | tf_op jit(solution)/shard_map/ppermute | solution.py:425
  76.3 30.2 %collective-permute-start.16 = (bf16[384,576]{0,1:T(8,128)(2,1)}, bf16[384,576]{0,1:T(8,128)(2,1)}, u32[]{:S(2)}, u32[]{:S(2)}) collective-permute-start(bf16[384,576]{0,1:T(8,128)(2,1)} %broadcast_select_fusion.55), channel_id=1, source_target_pairs={{0,2},{1,3},{2,0},{3,1},{4,6},{5,7},{6,4},{7,5},{8,10},{9,11},{10,... | collective-permute-start | bytes 1327112 | tf_op jit(solution)/shard_map/ppermute | solution.py:425
  77.6 31.8 %collective-permute-start.18 = (bf16[384,576]{0,1:T(8,128)(2,1)}, bf16[384,576]{0,1:T(8,128)(2,1)S(1)}, u32[]{:S(2)}, u32[]{:S(2)}) collective-permute-start(bf16[384,576]{0,1:T(8,128)(2,1)} %broadcast_select_fusion.55), channel_id=1, source_target_pairs={{0,1},{1,0},{2,3},{3,2},{4,5},{5,4},{6,7},{7,6},{8,9},{9,8},{10,11... | collective-permute-start | bytes 1327112 | tf_op jit(solution)/shard_map/ppermute | solution.py:425
  77.6 33.7 %collective-permute-start.15 = (bf16[144,3072]{1,0:T(8,128)(2,1)}, bf16[144,3072]{1,0:T(8,128)(2,1)S(1)}, u32[]{:S(2)}, u32[]{:S(2)}) collective-permute-start(bf16[144,3072]{1,0:T(8,128)(2,1)} %broadcast_select_fusion.17), channel_id=1, source_target_pairs={{0,1},{1,0},{2,3},{3,2},{4,5},{5,4},{6,7},{7,6},{8,9},{9,8},{10,11... | collective-permute-start | bytes 2654216 | tf_op jit(solution)/shard_map/ppermute | solution.py:425
  116.5 24.7 %collective-permute-start.25 = (bf16[384,576]{0,1:T(8,128)(2,1)}, bf16[384,576]{0,1:T(8,128)(2,1)}, u32[]{:S(2)}, u32[]{:S(2)}) collective-permute-start(bf16[384,576]{0,1:T(8,128)(2,1)} %broadcast_select_fusion.38), channel_id=1, source_target_pairs={{0,2},{1,3},{2,0},{3,1},{4,6},{5,7},{6,4},{7,5},{8,10},{9,11},{10,... | collective-permute-start | bytes 1327112 | tf_op jit(solution)/shard_map/ppermute | solution.py:425
  117.8 41.3 %collective-permute-start.27 = (bf16[384,576]{0,1:T(8,128)(2,1)}, bf16[384,576]{0,1:T(8,128)(2,1)}, u32[]{:S(2)}, u32[]{:S(2)}) collective-permute-start(bf16[384,576]{0,1:T(8,128)(2,1)} %broadcast_select_fusion.38), channel_id=1, source_target_pairs={{0,1},{1,0},{2,3},{3,2},{4,5},{5,4},{6,7},{7,6},{8,9},{9,8},{10,11... | collective-permute-start | bytes 1327112 | tf_op jit(solution)/shard_map/ppermute | solution.py:425
  117.9 22.2 %collective-permute-start.19 = (bf16[144,1538]{1,0:T(8,128)(2,1)S(1)}, bf16[144,1538]{1,0:T(8,128)(2,1)S(1)}, u32[]{:S(2)}, u32[]{:S(2)}) collective-permute-start(bf16[144,1538]{1,0:T(8,128)(2,1)S(1)} %broadcast_select_fusion.20), channel_id=1, source_target_pairs={{0,2},{1,3},{2,0},{3,1},{4,6},{5,7},{6,4},{7,5},{8,10},{9,11},{10,... | collective-permute-start | bytes 1328840 | tf_op jit(solution)/shard_map/ppermute | solution.py:425
  118.6 23.1 %collective-permute-start.21 = (bf16[144,1538]{1,0:T(8,128)(2,1)S(1)}, bf16[144,1538]{1,0:T(8,128)(2,1)S(1)}, u32[]{:S(2)}, u32[]{:S(2)}) collective-permute-start(bf16[144,1538]{1,0:T(8,128)(2,1)S(1)} %broadcast_select_fusion.20), channel_id=1, source_target_pairs={{0,1},{1,0},{2,3},{3,2},{4,5},{5,4},{6,7},{7,6},{8,9},{9,8},{10,11... | collective-permute-start | bytes 1328840 | tf_op jit(solution)/shard_map/ppermute | solution.py:425
  119.9 39.2 %collective-permute-start.28 = (bf16[144,3072]{1,0:T(8,128)(2,1)}, bf16[144,3072]{1,0:T(8,128)(2,1)}, u32[]{:S(2)}, u32[]{:S(2)}) collective-permute-start(bf16[144,3072]{1,0:T(8,128)(2,1)} %broadcast_select_fusion), channel_id=1, source_target_pairs={{0,2},{1,3},{2,0},{3,1},{4,6},{5,7},{6,4},{7,5},{8,10},{9,11},{10,... | collective-permute-start | bytes 2654216 | tf_op jit(solution)/shard_map/ppermute | solution.py:425
  141.2 17.9 %collective-permute-start.26 = (bf16[384,576]{0,1:T(8,128)(2,1)}, bf16[384,576]{0,1:T(8,128)(2,1)}, u32[]{:S(2)}, u32[]{:S(2)}) collective-permute-start(bf16[384,576]{0,1:T(8,128)(2,1)} %collective-permute-done.25), channel_id=1, source_target_pairs={{0,1},{1,0},{2,3},{3,2},{4,5},{5,4},{6,7},{7,6},{8,9},{9,8},{10,11... | collective-permute-start | bytes 1327112 | tf_op jit(solution)/shard_map/ppermute | solution.py:425
  146.6 20.0 %collective-permute-start.23 = (bf16[512,384]{1,0:T(8,128)(2,1)}, bf16[512,384]{1,0:T(8,128)(2,1)}, u32[]{:S(2)}, u32[]{:S(2)}) collective-permute-start(bf16[512,384]{1,0:T(8,128)(2,1)} %pad_maximum_fusion.30), channel_id=1, source_target_pairs={{0,2},{1,3},{2,0},{3,1},{4,6},{5,7},{6,4},{7,5},{8,10},{9,11},{10,... | collective-permute-start | bytes 1179656 | tf_op jit(solution)/shard_map/ppermute | solution.py:425
  148.8 41.2 %collective-permute-start.30 = (bf16[144,3072]{1,0:T(8,128)(2,1)}, bf16[144,3072]{1,0:T(8,128)(2,1)}, u32[]{:S(2)}, u32[]{:S(2)}) collective-permute-start(bf16[144,3072]{1,0:T(8,128)(2,1)} %broadcast_select_fusion), channel_id=1, source_target_pairs={{0,1},{1,0},{2,3},{3,2},{4,5},{5,4},{6,7},{7,6},{8,9},{9,8},{10,11... | collective-permute-start | bytes 2654216 | tf_op jit(solution)/shard_map/ppermute | solution.py:425
  159.1 31.0 %collective-permute-start.29 = (bf16[144,3072]{1,0:T(8,128)(2,1)}, bf16[144,3072]{1,0:T(8,128)(2,1)}, u32[]{:S(2)}, u32[]{:S(2)}) collective-permute-start(bf16[144,3072]{1,0:T(8,128)(2,1)} %collective-permute-done.28), channel_id=1, source_target_pairs={{0,1},{1,0},{2,3},{3,2},{4,5},{5,4},{6,7},{7,6},{8,9},{9,8},{10,11... | collective-permute-start | bytes 2654216 | tf_op jit(solution)/shard_map/ppermute | solution.py:425
  245.5 46.0 %collective-permute-start.33 = (bf16[144,3072]{1,0:T(8,128)(2,1)}, bf16[144,3072]{1,0:T(8,128)(2,1)}, u32[]{:S(2)}, u32[]{:S(2)}) collective-permute-start(bf16[144,3072]{1,0:T(8,128)(2,1)} %get-tuple-element.137), channel_id=1, source_target_pairs={{0,1},{1,0},{2,3},{3,2},{4,5},{5,4},{6,7},{7,6},{8,9},{9,8},{10,11... | collective-permute-start | bytes 2654216 | tf_op jit(solution)/shard_map/ppermute | solution.py:425
  249.1 13.0 %collective-permute-start.38 = (bf16[384,576]{0,1:T(8,128)(2,1)S(1)}, bf16[384,576]{0,1:T(8,128)(2,1)S(1)}, u32[]{:S(2)}, u32[]{:S(2)}) collective-permute-start(bf16[384,576]{0,1:T(8,128)(2,1)S(1)} %add_convert_fusion.16), channel_id=1, source_target_pairs={{0,2},{1,3},{2,0},{3,1},{4,6},{5,7},{6,4},{7,5},{8,10},{9,11},{10,... | collective-permute-start | bytes 1327112 | tf_op jit(solution)/shard_map/ppermute | solution.py:425
  249.8 20.8 %collective-permute-start.32 = (bf16[512,384]{1,0:T(8,128)(2,1)S(1)}, bf16[512,384]{1,0:T(8,128)(2,1)S(1)}, u32[]{:S(2)}, u32[]{:S(2)}) collective-permute-start(bf16[512,384]{1,0:T(8,128)(2,1)S(1)} %fusion.43), channel_id=1, source_target_pairs={{0,2},{1,3},{2,0},{3,1},{4,6},{5,7},{6,4},{7,5},{8,10},{9,11},{10,... | collective-permute-start | bytes 1179656 | tf_op jit(solution)/shard_map/ppermute | solution.py:425
  252.6 38.9 %collective-permute-start.35 = (bf16[144,3072]{1,0:T(8,128)(2,1)}, bf16[144,3072]{1,0:T(8,128)(2,1)}, u32[]{:S(2)}, u32[]{:S(2)}) collective-permute-start(bf16[144,3072]{1,0:T(8,128)(2,1)} %add_convert_fusion.4), channel_id=1, source_target_pairs={{0,2},{1,3},{2,0},{3,1},{4,6},{5,7},{6,4},{7,5},{8,10},{9,11},{10,... | collective-permute-start | bytes 2654216 | tf_op jit(solution)/shard_map/ppermute | solution.py:425
  290.5 23.5 %collective-permute-start.46 = (bf16[144,2048]{1,0:T(8,128)(2,1)S(1)}, bf16[144,2048]{1,0:T(8,128)(2,1)S(1)}, u32[]{:S(2)}, u32[]{:S(2)}) collective-permute-start(bf16[144,2048]{1,0:T(8,128)(2,1)S(1)} %get-tuple-element.150), channel_id=1, source_target_pairs={{0,1},{1,0},{2,3},{3,2},{4,5},{5,4},{6,7},{7,6},{8,9},{9,8},{10,11... | collective-permute-start | bytes 1769480 | tf_op jit(solution)/shard_map/ppermute | solution.py:425
  290.5 50.8 %collective-permute-start.45 = (bf16[144,2048]{1,0:T(8,128)(2,1)S(1)}, bf16[144,2048]{1,0:T(8,128)(2,1)S(1)}, u32[]{:S(2)}, u32[]{:S(2)}) collective-permute-start(bf16[144,2048]{1,0:T(8,128)(2,1)S(1)} %get-tuple-element.149), channel_id=1, source_target_pairs={{0,1},{1,0},{2,3},{3,2},{4,5},{5,4},{6,7},{7,6},{8,9},{9,8},{10,11... | collective-permute-start | bytes 1769480 | tf_op jit(solution)/shard_map/ppermute | solution.py:425
  307.7 14.0 %collective-permute-start.43 = (bf16[96,576]{0,1:T(8,128)(2,1)S(1)}, bf16[96,576]{0,1:T(8,128)(2,1)S(1)}, u32[]{:S(2)}, u32[]{:S(2)}) collective-permute-start(bf16[96,576]{0,1:T(8,128)(2,1)S(1)} %get-tuple-element.232), channel_id=1, source_target_pairs={{0,8},{4,12},{8,0},{12,4},{1,9},{5,13},{9,1},{13,5},{2,10},{6,14},... | collective-permute-start | bytes 331784 | tf_op jit(solution)/shard_map/ppermute | solution.py:425
  310.3 13.8 %collective-permute-start.44 = (bf16[96,576]{0,1:T(8,128)(2,1)S(1)}, bf16[96,576]{0,1:T(8,128)(2,1)S(1)}, u32[]{:S(2)}, u32[]{:S(2)}) collective-permute-start(bf16[96,576]{0,1:T(8,128)(2,1)S(1)} %get-tuple-element.231), channel_id=1, source_target_pairs={{0,12},{4,8},{8,4},{12,0},{1,13},{5,9},{9,5},{13,1},{2,14},{6,10},... | collective-permute-start | bytes 331784 | tf_op jit(solution)/shard_map/ppermute | solution.py:425
  314.0 11.9 %collective-permute-start.39 = (bf16[144,768]{1,0:T(8,128)(2,1)S(1)}, bf16[144,768]{1,0:T(8,128)(2,1)S(1)}, u32[]{:S(2)}, u32[]{:S(2)}) collective-permute-start(bf16[144,768]{1,0:T(8,128)(2,1)S(1)} %get-tuple-element.192), channel_id=1, source_target_pairs={{0,4},{4,0},{8,12},{12,8},{1,5},{5,1},{9,13},{13,9},{2,6},{6,2},{1... | collective-permute-start | bytes 663560 | tf_op jit(solution)/shard_map/ppermute | solution.py:425
  315.1 23.9 %collective-permute-start.40 = (bf16[144,768]{1,0:T(8,128)(2,1)S(1)}, bf16[144,768]{1,0:T(8,128)(2,1)S(1)}, u32[]{:S(2)}, u32[]{:S(2)}) collective-permute-start(bf16[144,768]{1,0:T(8,128)(2,1)S(1)} %get-tuple-element.194), channel_id=1, source_target_pairs={{0,8},{4,12},{8,0},{12,4},{1,9},{5,13},{9,1},{13,5},{2,10},{6,14},... | collective-permute-start | bytes 663560 | tf_op jit(solution)/shard_map/ppermute | solution.py:425
  321.7 17.4 %collective-permute-start.41 = (bf16[144,768]{1,0:T(8,128)(2,1)S(1)}, bf16[144,768]{1,0:T(8,128)(2,1)S(1)}, u32[]{:S(2)}, u32[]{:S(2)}) collective-permute-start(bf16[144,768]{1,0:T(8,128)(2,1)S(1)} %get-tuple-element.193), channel_id=1, source_target_pairs={{0,12},{4,8},{8,4},{12,0},{1,13},{5,9},{9,5},{13,1},{2,14},{6,10},... | collective-permute-start | bytes 663560 | tf_op jit(solution)/shard_map/ppermute | solution.py:425
  324.1 16.3 %collective-permute-start.52 = (bf16[384,576]{0,1:T(8,128)(2,1)S(1)}, bf16[384,576]{0,1:T(8,128)(2,1)S(1)}, u32[]{:S(2)}, u32[]{:S(2)}) collective-permute-start(bf16[384,576]{0,1:T(8,128)(2,1)S(1)} %get-tuple-element.162), channel_id=1, source_target_pairs={{0,1},{1,0},{2,3},{3,2},{4,5},{5,4},{6,7},{7,6},{8,9},{9,8},{10,11... | collective-permute-start | bytes 1327112 | tf_op jit(solution)/shard_map/ppermute | solution.py:425
  325.9 15.5 %collective-permute-start.47 = (bf16[144,2048]{1,0:T(8,128)(2,1)S(1)}, bf16[144,2048]{1,0:T(8,128)(2,1)S(1)}, u32[]{:S(2)}, u32[]{:S(2)}) collective-permute-start(bf16[144,2048]{1,0:T(8,128)(2,1)S(1)} %add_convert_fusion.10), channel_id=1, source_target_pairs={{0,2},{1,3},{2,0},{3,1},{4,6},{5,7},{6,4},{7,5},{8,10},{9,11},{10,... | collective-permute-start | bytes 1769480 | tf_op jit(solution)/shard_map/ppermute | solution.py:425
  339.1 76.6 %collective-permute-start.51 = (bf16[384,576]{0,1:T(8,128)(2,1)}, bf16[384,576]{0,1:T(8,128)(2,1)}, u32[]{:S(2)}, u32[]{:S(2)}) collective-permute-start(bf16[384,576]{0,1:T(8,128)(2,1)} %get-tuple-element.161), channel_id=1, source_target_pairs={{0,1},{1,0},{2,3},{3,2},{4,5},{5,4},{6,7},{7,6},{8,9},{9,8},{10,11... | collective-permute-start | bytes 1327112 | tf_op jit(solution)/shard_map/ppermute | solution.py:425
  339.1 48.9 %collective-permute-start.49 = (bf16[144,3072]{1,0:T(8,128)(2,1)}, bf16[144,3072]{1,0:T(8,128)(2,1)}, u32[]{:S(2)}, u32[]{:S(2)}) collective-permute-start(bf16[144,3072]{1,0:T(8,128)(2,1)} %get-tuple-element.136), channel_id=1, source_target_pairs={{0,1},{1,0},{2,3},{3,2},{4,5},{5,4},{6,7},{7,6},{8,9},{9,8},{10,11... | collective-permute-start | bytes 2654216 | tf_op jit(solution)/shard_map/ppermute | solution.py:425
  340.4 76.6 %collective-permute-start.48 = (bf16[144,3072]{1,0:T(8,128)(2,1)}, bf16[144,3072]{1,0:T(8,128)(2,1)}, u32[]{:S(2)}, u32[]{:S(2)}) collective-permute-start(bf16[144,3072]{1,0:T(8,128)(2,1)} %get-tuple-element.135), channel_id=1, source_target_pairs={{0,1},{1,0},{2,3},{3,2},{4,5},{5,4},{6,7},{7,6},{8,9},{9,8},{10,11... | collective-permute-start | bytes 2654216 | tf_op jit(solution)/shard_map/ppermute | solution.py:425
  342.5 48.6 %collective-permute-start.56 = (bf16[144,512]{1,0:T(8,128)(2,1)}, bf16[144,512]{1,0:T(8,128)(2,1)}, u32[]{:S(2)}, u32[]{:S(2)}) collective-permute-start(bf16[144,512]{1,0:T(8,128)(2,1)} %get-tuple-element.212), channel_id=1, source_target_pairs={{0,4},{4,0},{8,12},{12,8},{1,5},{5,1},{9,13},{13,9},{2,6},{6,2},{1... | collective-permute-start | bytes 442376 | tf_op jit(solution)/shard_map/ppermute | solution.py:425
  350.7 34.1 %collective-permute-start.55 = (bf16[96,576]{0,1:T(8,128)(2,1)}, bf16[96,576]{0,1:T(8,128)(2,1)}, u32[]{:S(2)}, u32[]{:S(2)}) collective-permute-start(bf16[96,576]{0,1:T(8,128)(2,1)} %add_convert_fusion.37), channel_id=1, source_target_pairs={{0,16},{1,17},{2,18},{3,19},{4,20},{5,21},{6,22},{7,23},{8,24},{9,... | collective-permute-start | bytes 331784 | tf_op jit(solution)/shard_map/ppermute | solution.py:534
  384.9 13.3 %collective-permute-start.57 = (bf16[144,512]{1,0:T(8,128)(2,1)S(1)}, bf16[144,512]{1,0:T(8,128)(2,1)S(1)}, u32[]{:S(2)}, u32[]{:S(2)}) collective-permute-start(bf16[144,512]{1,0:T(8,128)(2,1)S(1)} %copy-done.78), channel_id=1, source_target_pairs={{0,8},{4,12},{8,0},{12,4},{1,9},{5,13},{9,1},{13,5},{2,10},{6,14},... | collective-permute-start | bytes 442376 | tf_op jit(solution)/shard_map/ppermute | solution.py:425
  388.0 11.4 %collective-permute-start.58 = (bf16[144,512]{1,0:T(8,128)(2,1)S(1)}, bf16[144,512]{1,0:T(8,128)(2,1)S(1)}, u32[]{:S(2)}, u32[]{:S(2)}) collective-permute-start(bf16[144,512]{1,0:T(8,128)(2,1)S(1)} %copy-done.77), channel_id=1, source_target_pairs={{0,12},{4,8},{8,4},{12,0},{1,13},{5,9},{9,5},{13,1},{2,14},{6,10},... | collective-permute-start | bytes 442376 | tf_op jit(solution)/shard_map/ppermute | solution.py:425
  391.1 24.6 %collective-permute-start.53 = (bf16[384,576]{0,1:T(8,128)(2,1)S(1)}, bf16[384,576]{0,1:T(8,128)(2,1)S(1)}, u32[]{:S(2)}, u32[]{:S(2)}) collective-permute-start(bf16[384,576]{0,1:T(8,128)(2,1)S(1)} %copy-done.71), channel_id=1, source_target_pairs={{0,2},{1,3},{2,0},{3,1},{4,6},{5,7},{6,4},{7,5},{8,10},{9,11},{10,... | collective-permute-start | bytes 1327112 | tf_op jit(solution)/shard_map/ppermute | solution.py:425
  399.5 21.6 %collective-permute-start.50 = (bf16[144,3072]{1,0:T(8,128)(2,1)S(1)}, bf16[144,3072]{1,0:T(8,128)(2,1)S(1)}, u32[]{:S(2)}, u32[]{:S(2)}) collective-permute-start(bf16[144,3072]{1,0:T(8,128)(2,1)S(1)} %add_convert_fusion.1), channel_id=1, source_target_pairs={{0,2},{1,3},{2,0},{3,1},{4,6},{5,7},{6,4},{7,5},{8,10},{9,11},{10,... | collective-permute-start | bytes 2654216 | tf_op jit(solution)/shard_map/ppermute | solution.py:425
  409.9 106.3 %collective-permute-start.64 = (bf16[256,576]{0,1:T(8,128)(2,1)}, bf16[256,576]{0,1:T(8,128)(2,1)}, u32[]{:S(2)}, u32[]{:S(2)}) collective-permute-start(bf16[256,576]{0,1:T(8,128)(2,1)} %get-tuple-element.208), channel_id=1, source_target_pairs={{0,16},{2,17},{3,18},{1,19},{4,20},{6,21},{7,22},{5,23},{8,24},{10... | collective-permute-start | bytes 884744 | tf_op jit(solution)/shard_map/ppermute | solution.py:509
  424.2 13.8 %collective-permute-start.88 = (bf16[96,576]{0,1:T(8,128)(2,1)S(1)}, bf16[96,576]{0,1:T(8,128)(2,1)S(1)}, u32[]{:S(2)}, u32[]{:S(2)}) collective-permute-start(bf16[96,576]{0,1:T(8,128)(2,1)S(1)} %get-tuple-element.229), channel_id=1, source_target_pairs={{0,8},{4,12},{8,0},{12,4},{1,9},{5,13},{9,1},{13,5},{2,10},{6,14},... | collective-permute-start | bytes 331784 | tf_op jit(solution)/shard_map/ppermute | solution.py:425
  426.2 11.8 %collective-permute-start.89 = (bf16[96,576]{0,1:T(8,128)(2,1)S(1)}, bf16[96,576]{0,1:T(8,128)(2,1)S(1)}, u32[]{:S(2)}, u32[]{:S(2)}) collective-permute-start(bf16[96,576]{0,1:T(8,128)(2,1)S(1)} %get-tuple-element.228), channel_id=1, source_target_pairs={{0,12},{4,8},{8,4},{12,0},{1,13},{5,9},{9,5},{13,1},{2,14},{6,10},... | collective-permute-start | bytes 331784 | tf_op jit(solution)/shard_map/ppermute | solution.py:425
  427.7 43.5 %collective-permute-start.60 = (bf16[2,512,384]{2,1,0:T(8,128)(2,1)S(1)}, bf16[2,512,384]{2,1,0:T(8,128)(2,1)S(1)}, u32[]{:S(2)}, u32[]{:S(2)}) collective-permute-start(bf16[2,512,384]{2,1,0:T(8,128)(2,1)S(1)} %slice.252), channel_id=1, source_target_pairs={{0,1},{1,0},{2,3},{3,2},{4,5},{5,4},{6,7},{7,6},{8,9},{9,8},{10,11... | collective-permute-start | bytes 2359304 | tf_op jit(solution)/shard_map/ppermute | solution.py:425
  441.8 17.6 %collective-permute-start.81 = (bf16[144,768]{1,0:T(8,128)(2,1)S(1)}, bf16[144,768]{1,0:T(8,128)(2,1)S(1)}, u32[]{:S(2)}, u32[]{:S(2)}) collective-permute-start(bf16[144,768]{1,0:T(8,128)(2,1)S(1)} %get-tuple-element.191), channel_id=1, source_target_pairs={{0,8},{4,12},{8,0},{12,4},{1,9},{5,13},{9,1},{13,5},{2,10},{6,14},... | collective-permute-start | bytes 663560 | tf_op jit(solution)/shard_map/ppermute | solution.py:425
  445.2 17.3 %collective-permute-start.82 = (bf16[144,768]{1,0:T(8,128)(2,1)S(1)}, bf16[144,768]{1,0:T(8,128)(2,1)S(1)}, u32[]{:S(2)}, u32[]{:S(2)}) collective-permute-start(bf16[144,768]{1,0:T(8,128)(2,1)S(1)} %get-tuple-element.190), channel_id=1, source_target_pairs={{0,12},{4,8},{8,4},{12,0},{1,13},{5,9},{9,5},{13,1},{2,14},{6,10},... | collective-permute-start | bytes 663560 | tf_op jit(solution)/shard_map/ppermute | solution.py:425
  450.1 69.7 %collective-permute-start.65 = (bf16[256,576]{0,1:T(8,128)(2,1)}, bf16[256,576]{0,1:T(8,128)(2,1)}, u32[]{:S(2)}, u32[]{:S(2)}) collective-permute-start(bf16[256,576]{0,1:T(8,128)(2,1)} %get-tuple-element.209), channel_id=1, source_target_pairs={{1,16},{3,17},{2,18},{0,19},{5,20},{7,21},{6,22},{4,23},{9,24},{11... | collective-permute-start | bytes 884744 | tf_op jit(solution)/shard_map/ppermute | solution.py:509
  459.4 11.9 %collective-permute-start.91 = (bf16[96,576]{0,1:T(8,128)(2,1)S(1)}, bf16[96,576]{0,1:T(8,128)(2,1)S(1)}, u32[]{:S(2)}, u32[]{:S(2)}) collective-permute-start(bf16[96,576]{0,1:T(8,128)(2,1)S(1)} %fusion.57), channel_id=1, source_target_pairs={{0,12},{4,8},{8,4},{12,0},{1,13},{5,9},{9,5},{13,1},{2,14},{6,10},... | collective-permute-start | bytes 331784 | tf_op jit(solution)/shard_map/ppermute | solution.py:425
  462.5 13.4 %collective-permute-start.92 = (bf16[96,576]{0,1:T(8,128)(2,1)S(1)}, bf16[96,576]{0,1:T(8,128)(2,1)S(1)}, u32[]{:S(2)}, u32[]{:S(2)}) collective-permute-start(bf16[96,576]{0,1:T(8,128)(2,1)S(1)} %fusion.57), channel_id=1, source_target_pairs={{0,8},{4,12},{8,0},{12,4},{1,9},{5,13},{9,1},{13,5},{2,10},{6,14},... | collective-permute-start | bytes 331784 | tf_op jit(solution)/shard_map/ppermute | solution.py:425
  479.3 14.4 %collective-permute-start.84 = (bf16[144,768]{1,0:T(8,128)(2,1)S(1)}, bf16[144,768]{1,0:T(8,128)(2,1)}, u32[]{:S(2)}, u32[]{:S(2)}) collective-permute-start(bf16[144,768]{1,0:T(8,128)(2,1)S(1)} %fusion.51), channel_id=1, source_target_pairs={{0,12},{4,8},{8,4},{12,0},{1,13},{5,9},{9,5},{13,1},{2,14},{6,10},... | collective-permute-start | bytes 663560 | tf_op jit(solution)/shard_map/ppermute | solution.py:425
  480.8 16.9 %collective-permute-start.85 = (bf16[144,768]{1,0:T(8,128)(2,1)S(1)}, bf16[144,768]{1,0:T(8,128)(2,1)}, u32[]{:S(2)}, u32[]{:S(2)}) collective-permute-start(bf16[144,768]{1,0:T(8,128)(2,1)S(1)} %fusion.51), channel_id=1, source_target_pairs={{0,8},{4,12},{8,0},{12,4},{1,9},{5,13},{9,1},{13,5},{2,10},{6,14},... | collective-permute-start | bytes 663560 | tf_op jit(solution)/shard_map/ppermute | solution.py:425
  483.6 14.1 %collective-permute-start.86 = (bf16[144,768]{1,0:T(8,128)(2,1)S(1)}, bf16[144,768]{1,0:T(8,128)(2,1)}, u32[]{:S(2)}, u32[]{:S(2)}) collective-permute-start(bf16[144,768]{1,0:T(8,128)(2,1)S(1)} %fusion.51), channel_id=1, source_target_pairs={{0,4},{4,0},{8,12},{12,8},{1,5},{5,1},{9,13},{13,9},{2,6},{6,2},{1... | collective-permute-start | bytes 663560 | tf_op jit(solution)/shard_map/ppermute | solution.py:425
  499.4 16.2 %collective-permute-start.72 = (bf16[144,2048]{1,0:T(8,128)(2,1)S(1)}, bf16[144,2048]{1,0:T(8,128)(2,1)S(1)}, u32[]{:S(2)}, u32[]{:S(2)}) collective-permute-start(bf16[144,2048]{1,0:T(8,128)(2,1)S(1)} %add_convert_fusion.7), channel_id=1, source_target_pairs={{0,2},{1,3},{2,0},{3,1},{4,6},{5,7},{6,4},{7,5},{8,10},{9,11},{10,... | collective-permute-start | bytes 1769480 | tf_op jit(solution)/shard_map/ppermute | solution.py:425
  501.1 20.6 %collective-permute-start.62 = (bf16[256,576]{0,1:T(8,128)(2,1)S(1)}, bf16[256,576]{0,1:T(8,128)(2,1)S(1)}, u32[]{:S(2)}, u32[]{:S(2)}) collective-permute-start(bf16[256,576]{0,1:T(8,128)(2,1)S(1)} %get-tuple-element.210), channel_id=1, source_target_pairs={{0,0},{2,1},{3,2},{1,3},{4,4},{6,5},{7,6},{5,7},{8,8},{10,9},{11,1... | collective-permute-start | bytes 884744 | tf_op jit(solution)/shard_map/ppermute | solution.py:509
  501.8 31.6 %collective-permute-start.63 = (bf16[256,576]{0,1:T(8,128)(2,1)S(1)}, bf16[256,576]{0,1:T(8,128)(2,1)S(1)}, u32[]{:S(2)}, u32[]{:S(2)}) collective-permute-start(bf16[256,576]{0,1:T(8,128)(2,1)S(1)} %get-tuple-element.211), channel_id=1, source_target_pairs={{1,0},{3,1},{2,2},{0,3},{5,4},{7,5},{6,6},{4,7},{9,8},{11,9},{10,1... | collective-permute-start | bytes 884744 | tf_op jit(solution)/shard_map/ppermute | solution.py:509
  516.3 14.4 %collective-permute-start.74 = (bf16[144,512]{1,0:T(8,128)(2,1)S(1)}, bf16[144,512]{1,0:T(8,128)(2,1)S(1)}, u32[]{:S(2)}, u32[]{:S(2)}) collective-permute-start(bf16[144,512]{1,0:T(8,128)(2,1)S(1)} %get-tuple-element.207), channel_id=1, source_target_pairs={{0,8},{4,12},{8,0},{12,4},{1,9},{5,13},{9,1},{13,5},{2,10},{6,14},... | collective-permute-start | bytes 442376 | tf_op jit(solution)/shard_map/ppermute | solution.py:425
  519.8 12.3 %collective-permute-start.75 = (bf16[144,512]{1,0:T(8,128)(2,1)S(1)}, bf16[144,512]{1,0:T(8,128)(2,1)S(1)}, u32[]{:S(2)}, u32[]{:S(2)}) collective-permute-start(bf16[144,512]{1,0:T(8,128)(2,1)S(1)} %get-tuple-element.206), channel_id=1, source_target_pairs={{0,12},{4,8},{8,4},{12,0},{1,13},{5,9},{9,5},{13,1},{2,14},{6,10},... | collective-permute-start | bytes 442376 | tf_op jit(solution)/shard_map/ppermute | solution.py:425
  521.7 14.3 %collective-permute-start.68 = (bf16[256,576]{0,1:T(8,128)(2,1)}, bf16[256,576]{0,1:T(8,128)(2,1)S(1)}, u32[]{:S(2)}, u32[]{:S(2)}) collective-permute-start(bf16[256,576]{0,1:T(8,128)(2,1)} %get-tuple-element.208), channel_id=1, source_target_pairs={{16,16},{18,17},{19,18},{17,19},{20,20},{22,21},{23,22},{21,23},{2... | collective-permute-start | bytes 884744 | tf_op jit(solution)/shard_map/ppermute | solution.py:509
  523.1 12.9 %collective-permute-start.69 = (bf16[256,576]{0,1:T(8,128)(2,1)}, bf16[256,576]{0,1:T(8,128)(2,1)S(1)}, u32[]{:S(2)}, u32[]{:S(2)}) collective-permute-start(bf16[256,576]{0,1:T(8,128)(2,1)} %get-tuple-element.209), channel_id=1, source_target_pairs={{17,16},{19,17},{18,18},{16,19},{21,20},{23,21},{22,22},{20,23},{2... | collective-permute-start | bytes 884744 | tf_op jit(solution)/shard_map/ppermute | solution.py:509
  533.4 15.4 %collective-permute-start.76 = (bf16[144,512]{1,0:T(8,128)(2,1)S(1)}, bf16[144,512]{1,0:T(8,128)(2,1)S(1)}, u32[]{:S(2)}, u32[]{:S(2)}) collective-permute-start(bf16[144,512]{1,0:T(8,128)(2,1)S(1)} %add_convert_fusion.33), channel_id=1, source_target_pairs={{16,0},{17,1},{18,2},{19,3},{20,4},{21,5},{22,6},{23,7},{24,8},{25... | collective-permute-start | bytes 442376 | tf_op jit(solution)/shard_map/ppermute | solution.py:534
  (122 other events, 834.3 us)

commit v4 on v3

--- a/solution.py
+++ b/solution.py
@@ -781,12 +781,12 @@
     grad_query, parts = attend_backward(
         query_rot, blocks, grad_heads, attended, log_total, index
     )
-    parts, pending = tied(parts, pending)
     received = xor_send(parts[1::2], "shard", 1)
     own_sum = add_low(parts[0], received[0])
     cross_sum = add_low(parts[2], received[1])
     key_width = KV_HEADS * HEAD
     grad_kv = own_sum.astype(jnp.float32) + xor_send(cross_sum, "shard", 2).astype(jnp.float32)
+    grad_kv, pending = tied(grad_kv, pending)
     grad_query_rows = (
         rotate_back(grad_query.reshape(1, tok_count, HEADS, HEAD), tables)
         .astype(jnp.bfloat16)

time: 574 us -> 593 us (1.033)
  the two profiles are of different devices: /device:TPU:0 before, /device:TPU:5 now
where the time goes in v4:
time: 593 us; the launch traced here: 584 us
  waiting for transfers between devices  198 us (33%)
  starting transfers between devices  122 us (21%)
  Pallas kernels  77.7 us (13%)
  other arithmetic  69.1 us (12%)
  local copies, waits for them, and re-layouts  61 us (10%)
  matrix products  52.8 us (9%)
    ppermute x76, waiting for transfers between devices, xor_send(): return lax.ppermute(value, axis, [(i, i ^ bits) for i in range(peers)])  154 us
    ppermute x76, starting transfers between devices, xor_send(): return lax.ppermute(value, axis, [(i, i ^ bits) for i in range(peers)])  86.7 us
    pallas_call x2, Pallas kernels, attend_backward(): pl.pallas_call(attend_backward_kernel, out_shape=(jax.ShapeDtypeStruct((r...  45.4 us
    pallas_call x2, Pallas kernels, attend_forward(): pl.pallas_call(attend_forward_kernel, out_shape=(jax.ShapeDtypeStruct((ro...  32.3 us
    dot_general x8, matrix products, input_grad(): jnp.einsum('rf,df->rd', gradient, weight, preferred_element_type=jnp.floa...  21.2 us
    ppermute x8, starting transfers between devices, unfold_rows(): lax.ppermute(parts[half], ('section', 'shard'), section_pairs(half, moves...  18.2 us
    dot_general x8, matrix products, weight_grad(): jnp.einsum('rd,rf->df', left_side, right_side, preferred_element_type=jnp...  17.5 us
    ppermute x8, waiting for transfers between devices, unfold_rows(): lax.ppermute(parts[half], ('section', 'shard'), section_pairs(half, moves...  16.9 us
  transfers between devices with their start and end apart: 94, of which 34 were waited for; matrix products, arithmetic and copies ran while one was open for 22% of the time, Pallas kernels for 9%

profile of v4, /device:TPU:5, one launch (start us, length us, event | category | flops | bytes accessed | tf_op | source)
XLA Modules:
  0.0 584.3 jit_solution(5556875191411279475)
XLA Ops:
  10.3 3.4 collective-permute-start.3
  17.2 4.6 collective-permute-done
  21.8 7.8 %collective-permute-done.1 = bf16[256,576]{0,1:T(8,128)(2,1)} collective-permute-done((bf16[256,576]{0,1:T(8,128)(2,1)}, bf16[256,576]{0,1:T(8,128)(2,1)}, u32[]{:S(2)}, u32[]{:S(2)}) %collective-permute-start.1) | collective-permute-done | bytes 294944 | tf_op jit(solution)/shard_map/ppermute | solution.py:491
  30.7 5.2 collective-permute-done.5
  47.1 20.4 %collective-permute-done.9 = bf16[384,576]{0,1:T(8,128)(2,1)} collective-permute-done((bf16[384,576]{0,1:T(8,128)(2,1)}, bf16[384,576]{0,1:T(8,128)(2,1)}, u32[]{:S(2)}, u32[]{:S(2)}) %collective-permute-start.9) | collective-permute-done | bytes 442400 | tf_op jit(solution)/shard_map/ppermute | solution.py:425
  76.7 16.0 %shard_map.177 = (bf16[512,576]{1,0:T(8,128)(2,1)S(1)}, f32[512,576]{1,0:T(8,128)S(1)}, f32[16,512]{1,0:T(8,128)S(1)}) custom-call(s32[1]{0:T(128)} %bitcast.4.index_ref, bf16[512,576]{1,0:T(8,128)(2,1)S(1)} %copy.60.q_ref, bf16[4,512,384]{2,1,0:T(8,128)(2,1)} %pad_maximum_fusion.12.blocks_ref), custom_call_target="tpu_custom_call" | custom-call | flops 2415919104 | bytes 4194304 | tf_op jit(solution)/shard_map/pallas_call | solution.py:668
  92.7 11.6 %collective-permute-done.16 = bf16[384,576]{0,1:T(8,128)(2,1)} collective-permute-done((bf16[384,576]{0,1:T(8,128)(2,1)}, bf16[384,576]{0,1:T(8,128)(2,1)}, u32[]{:S(2)}, u32[]{:S(2)}) %collective-permute-start.16) | collective-permute-done | bytes 442400 | tf_op jit(solution)/shard_map/ppermute | solution.py:425
  105.5 2.3 multiply_reduce_fusion.5
  109.8 2.4 broadcast_select_fusion.16
  112.7 2.3 broadcast_select_fusion.38
  119.1 2.7 fusion.69
  124.6 12.2 %collective-permute-done.19 = bf16[144,1538]{1,0:T(8,128)(2,1)S(1)} collective-permute-done((bf16[144,1538]{1,0:T(8,128)(2,1)S(1)}, bf16[144,1538]{1,0:T(8,128)(2,1)S(1)}, u32[]{:S(2)}, u32[]{:S(2)}) %collective-permute-start.19) | collective-permute-done | bytes 442976 | tf_op jit(solution)/shard_map/ppermute | solution.py:425
  136.7 2.3 collective-permute-start.20
  147.3 8.5 %collective-permute-done.28 = bf16[144,3072]{1,0:T(8,128)(2,1)} collective-permute-done((bf16[144,3072]{1,0:T(8,128)(2,1)}, bf16[144,3072]{1,0:T(8,128)(2,1)}, u32[]{:S(2)}, u32[]{:S(2)}) %collective-permute-start.28) | collective-permute-done | bytes 884768 | tf_op jit(solution)/shard_map/ppermute | solution.py:425
  155.8 2.3 collective-permute-start.29
  158.1 2.9 broadcast_select_fusion.50
  161.1 3.1 collective-permute-done.23
  167.3 2.7 pad_maximum_fusion.13.blocks_ref
  170.0 16.3 %shard_map.178 = (bf16[512,576]{1,0:T(8,128)(2,1)S(1)}, f32[512,576]{1,0:T(8,128)S(1)}, f32[16,512]{1,0:T(8,128)S(1)}) custom-call(s32[1]{0:T(128)} %bitcast.4.index_ref, bf16[512,576]{1,0:T(8,128)(2,1)S(1)} %copy.63.q_ref, bf16[4,512,384]{2,1,0:T(8,128)(2,1)} %pad_maximum_fusion.13.blocks_ref), custom_call_target="tpu_custom_call" | custom-call | flops 2415919104 | bytes 4194304 | tf_op jit(solution)/shard_map/pallas_call | solution.py:668
  187.5 2.3 broadcast_select_fusion.12
  189.8 2.8 fusion.41
  192.7 3.9 multiply_convert_fusion.4
  196.6 2.2 multiply_reduce_fusion.1
  198.8 3.8 convolution_convert_fusion.1
  202.6 2.3 convolution_convert_fusion.3
  213.5 22.7 %shard_map.179 = (f32[512,576]{1,0:T(8,128)S(1)}, bf16[4,512,384]{2,1,0:T(8,128)(2,1)}) custom-call(s32[1]{0:T(128)} %bitcast.4.index_ref, bf16[512,576]{1,0:T(8,128)(2,1)S(1)} %copy-done.1, bf16[4,512,384]{2,1,0:T(8,128)(2,1)} %pad_maximum_fusion.13.blocks_ref, bf16[512,576]{1,0:T(8,128)(2,1)S(1)} %copy-done.2, f32[512,576]{1,0:T(8,128)S(1)} %copy-done.6, ...), custom_call_target="tpu_custom_call" | custom-call | flops 6039797760 | bytes 8388608 | tf_op jit(solution)/shard_map/pallas_call | solution.py:691
  251.4 7.7 %collective-permute-done.38 = bf16[384,576]{0,1:T(8,128)(2,1)S(1)} collective-permute-done((bf16[384,576]{0,1:T(8,128)(2,1)S(1)}, bf16[384,576]{0,1:T(8,128)(2,1)S(1)}, u32[]{:S(2)}, u32[]{:S(2)}) %collective-permute-start.38) | collective-permute-done | bytes 442400 | tf_op jit(solution)/shard_map/ppermute | solution.py:425
  260.1 7.4 %collective-permute-done.32 = bf16[512,384]{1,0:T(8,128)(2,1)S(1)} collective-permute-done((bf16[512,384]{1,0:T(8,128)(2,1)S(1)}, bf16[512,384]{1,0:T(8,128)(2,1)S(1)}, u32[]{:S(2)}, u32[]{:S(2)}) %collective-permute-start.32) | collective-permute-done | bytes 393248 | tf_op jit(solution)/shard_map/ppermute | solution.py:425
  274.0 3.5 fusion.26
  280.2 5.6 concatenate.211
  289.2 2.2 add_convert_fusion.3
  291.5 4.9 multiply_convert_fusion.1
  305.3 2.3 collective-permute-start.43
  312.3 2.6 collective-permute-start.40
  315.0 4.0 collective-permute-start.41
  319.0 3.4 collective-permute-start.54
  324.6 10.1 %collective-permute-done.40 = bf16[144,768]{1,0:T(8,128)(2,1)S(1)} collective-permute-done((bf16[144,768]{1,0:T(8,128)(2,1)S(1)}, bf16[144,768]{1,0:T(8,128)(2,1)S(1)}, u32[]{:S(2)}, u32[]{:S(2)}) %collective-permute-start.40) | collective-permute-done | bytes 221216 | tf_op jit(solution)/shard_map/ppermute | solution.py:425
  334.7 2.7 collective-permute-start.53
  340.2 7.7 %collective-permute-start.58 = (bf16[144,512]{1,0:T(8,128)(2,1)}, bf16[144,512]{1,0:T(8,128)(2,1)}, u32[]{:S(2)}, u32[]{:S(2)}) collective-permute-start(bf16[144,512]{1,0:T(8,128)(2,1)} %get-tuple-element.212), channel_id=1, source_target_pairs={{0,4},{4,0},{8,12},{12,8},{1,5},{5,1},{9,13},{13,9},{2,6},{6,2},{1... | collective-permute-start | bytes 442376 | tf_op jit(solution)/shard_map/ppermute | solution.py:425
  350.0 3.3 collective-permute-start.57
  356.8 22.7 %shard_map.180 = (f32[512,576]{1,0:T(8,128)S(1)}, bf16[4,512,384]{2,1,0:T(8,128)(2,1)}) custom-call(s32[1]{0:T(128)} %bitcast.4.index_ref, bf16[512,576]{1,0:T(8,128)(2,1)S(1)} %copy.60.q_ref, bf16[4,512,384]{2,1,0:T(8,128)(2,1)} %pad_maximum_fusion.12.blocks_ref, bf16[512,576]{1,0:T(8,128)(2,1)S(1)} %copy.72.grads_ref, f32[512,576]{1,0:T(8,128)S(1)} %copy-done.4, ...), custom_call_target="tpu_custom_call" | custom-call | flops 6039797760 | bytes 8388608 | tf_op jit(solution)/shard_map/pallas_call | solution.py:691
  393.1 2.4 collective-permute-start.48
  403.7 5.6 collective-permute-start.64
  411.2 3.4 collective-permute-start.65
  416.1 4.4 collective-permute-start.49
  420.5 9.7 %collective-permute-done.52 = bf16[144,3072]{1,0:T(8,128)(2,1)S(1)} collective-permute-done((bf16[144,3072]{1,0:T(8,128)(2,1)S(1)}, bf16[144,3072]{1,0:T(8,128)(2,1)S(1)}, u32[]{:S(2)}, u32[]{:S(2)}) %collective-permute-start.52) | collective-permute-done | bytes 884768 | tf_op jit(solution)/shard_map/ppermute | solution.py:425
  430.6 8.0 %collective-permute-done.49 = bf16[512,384]{1,0:T(8,128)(2,1)S(1)} collective-permute-done((bf16[512,384]{1,0:T(8,128)(2,1)S(1)}, bf16[512,384]{1,0:T(8,128)(2,1)S(1)}, u32[]{:S(2)}, u32[]{:S(2)}) %collective-permute-start.49) | collective-permute-done | bytes 393248 | tf_op jit(solution)/shard_map/ppermute | solution.py:425
  445.3 3.2 convolution_convert_fusion.4
  451.4 2.6 collective-permute-start.87
  456.9 5.4 concatenate.227
  464.6 3.3 collective-permute-start.62
  474.0 3.3 collective-permute-done.90
  478.5 4.7 collective-permute-done.80
  483.9 5.9 %collective-permute-done.81 = bf16[144,768]{1,0:T(8,128)(2,1)S(1)} collective-permute-done((bf16[144,768]{1,0:T(8,128)(2,1)S(1)}, bf16[144,768]{1,0:T(8,128)(2,1)S(1)}, u32[]{:S(2)}, u32[]{:S(2)}) %collective-permute-start.81) | collective-permute-done | bytes 221216 | tf_op jit(solution)/shard_map/ppermute | solution.py:425
  493.1 3.2 collective-permute-start.71
  497.8 10.4 %collective-permute-done.66 = bf16[256,576]{0,1:T(8,128)(2,1)S(1)} collective-permute-done((bf16[256,576]{0,1:T(8,128)(2,1)S(1)}, bf16[256,576]{0,1:T(8,128)(2,1)S(1)}, u32[]{:S(2)}, u32[]{:S(2)}) %collective-permute-start.66) | collective-permute-done | bytes 294944 | tf_op jit(solution)/shard_map/ppermute | solution.py:509
  508.2 6.5 %collective-permute-done.67 = bf16[256,576]{0,1:T(8,128)(2,1)S(1)} collective-permute-done((bf16[256,576]{0,1:T(8,128)(2,1)S(1)}, bf16[256,576]{0,1:T(8,128)(2,1)S(1)}, u32[]{:S(2)}, u32[]{:S(2)}) %collective-permute-start.67) | collective-permute-done | bytes 294944 | tf_op jit(solution)/shard_map/ppermute | solution.py:509
  519.9 5.7 collective-permute-done.83
  529.3 3.8 collective-permute-done.72
  537.1 10.5 %collective-permute-done.85 = bf16[144,768]{1,0:T(8,128)(2,1)S(1)} collective-permute-done((bf16[144,768]{1,0:T(8,128)(2,1)S(1)}, bf16[144,768]{1,0:T(8,128)(2,1)S(1)}, u32[]{:S(2)}, u32[]{:S(2)}) %collective-permute-start.85) | collective-permute-done | bytes 221216 | tf_op jit(solution)/shard_map/ppermute | solution.py:425
  549.1 7.2 %collective-permute-done.74 = bf16[144,512]{1,0:T(8,128)(2,1)S(1)} collective-permute-done((bf16[144,512]{1,0:T(8,128)(2,1)S(1)}, bf16[144,512]{1,0:T(8,128)(2,1)S(1)}, u32[]{:S(2)}, u32[]{:S(2)}) %collective-permute-start.74) | collective-permute-done | bytes 147488 | tf_op jit(solution)/shard_map/ppermute | solution.py:425
  557.9 5.6 collective-permute-done.76
  564.2 3.7 collective-permute-start.78
  570.5 10.2 %collective-permute-done.78 = bf16[144,512]{1,0:T(8,128)(2,1)S(1)} collective-permute-done((bf16[144,512]{1,0:T(8,128)(2,1)S(1)}, bf16[144,512]{1,0:T(8,128)(2,1)S(1)}, u32[]{:S(2)}, u32[]{:S(2)}) %collective-permute-start.78) | collective-permute-done | bytes 147488 | tf_op jit(solution)/shard_map/ppermute | solution.py:425
  (500 shorter events, 193.9 us)
Async XLA Ops:
  3.8 11.9 %collective-permute-start.4 = (bf16[144,1538]{1,0:T(8,128)(2,1)S(1)}, bf16[144,1538]{1,0:T(8,128)(2,1)S(1)}, u32[]{:S(2)}, u32[]{:S(2)}) collective-permute-start(bf16[144,1538]{1,0:T(8,128)(2,1)S(1)} %concatenate.191), channel_id=1, source_target_pairs={{0,16},{16,0},{1,17},{17,1},{2,18},{18,2},{3,19},{19,3},{4,20},{20... | collective-permute-start | bytes 1328840 | tf_op jit(solution)/shard_map/ppermute | solution.py:425
  6.1 15.7 %collective-permute-start = (bf16[256,576]{0,1:T(8,128)(2,1)}, bf16[256,576]{0,1:T(8,128)(2,1)}, u32[]{:S(2)}, u32[]{:S(2)}) collective-permute-start(bf16[256,576]{0,1:T(8,128)(2,1)} %get-tuple-element.181), channel_id=1, source_target_pairs={{0,17},{1,19},{2,18},{3,16},{16,1},{17,3},{18,2},{19,0},{4,21},{5,... | collective-permute-start | bytes 884744 | tf_op jit(solution)/shard_map/ppermute | solution.py:491
  6.6 22.9 %collective-permute-start.1 = (bf16[256,576]{0,1:T(8,128)(2,1)}, bf16[256,576]{0,1:T(8,128)(2,1)}, u32[]{:S(2)}, u32[]{:S(2)}) collective-permute-start(bf16[256,576]{0,1:T(8,128)(2,1)} %get-tuple-element.184), channel_id=1, source_target_pairs={{0,16},{1,18},{2,19},{3,17},{16,0},{17,2},{18,3},{19,1},{4,20},{5,... | collective-permute-start | bytes 884744 | tf_op jit(solution)/shard_map/ppermute | solution.py:491
  8.4 27.9 %collective-permute-start.2 = (bf16[256,576]{0,1:T(8,128)(2,1)}, bf16[256,576]{0,1:T(8,128)(2,1)S(1)}, u32[]{:S(2)}, u32[]{:S(2)}) collective-permute-start(bf16[256,576]{0,1:T(8,128)(2,1)} %get-tuple-element.182), channel_id=1, source_target_pairs={{0,1},{1,3},{2,2},{3,0},{16,17},{17,19},{18,18},{19,16},{4,5},{5,7... | collective-permute-start | bytes 884744 | tf_op jit(solution)/shard_map/ppermute | solution.py:491
  10.3 26.0 %collective-permute-start.3 = (bf16[256,576]{0,1:T(8,128)(2,1)}, bf16[256,576]{0,1:T(8,128)(2,1)S(1)}, u32[]{:S(2)}, u32[]{:S(2)}) collective-permute-start(bf16[256,576]{0,1:T(8,128)(2,1)} %get-tuple-element.183), channel_id=1, source_target_pairs={{0,0},{1,2},{2,3},{3,1},{16,16},{17,18},{18,19},{19,17},{4,4},{5,6... | collective-permute-start | bytes 884744 | tf_op jit(solution)/shard_map/ppermute | solution.py:491
  16.6 19.4 %collective-permute-start.5 = (bf16[144,1538]{1,0:T(8,128)(2,1)}, bf16[144,1538]{1,0:T(8,128)(2,1)}, u32[]{:S(2)}, u32[]{:S(2)}) collective-permute-start(bf16[144,1538]{1,0:T(8,128)(2,1)} %broadcast_select_fusion.21), channel_id=1, source_target_pairs={{0,2},{1,3},{2,0},{3,1},{4,6},{5,7},{6,4},{7,5},{8,10},{9,11},{10,... | collective-permute-start | bytes 1328840 | tf_op jit(solution)/shard_map/ppermute | solution.py:425
  36.7 33.6 %collective-permute-start.8 = (bf16[144,3072]{1,0:T(8,128)(2,1)S(1)}, bf16[144,3072]{1,0:T(8,128)(2,1)S(1)}, u32[]{:S(2)}, u32[]{:S(2)}) collective-permute-start(bf16[144,3072]{1,0:T(8,128)(2,1)S(1)} %pad_maximum_fusion.16), channel_id=1, source_target_pairs={{0,16},{16,0},{1,17},{17,1},{2,18},{18,2},{3,19},{19,3},{4,20},{20... | collective-permute-start | bytes 2654216 | tf_op jit(solution)/shard_map/ppermute | solution.py:425
  37.3 30.1 %collective-permute-start.9 = (bf16[384,576]{0,1:T(8,128)(2,1)}, bf16[384,576]{0,1:T(8,128)(2,1)}, u32[]{:S(2)}, u32[]{:S(2)}) collective-permute-start(bf16[384,576]{0,1:T(8,128)(2,1)} %bitcast.13), channel_id=1, source_target_pairs={{0,16},{16,0},{1,17},{17,1},{2,18},{18,2},{3,19},{19,3},{4,20},{20... | collective-permute-start | bytes 1327112 | tf_op jit(solution)/shard_map/ppermute | solution.py:425
  46.6 23.7 %collective-permute-start.11 = (bf16[512,384]{1,0:T(8,128)(2,1)S(1)}, bf16[512,384]{1,0:T(8,128)(2,1)S(1)}, u32[]{:S(2)}, u32[]{:S(2)}) collective-permute-start(bf16[512,384]{1,0:T(8,128)(2,1)S(1)} %pad_maximum_fusion.29), channel_id=1, source_target_pairs={{0,2},{1,3},{2,0},{3,1},{4,6},{5,7},{6,4},{7,5},{8,10},{9,11},{10,... | collective-permute-start | bytes 1179656 | tf_op jit(solution)/shard_map/ppermute | solution.py:425
  73.6 31.9 %collective-permute-start.13 = (bf16[144,3072]{1,0:T(8,128)(2,1)}, bf16[144,3072]{1,0:T(8,128)(2,1)}, u32[]{:S(2)}, u32[]{:S(2)}) collective-permute-start(bf16[144,3072]{1,0:T(8,128)(2,1)} %broadcast_select_fusion.17), channel_id=1, source_target_pairs={{0,2},{1,3},{2,0},{3,1},{4,6},{5,7},{6,4},{7,5},{8,10},{9,11},{10,... | collective-permute-start | bytes 2654216 | tf_op jit(solution)/shard_map/ppermute | solution.py:425
  74.0 30.2 %collective-permute-start.16 = (bf16[384,576]{0,1:T(8,128)(2,1)}, bf16[384,576]{0,1:T(8,128)(2,1)}, u32[]{:S(2)}, u32[]{:S(2)}) collective-permute-start(bf16[384,576]{0,1:T(8,128)(2,1)} %broadcast_select_fusion.55), channel_id=1, source_target_pairs={{0,2},{1,3},{2,0},{3,1},{4,6},{5,7},{6,4},{7,5},{8,10},{9,11},{10,... | collective-permute-start | bytes 1327112 | tf_op jit(solution)/shard_map/ppermute | solution.py:425
  75.6 32.2 %collective-permute-start.18 = (bf16[384,576]{0,1:T(8,128)(2,1)}, bf16[384,576]{0,1:T(8,128)(2,1)S(1)}, u32[]{:S(2)}, u32[]{:S(2)}) collective-permute-start(bf16[384,576]{0,1:T(8,128)(2,1)} %broadcast_select_fusion.55), channel_id=1, source_target_pairs={{0,1},{1,0},{2,3},{3,2},{4,5},{5,4},{6,7},{7,6},{8,9},{9,8},{10,11... | collective-permute-start | bytes 1327112 | tf_op jit(solution)/shard_map/ppermute | solution.py:425
  76.6 33.2 %collective-permute-start.15 = (bf16[144,3072]{1,0:T(8,128)(2,1)}, bf16[144,3072]{1,0:T(8,128)(2,1)S(1)}, u32[]{:S(2)}, u32[]{:S(2)}) collective-permute-start(bf16[144,3072]{1,0:T(8,128)(2,1)} %broadcast_select_fusion.17), channel_id=1, source_target_pairs={{0,1},{1,0},{2,3},{3,2},{4,5},{5,4},{6,7},{7,6},{8,9},{9,8},{10,11... | collective-permute-start | bytes 2654216 | tf_op jit(solution)/shard_map/ppermute | solution.py:425
  115.0 25.2 %collective-permute-start.25 = (bf16[384,576]{0,1:T(8,128)(2,1)}, bf16[384,576]{0,1:T(8,128)(2,1)}, u32[]{:S(2)}, u32[]{:S(2)}) collective-permute-start(bf16[384,576]{0,1:T(8,128)(2,1)} %broadcast_select_fusion.38), channel_id=1, source_target_pairs={{0,2},{1,3},{2,0},{3,1},{4,6},{5,7},{6,4},{7,5},{8,10},{9,11},{10,... | collective-permute-start | bytes 1327112 | tf_op jit(solution)/shard_map/ppermute | solution.py:425
  115.5 42.6 %collective-permute-start.27 = (bf16[384,576]{0,1:T(8,128)(2,1)}, bf16[384,576]{0,1:T(8,128)(2,1)}, u32[]{:S(2)}, u32[]{:S(2)}) collective-permute-start(bf16[384,576]{0,1:T(8,128)(2,1)} %broadcast_select_fusion.38), channel_id=1, source_target_pairs={{0,1},{1,0},{2,3},{3,2},{4,5},{5,4},{6,7},{7,6},{8,9},{9,8},{10,11... | collective-permute-start | bytes 1327112 | tf_op jit(solution)/shard_map/ppermute | solution.py:425
  116.3 20.4 %collective-permute-start.19 = (bf16[144,1538]{1,0:T(8,128)(2,1)S(1)}, bf16[144,1538]{1,0:T(8,128)(2,1)S(1)}, u32[]{:S(2)}, u32[]{:S(2)}) collective-permute-start(bf16[144,1538]{1,0:T(8,128)(2,1)S(1)} %broadcast_select_fusion.20), channel_id=1, source_target_pairs={{0,2},{1,3},{2,0},{3,1},{4,6},{5,7},{6,4},{7,5},{8,10},{9,11},{10,... | collective-permute-start | bytes 1328840 | tf_op jit(solution)/shard_map/ppermute | solution.py:425
  117.4 22.9 %collective-permute-start.21 = (bf16[144,1538]{1,0:T(8,128)(2,1)S(1)}, bf16[144,1538]{1,0:T(8,128)(2,1)S(1)}, u32[]{:S(2)}, u32[]{:S(2)}) collective-permute-start(bf16[144,1538]{1,0:T(8,128)(2,1)S(1)} %broadcast_select_fusion.20), channel_id=1, source_target_pairs={{0,1},{1,0},{2,3},{3,2},{4,5},{5,4},{6,7},{7,6},{8,9},{9,8},{10,11... | collective-permute-start | bytes 1328840 | tf_op jit(solution)/shard_map/ppermute | solution.py:425
  118.7 37.1 %collective-permute-start.28 = (bf16[144,3072]{1,0:T(8,128)(2,1)}, bf16[144,3072]{1,0:T(8,128)(2,1)}, u32[]{:S(2)}, u32[]{:S(2)}) collective-permute-start(bf16[144,3072]{1,0:T(8,128)(2,1)} %broadcast_select_fusion), channel_id=1, source_target_pairs={{0,2},{1,3},{2,0},{3,1},{4,6},{5,7},{6,4},{7,5},{8,10},{9,11},{10,... | collective-permute-start | bytes 2654216 | tf_op jit(solution)/shard_map/ppermute | solution.py:425
  140.2 17.9 %collective-permute-start.26 = (bf16[384,576]{0,1:T(8,128)(2,1)}, bf16[384,576]{0,1:T(8,128)(2,1)}, u32[]{:S(2)}, u32[]{:S(2)}) collective-permute-start(bf16[384,576]{0,1:T(8,128)(2,1)} %collective-permute-done.25), channel_id=1, source_target_pairs={{0,1},{1,0},{2,3},{3,2},{4,5},{5,4},{6,7},{7,6},{8,9},{9,8},{10,11... | collective-permute-start | bytes 1327112 | tf_op jit(solution)/shard_map/ppermute | solution.py:425
  145.2 19.0 %collective-permute-start.23 = (bf16[512,384]{1,0:T(8,128)(2,1)}, bf16[512,384]{1,0:T(8,128)(2,1)}, u32[]{:S(2)}, u32[]{:S(2)}) collective-permute-start(bf16[512,384]{1,0:T(8,128)(2,1)} %pad_maximum_fusion.30), channel_id=1, source_target_pairs={{0,2},{1,3},{2,0},{3,1},{4,6},{5,7},{6,4},{7,5},{8,10},{9,11},{10,... | collective-permute-start | bytes 1179656 | tf_op jit(solution)/shard_map/ppermute | solution.py:425
  146.6 40.9 %collective-permute-start.30 = (bf16[144,3072]{1,0:T(8,128)(2,1)}, bf16[144,3072]{1,0:T(8,128)(2,1)}, u32[]{:S(2)}, u32[]{:S(2)}) collective-permute-start(bf16[144,3072]{1,0:T(8,128)(2,1)} %broadcast_select_fusion), channel_id=1, source_target_pairs={{0,1},{1,0},{2,3},{3,2},{4,5},{5,4},{6,7},{7,6},{8,9},{9,8},{10,11... | collective-permute-start | bytes 2654216 | tf_op jit(solution)/shard_map/ppermute | solution.py:425
  155.8 31.7 %collective-permute-start.29 = (bf16[144,3072]{1,0:T(8,128)(2,1)}, bf16[144,3072]{1,0:T(8,128)(2,1)}, u32[]{:S(2)}, u32[]{:S(2)}) collective-permute-start(bf16[144,3072]{1,0:T(8,128)(2,1)} %collective-permute-done.28), channel_id=1, source_target_pairs={{0,1},{1,0},{2,3},{3,2},{4,5},{5,4},{6,7},{7,6},{8,9},{9,8},{10,11... | collective-permute-start | bytes 2654216 | tf_op jit(solution)/shard_map/ppermute | solution.py:425
  243.3 45.9 %collective-permute-start.33 = (bf16[144,3072]{1,0:T(8,128)(2,1)}, bf16[144,3072]{1,0:T(8,128)(2,1)}, u32[]{:S(2)}, u32[]{:S(2)}) collective-permute-start(bf16[144,3072]{1,0:T(8,128)(2,1)} %get-tuple-element.137), channel_id=1, source_target_pairs={{0,1},{1,0},{2,3},{3,2},{4,5},{5,4},{6,7},{7,6},{8,9},{9,8},{10,11... | collective-permute-start | bytes 2654216 | tf_op jit(solution)/shard_map/ppermute | solution.py:425
  248.7 18.8 %collective-permute-start.32 = (bf16[512,384]{1,0:T(8,128)(2,1)S(1)}, bf16[512,384]{1,0:T(8,128)(2,1)S(1)}, u32[]{:S(2)}, u32[]{:S(2)}) collective-permute-start(bf16[512,384]{1,0:T(8,128)(2,1)S(1)} %fusion.43), channel_id=1, source_target_pairs={{0,2},{1,3},{2,0},{3,1},{4,6},{5,7},{6,4},{7,5},{8,10},{9,11},{10,... | collective-permute-start | bytes 1179656 | tf_op jit(solution)/shard_map/ppermute | solution.py:425
  250.2 39.1 %collective-permute-start.35 = (bf16[144,3072]{1,0:T(8,128)(2,1)}, bf16[144,3072]{1,0:T(8,128)(2,1)}, u32[]{:S(2)}, u32[]{:S(2)}) collective-permute-start(bf16[144,3072]{1,0:T(8,128)(2,1)} %add_convert_fusion.4), channel_id=1, source_target_pairs={{0,2},{1,3},{2,0},{3,1},{4,6},{5,7},{6,4},{7,5},{8,10},{9,11},{10,... | collective-permute-start | bytes 2654216 | tf_op jit(solution)/shard_map/ppermute | solution.py:425
  287.3 23.8 %collective-permute-start.46 = (bf16[144,2048]{1,0:T(8,128)(2,1)S(1)}, bf16[144,2048]{1,0:T(8,128)(2,1)S(1)}, u32[]{:S(2)}, u32[]{:S(2)}) collective-permute-start(bf16[144,2048]{1,0:T(8,128)(2,1)S(1)} %get-tuple-element.150), channel_id=1, source_target_pairs={{0,1},{1,0},{2,3},{3,2},{4,5},{5,4},{6,7},{7,6},{8,9},{9,8},{10,11... | collective-permute-start | bytes 1769480 | tf_op jit(solution)/shard_map/ppermute | solution.py:425
  288.8 50.3 %collective-permute-start.45 = (bf16[144,2048]{1,0:T(8,128)(2,1)S(1)}, bf16[144,2048]{1,0:T(8,128)(2,1)S(1)}, u32[]{:S(2)}, u32[]{:S(2)}) collective-permute-start(bf16[144,2048]{1,0:T(8,128)(2,1)S(1)} %get-tuple-element.149), channel_id=1, source_target_pairs={{0,1},{1,0},{2,3},{3,2},{4,5},{5,4},{6,7},{7,6},{8,9},{9,8},{10,11... | collective-permute-start | bytes 1769480 | tf_op jit(solution)/shard_map/ppermute | solution.py:425
  312.3 22.4 %collective-permute-start.40 = (bf16[144,768]{1,0:T(8,128)(2,1)S(1)}, bf16[144,768]{1,0:T(8,128)(2,1)S(1)}, u32[]{:S(2)}, u32[]{:S(2)}) collective-permute-start(bf16[144,768]{1,0:T(8,128)(2,1)S(1)} %get-tuple-element.194), channel_id=1, source_target_pairs={{0,8},{4,12},{8,0},{12,4},{1,9},{5,13},{9,1},{13,5},{2,10},{6,14},... | collective-permute-start | bytes 663560 | tf_op jit(solution)/shard_map/ppermute | solution.py:425
  315.0 22.4 %collective-permute-start.41 = (bf16[144,768]{1,0:T(8,128)(2,1)S(1)}, bf16[144,768]{1,0:T(8,128)(2,1)S(1)}, u32[]{:S(2)}, u32[]{:S(2)}) collective-permute-start(bf16[144,768]{1,0:T(8,128)(2,1)S(1)} %get-tuple-element.193), channel_id=1, source_target_pairs={{0,12},{4,8},{8,4},{12,0},{1,13},{5,9},{9,5},{13,1},{2,14},{6,10},... | collective-permute-start | bytes 663560 | tf_op jit(solution)/shard_map/ppermute | solution.py:425
  319.0 19.2 %collective-permute-start.54 = (bf16[384,576]{0,1:T(8,128)(2,1)S(1)}, bf16[384,576]{0,1:T(8,128)(2,1)S(1)}, u32[]{:S(2)}, u32[]{:S(2)}) collective-permute-start(bf16[384,576]{0,1:T(8,128)(2,1)S(1)} %get-tuple-element.162), channel_id=1, source_target_pairs={{0,1},{1,0},{2,3},{3,2},{4,5},{5,4},{6,7},{7,6},{8,9},{9,8},{10,11... | collective-permute-start | bytes 1327112 | tf_op jit(solution)/shard_map/ppermute | solution.py:425
  322.4 16.7 %collective-permute-start.47 = (bf16[144,2048]{1,0:T(8,128)(2,1)S(1)}, bf16[144,2048]{1,0:T(8,128)(2,1)S(1)}, u32[]{:S(2)}, u32[]{:S(2)}) collective-permute-start(bf16[144,2048]{1,0:T(8,128)(2,1)S(1)} %add_convert_fusion.10), channel_id=1, source_target_pairs={{0,2},{1,3},{2,0},{3,1},{4,6},{5,7},{6,4},{7,5},{8,10},{9,11},{10,... | collective-permute-start | bytes 1769480 | tf_op jit(solution)/shard_map/ppermute | solution.py:425
  334.7 69.0 %collective-permute-start.53 = (bf16[384,576]{0,1:T(8,128)(2,1)}, bf16[384,576]{0,1:T(8,128)(2,1)}, u32[]{:S(2)}, u32[]{:S(2)}) collective-permute-start(bf16[384,576]{0,1:T(8,128)(2,1)} %get-tuple-element.161), channel_id=1, source_target_pairs={{0,1},{1,0},{2,3},{3,2},{4,5},{5,4},{6,7},{7,6},{8,9},{9,8},{10,11... | collective-permute-start | bytes 1327112 | tf_op jit(solution)/shard_map/ppermute | solution.py:425
  337.4 59.2 %collective-permute-start.51 = (bf16[144,3072]{1,0:T(8,128)(2,1)}, bf16[144,3072]{1,0:T(8,128)(2,1)}, u32[]{:S(2)}, u32[]{:S(2)}) collective-permute-start(bf16[144,3072]{1,0:T(8,128)(2,1)} %get-tuple-element.136), channel_id=1, source_target_pairs={{0,1},{1,0},{2,3},{3,2},{4,5},{5,4},{6,7},{7,6},{8,9},{9,8},{10,11... | collective-permute-start | bytes 2654216 | tf_op jit(solution)/shard_map/ppermute | solution.py:425
  340.2 49.8 %collective-permute-start.58 = (bf16[144,512]{1,0:T(8,128)(2,1)}, bf16[144,512]{1,0:T(8,128)(2,1)}, u32[]{:S(2)}, u32[]{:S(2)}) collective-permute-start(bf16[144,512]{1,0:T(8,128)(2,1)} %get-tuple-element.212), channel_id=1, source_target_pairs={{0,4},{4,0},{8,12},{12,8},{1,5},{5,1},{9,13},{13,9},{2,6},{6,2},{1... | collective-permute-start | bytes 442376 | tf_op jit(solution)/shard_map/ppermute | solution.py:425
  347.9 43.8 %collective-permute-start.59 = (bf16[144,512]{1,0:T(8,128)(2,1)}, bf16[144,512]{1,0:T(8,128)(2,1)}, u32[]{:S(2)}, u32[]{:S(2)}) collective-permute-start(bf16[144,512]{1,0:T(8,128)(2,1)} %get-tuple-element.214), channel_id=1, source_target_pairs={{0,8},{4,12},{8,0},{12,4},{1,9},{5,13},{9,1},{13,5},{2,10},{6,14},... | collective-permute-start | bytes 442376 | tf_op jit(solution)/shard_map/ppermute | solution.py:425
  350.0 37.2 %collective-permute-start.57 = (bf16[96,576]{0,1:T(8,128)(2,1)}, bf16[96,576]{0,1:T(8,128)(2,1)}, u32[]{:S(2)}, u32[]{:S(2)}) collective-permute-start(bf16[96,576]{0,1:T(8,128)(2,1)} %add_convert_fusion.37), channel_id=1, source_target_pairs={{0,16},{1,17},{2,18},{3,19},{4,20},{5,21},{6,22},{7,23},{8,24},{9,... | collective-permute-start | bytes 331784 | tf_op jit(solution)/shard_map/ppermute | solution.py:534
  390.1 30.4 %collective-permute-start.50 = (bf16[144,3072]{1,0:T(8,128)(2,1)S(1)}, bf16[144,3072]{1,0:T(8,128)(2,1)S(1)}, u32[]{:S(2)}, u32[]{:S(2)}) collective-permute-start(bf16[144,3072]{1,0:T(8,128)(2,1)S(1)} %copy-done.63), channel_id=1, source_target_pairs={{0,1},{1,0},{2,3},{3,2},{4,5},{5,4},{6,7},{7,6},{8,9},{9,8},{10,11... | collective-permute-start | bytes 2654216 | tf_op jit(solution)/shard_map/ppermute | solution.py:425
  393.1 22.9 %collective-permute-start.48 = (bf16[2,512,384]{2,1,0:T(8,128)(2,1)}, bf16[2,512,384]{2,1,0:T(8,128)(2,1)S(1)}, u32[]{:S(2)}, u32[]{:S(2)}) collective-permute-start(bf16[2,512,384]{2,1,0:T(8,128)(2,1)} %slice.252), channel_id=1, source_target_pairs={{0,1},{1,0},{2,3},{3,2},{4,5},{5,4},{6,7},{7,6},{8,9},{9,8},{10,11... | collective-permute-start | bytes 2359304 | tf_op jit(solution)/shard_map/ppermute | solution.py:425
  399.4 11.9 %collective-permute-start.55 = (bf16[384,576]{0,1:T(8,128)(2,1)S(1)}, bf16[384,576]{0,1:T(8,128)(2,1)S(1)}, u32[]{:S(2)}, u32[]{:S(2)}) collective-permute-start(bf16[384,576]{0,1:T(8,128)(2,1)S(1)} %copy-done.76), channel_id=1, source_target_pairs={{0,2},{1,3},{2,0},{3,1},{4,6},{5,7},{6,4},{7,5},{8,10},{9,11},{10,... | collective-permute-start | bytes 1327112 | tf_op jit(solution)/shard_map/ppermute | solution.py:425
  401.4 28.8 %collective-permute-start.52 = (bf16[144,3072]{1,0:T(8,128)(2,1)S(1)}, bf16[144,3072]{1,0:T(8,128)(2,1)S(1)}, u32[]{:S(2)}, u32[]{:S(2)}) collective-permute-start(bf16[144,3072]{1,0:T(8,128)(2,1)S(1)} %add_convert_fusion.1), channel_id=1, source_target_pairs={{0,2},{1,3},{2,0},{3,1},{4,6},{5,7},{6,4},{7,5},{8,10},{9,11},{10,... | collective-permute-start | bytes 2654216 | tf_op jit(solution)/shard_map/ppermute | solution.py:425
  403.7 68.8 %collective-permute-start.64 = (bf16[256,576]{0,1:T(8,128)(2,1)}, bf16[256,576]{0,1:T(8,128)(2,1)}, u32[]{:S(2)}, u32[]{:S(2)}) collective-permute-start(bf16[256,576]{0,1:T(8,128)(2,1)} %get-tuple-element.208), channel_id=1, source_target_pairs={{0,16},{2,17},{3,18},{1,19},{4,20},{6,21},{7,22},{5,23},{8,24},{10... | collective-permute-start | bytes 884744 | tf_op jit(solution)/shard_map/ppermute | solution.py:509
  411.2 62.1 %collective-permute-start.65 = (bf16[256,576]{0,1:T(8,128)(2,1)}, bf16[256,576]{0,1:T(8,128)(2,1)}, u32[]{:S(2)}, u32[]{:S(2)}) collective-permute-start(bf16[256,576]{0,1:T(8,128)(2,1)} %get-tuple-element.209), channel_id=1, source_target_pairs={{1,16},{3,17},{2,18},{0,19},{5,20},{7,21},{6,22},{4,23},{9,24},{11... | collective-permute-start | bytes 884744 | tf_op jit(solution)/shard_map/ppermute | solution.py:509
  416.1 22.5 %collective-permute-start.49 = (bf16[512,384]{1,0:T(8,128)(2,1)S(1)}, bf16[512,384]{1,0:T(8,128)(2,1)S(1)}, u32[]{:S(2)}, u32[]{:S(2)}) collective-permute-start(bf16[512,384]{1,0:T(8,128)(2,1)S(1)} %fusion.45), channel_id=1, source_target_pairs={{0,2},{1,3},{2,0},{3,1},{4,6},{5,7},{6,4},{7,5},{8,10},{9,11},{10,... | collective-permute-start | bytes 1179656 | tf_op jit(solution)/shard_map/ppermute | solution.py:425
  451.4 13.2 %collective-permute-start.87 = (bf16[96,576]{0,1:T(8,128)(2,1)}, bf16[96,576]{0,1:T(8,128)(2,1)}, u32[]{:S(2)}, u32[]{:S(2)}) collective-permute-start(bf16[96,576]{0,1:T(8,128)(2,1)} %get-tuple-element.227), channel_id=1, source_target_pairs={{0,4},{4,0},{8,12},{12,8},{1,5},{5,1},{9,13},{13,9},{2,6},{6,2},{1... | collective-permute-start | bytes 331784 | tf_op jit(solution)/shard_map/ppermute | solution.py:425
  454.0 13.8 %collective-permute-start.88 = (bf16[96,576]{0,1:T(8,128)(2,1)}, bf16[96,576]{0,1:T(8,128)(2,1)}, u32[]{:S(2)}, u32[]{:S(2)}) collective-permute-start(bf16[96,576]{0,1:T(8,128)(2,1)} %get-tuple-element.229), channel_id=1, source_target_pairs={{0,8},{4,12},{8,0},{12,4},{1,9},{5,13},{9,1},{13,5},{2,10},{6,14},... | collective-permute-start | bytes 331784 | tf_op jit(solution)/shard_map/ppermute | solution.py:425
  454.0 15.9 %collective-permute-start.89 = (bf16[96,576]{0,1:T(8,128)(2,1)}, bf16[96,576]{0,1:T(8,128)(2,1)}, u32[]{:S(2)}, u32[]{:S(2)}) collective-permute-start(bf16[96,576]{0,1:T(8,128)(2,1)} %get-tuple-element.228), channel_id=1, source_target_pairs={{0,12},{4,8},{8,4},{12,0},{1,13},{5,9},{9,5},{13,1},{2,14},{6,10},... | collective-permute-start | bytes 331784 | tf_op jit(solution)/shard_map/ppermute | solution.py:425
  464.6 27.2 %collective-permute-start.62 = (bf16[256,576]{0,1:T(8,128)(2,1)S(1)}, bf16[256,576]{0,1:T(8,128)(2,1)S(1)}, u32[]{:S(2)}, u32[]{:S(2)}) collective-permute-start(bf16[256,576]{0,1:T(8,128)(2,1)S(1)} %get-tuple-element.210), channel_id=1, source_target_pairs={{0,0},{2,1},{3,2},{1,3},{4,4},{6,5},{7,6},{5,7},{8,8},{10,9},{11,1... | collective-permute-start | bytes 884744 | tf_op jit(solution)/shard_map/ppermute | solution.py:509
  467.8 25.3 %collective-permute-start.63 = (bf16[256,576]{0,1:T(8,128)(2,1)S(1)}, bf16[256,576]{0,1:T(8,128)(2,1)S(1)}, u32[]{:S(2)}, u32[]{:S(2)}) collective-permute-start(bf16[256,576]{0,1:T(8,128)(2,1)S(1)} %get-tuple-element.211), channel_id=1, source_target_pairs={{1,0},{3,1},{2,2},{0,3},{5,4},{7,5},{6,6},{4,7},{9,8},{11,9},{10,1... | collective-permute-start | bytes 884744 | tf_op jit(solution)/shard_map/ppermute | solution.py:509
  473.3 16.5 %collective-permute-start.81 = (bf16[144,768]{1,0:T(8,128)(2,1)S(1)}, bf16[144,768]{1,0:T(8,128)(2,1)S(1)}, u32[]{:S(2)}, u32[]{:S(2)}) collective-permute-start(bf16[144,768]{1,0:T(8,128)(2,1)S(1)} %get-tuple-element.191), channel_id=1, source_target_pairs={{0,8},{4,12},{8,0},{12,4},{1,9},{5,13},{9,1},{13,5},{2,10},{6,14},... | collective-permute-start | bytes 663560 | tf_op jit(solution)/shard_map/ppermute | solution.py:425
  477.3 13.2 %collective-permute-start.82 = (bf16[144,768]{1,0:T(8,128)(2,1)S(1)}, bf16[144,768]{1,0:T(8,128)(2,1)S(1)}, u32[]{:S(2)}, u32[]{:S(2)}) collective-permute-start(bf16[144,768]{1,0:T(8,128)(2,1)S(1)} %get-tuple-element.190), channel_id=1, source_target_pairs={{0,12},{4,8},{8,4},{12,0},{1,13},{5,9},{9,5},{13,1},{2,14},{6,10},... | collective-permute-start | bytes 663560 | tf_op jit(solution)/shard_map/ppermute | solution.py:425
  483.2 14.4 %collective-permute-start.68 = (bf16[256,576]{0,1:T(8,128)(2,1)}, bf16[256,576]{0,1:T(8,128)(2,1)S(1)}, u32[]{:S(2)}, u32[]{:S(2)}) collective-permute-start(bf16[256,576]{0,1:T(8,128)(2,1)} %get-tuple-element.208), channel_id=1, source_target_pairs={{16,16},{18,17},{19,18},{17,19},{20,20},{22,21},{23,22},{21,23},{2... | collective-permute-start | bytes 884744 | tf_op jit(solution)/shard_map/ppermute | solution.py:509
  490.5 17.7 %collective-permute-start.66 = (bf16[256,576]{0,1:T(8,128)(2,1)S(1)}, bf16[256,576]{0,1:T(8,128)(2,1)S(1)}, u32[]{:S(2)}, u32[]{:S(2)}) collective-permute-start(bf16[256,576]{0,1:T(8,128)(2,1)S(1)} %get-tuple-element.210), channel_id=1, source_target_pairs={{16,0},{18,1},{19,2},{17,3},{20,4},{22,5},{23,6},{21,7},{24,8},{26... | collective-permute-start | bytes 884744 | tf_op jit(solution)/shard_map/ppermute | solution.py:509
  491.8 22.9 %collective-permute-start.67 = (bf16[256,576]{0,1:T(8,128)(2,1)S(1)}, bf16[256,576]{0,1:T(8,128)(2,1)S(1)}, u32[]{:S(2)}, u32[]{:S(2)}) collective-permute-start(bf16[256,576]{0,1:T(8,128)(2,1)S(1)} %get-tuple-element.211), channel_id=1, source_target_pairs={{17,0},{19,1},{18,2},{16,3},{21,4},{23,5},{22,6},{20,7},{25,8},{27... | collective-permute-start | bytes 884744 | tf_op jit(solution)/shard_map/ppermute | solution.py:509
  493.1 23.3 %collective-permute-start.71 = (bf16[144,2048]{1,0:T(8,128)(2,1)S(1)}, bf16[144,2048]{1,0:T(8,128)(2,1)S(1)}, u32[]{:S(2)}, u32[]{:S(2)}) collective-permute-start(bf16[144,2048]{1,0:T(8,128)(2,1)S(1)} %get-tuple-element.148), channel_id=1, source_target_pairs={{0,1},{1,0},{2,3},{3,2},{4,5},{5,4},{6,7},{7,6},{8,9},{9,8},{10,11... | collective-permute-start | bytes 1769480 | tf_op jit(solution)/shard_map/ppermute | solution.py:425
  497.6 31.7 %collective-permute-start.70 = (bf16[144,2048]{1,0:T(8,128)(2,1)S(1)}, bf16[144,2048]{1,0:T(8,128)(2,1)S(1)}, u32[]{:S(2)}, u32[]{:S(2)}) collective-permute-start(bf16[144,2048]{1,0:T(8,128)(2,1)S(1)} %get-tuple-element.147), channel_id=1, source_target_pairs={{0,1},{1,0},{2,3},{3,2},{4,5},{5,4},{6,7},{7,6},{8,9},{9,8},{10,11... | collective-permute-start | bytes 1769480 | tf_op jit(solution)/shard_map/ppermute | solution.py:425
  497.7 20.1 %collective-permute-start.91 = (bf16[96,576]{0,1:T(8,128)(2,1)S(1)}, bf16[96,576]{0,1:T(8,128)(2,1)S(1)}, u32[]{:S(2)}, u32[]{:S(2)}) collective-permute-start(bf16[96,576]{0,1:T(8,128)(2,1)S(1)} %fusion.57), channel_id=1, source_target_pairs={{0,12},{4,8},{8,4},{12,0},{1,13},{5,9},{9,5},{13,1},{2,14},{6,10},... | collective-permute-start | bytes 331784 | tf_op jit(solution)/shard_map/ppermute | solution.py:425
  517.9 15.3 %collective-permute-start.72 = (bf16[144,2048]{1,0:T(8,128)(2,1)S(1)}, bf16[144,2048]{1,0:T(8,128)(2,1)S(1)}, u32[]{:S(2)}, u32[]{:S(2)}) collective-permute-start(bf16[144,2048]{1,0:T(8,128)(2,1)S(1)} %add_convert_fusion.7), channel_id=1, source_target_pairs={{0,2},{1,3},{2,0},{3,1},{4,6},{5,7},{6,4},{7,5},{8,10},{9,11},{10,... | collective-permute-start | bytes 1769480 | tf_op jit(solution)/shard_map/ppermute | solution.py:425
  527.2 20.4 %collective-permute-start.85 = (bf16[144,768]{1,0:T(8,128)(2,1)S(1)}, bf16[144,768]{1,0:T(8,128)(2,1)S(1)}, u32[]{:S(2)}, u32[]{:S(2)}) collective-permute-start(bf16[144,768]{1,0:T(8,128)(2,1)S(1)} %fusion.51), channel_id=1, source_target_pairs={{0,8},{4,12},{8,0},{12,4},{1,9},{5,13},{9,1},{13,5},{2,10},{6,14},... | collective-permute-start | bytes 663560 | tf_op jit(solution)/shard_map/ppermute | solution.py:425
  527.2 20.4 %collective-permute-start.86 = (bf16[144,768]{1,0:T(8,128)(2,1)S(1)}, bf16[144,768]{1,0:T(8,128)(2,1)S(1)}, u32[]{:S(2)}, u32[]{:S(2)}) collective-permute-start(bf16[144,768]{1,0:T(8,128)(2,1)S(1)} %fusion.51), channel_id=1, source_target_pairs={{0,4},{4,0},{8,12},{12,8},{1,5},{5,1},{9,13},{13,9},{2,6},{6,2},{1... | collective-permute-start | bytes 663560 | tf_op jit(solution)/shard_map/ppermute | solution.py:425
  533.5 15.6 %collective-permute-start.73 = (bf16[144,512]{1,0:T(8,128)(2,1)S(1)}, bf16[144,512]{1,0:T(8,128)(2,1)S(1)}, u32[]{:S(2)}, u32[]{:S(2)}) collective-permute-start(bf16[144,512]{1,0:T(8,128)(2,1)S(1)} %get-tuple-element.205), channel_id=1, source_target_pairs={{0,4},{4,0},{8,12},{12,8},{1,5},{5,1},{9,13},{13,9},{2,6},{6,2},{1... | collective-permute-start | bytes 442376 | tf_op jit(solution)/shard_map/ppermute | solution.py:425
  534.9 21.4 %collective-permute-start.74 = (bf16[144,512]{1,0:T(8,128)(2,1)S(1)}, bf16[144,512]{1,0:T(8,128)(2,1)S(1)}, u32[]{:S(2)}, u32[]{:S(2)}) collective-permute-start(bf16[144,512]{1,0:T(8,128)(2,1)S(1)} %get-tuple-element.207), channel_id=1, source_target_pairs={{0,8},{4,12},{8,0},{12,4},{1,9},{5,13},{9,1},{13,5},{2,10},{6,14},... | collective-permute-start | bytes 442376 | tf_op jit(solution)/shard_map/ppermute | solution.py:425
  535.3 21.1 %collective-permute-start.75 = (bf16[144,512]{1,0:T(8,128)(2,1)S(1)}, bf16[144,512]{1,0:T(8,128)(2,1)S(1)}, u32[]{:S(2)}, u32[]{:S(2)}) collective-permute-start(bf16[144,512]{1,0:T(8,128)(2,1)S(1)} %get-tuple-element.206), channel_id=1, source_target_pairs={{0,12},{4,8},{8,4},{12,0},{1,13},{5,9},{9,5},{13,1},{2,14},{6,10},... | collective-permute-start | bytes 442376 | tf_op jit(solution)/shard_map/ppermute | solution.py:425
  564.2 16.5 %collective-permute-start.78 = (bf16[144,512]{1,0:T(8,128)(2,1)S(1)}, bf16[144,512]{1,0:T(8,128)(2,1)S(1)}, u32[]{:S(2)}, u32[]{:S(2)}) collective-permute-start(bf16[144,512]{1,0:T(8,128)(2,1)S(1)} %fusion.56), channel_id=1, source_target_pairs={{0,8},{4,12},{8,0},{12,4},{1,9},{5,13},{9,1},{13,5},{2,10},{6,14},... | collective-permute-start | bytes 442376 | tf_op jit(solution)/shard_map/ppermute | solution.py:425
  567.9 12.8 %collective-permute-start.79 = (bf16[144,512]{1,0:T(8,128)(2,1)S(1)}, bf16[144,512]{1,0:T(8,128)(2,1)S(1)}, u32[]{:S(2)}, u32[]{:S(2)}) collective-permute-start(bf16[144,512]{1,0:T(8,128)(2,1)S(1)} %fusion.56), channel_id=1, source_target_pairs={{0,4},{4,0},{8,12},{12,8},{1,5},{5,1},{9,13},{13,9},{2,6},{6,2},{1... | collective-permute-start | bytes 442376 | tf_op jit(solution)/shard_map/ppermute | solution.py:425
  (127 other events, 919.9 us)
